TPU v7x, 512 devices: a whole 4x8x8 slice. The times are simulated.
512 devices in a mesh: ta: 16 (over y, core), gz: 8 (over z), gy: 4 (over x).
Axes of the slice: x: 4, y: 8, z: 8, core: 2. Of those that a mesh axis runs over, the one named last changes fastest.
Arguments:
- restricted: bfloat16 [4096, 2, 64, 256], P(('ta', 'gz', 'gy')), may hold values from -30 to 30
- couplings: bfloat16 [9, 1, 8, 16, 32, 64, 128], P(None, None, 'gy', 'gz', 'ta'), may hold values from -3 to 7
- owners: int32 [4096], P(('ta', 'gz', 'gy')), may hold values from 0 to 7, as said below
- coarse_site: int32 [4096], P(('ta', 'gz', 'gy')), may hold values from 0 to 7, as said below
Outputs:
- solution: bfloat16 [1, 8, 16, 32, 2, 64, 256], P(None, 'gy', 'gz', 'ta')
Inputs may be any that keep to these rules, and one draw needn't show every extreme that they name: `owners`: within one ta and gy index, every device sends exactly 1 of its aggregates to each device of its gz group. Within one ta and gy index, the pairs (owners, coarse_site) are all different: every coarse site receives exactly one aggregate.
All inputs are finite; a program needn't handle non-finite values.
Results may differ from a plain program's by a relative error of at most 0.0065.
Values may be sent and summed in bfloat16 or wider, within the bound.
No kernel may reach another device: no remote copies, remote signals or barrier semaphores. Data moves between devices by JAX's collectives and lax.ppermute only.
A program may use at most 128 MiB of HBM per device.

v0:
```python
import jax
import jax.numpy as jnp
from jax import lax
from jax.sharding import PartitionSpec as P


def padded_2(cells, sides, width):
    for axis, dim in sides:
        count = lax.axis_size(axis)
        head = lax.slice_in_dim(cells, 0, width, axis=dim)
        tail = lax.slice_in_dim(cells, cells.shape[dim] - width, cells.shape[dim], axis=dim)
        cells = jnp.concatenate(
            [
                lax.ppermute(tail, axis, [(i, (i + 1) % count) for i in range(count)]),
                cells,
                lax.ppermute(head, axis, [((i + 1) % count, i) for i in range(count)]),
            ],
            axis=dim,
        )
    return cells


def block_double(blocks):
    columns = blocks.shape[-1] // 2
    real_blk = blocks[..., :columns]
    imag_blk = blocks[..., columns:]
    upper = jnp.concatenate([real_blk, -imag_blk], axis=-1)
    lower = jnp.concatenate([imag_blk, real_blk], axis=-1)
    return jnp.concatenate([upper, lower], axis=-2)


def apply_blocks(doubled, current, neighbours):
    shape = current.shape
    fields = jnp.stack([current] + neighbours, axis=0)
    flat = fields.reshape((9,) + shape[:-3] + (2 * shape[-2], shape[-1]))
    result = jnp.einsum(
        "kabcdoi,kabcdiw->abcdow", doubled, flat, preferred_element_type=jnp.float32
    )
    return result.reshape(shape)


def operator_sites(doubled, values):
    padded = padded_2(values, (("ta", 3), ("gz", 2), ("gy", 1)), 1)
    neighbours = [
        jnp.roll(values, -1, 0),
        jnp.roll(values, 1, 0),
        padded[:, 2:, 1:-1, 1:-1],
        padded[:, :-2, 1:-1, 1:-1],
        padded[:, 1:-1, 2:, 1:-1],
        padded[:, 1:-1, :-2, 1:-1],
        padded[:, 1:-1, 1:-1, 2:],
        padded[:, 1:-1, 1:-1, :-2],
    ]
    return apply_blocks(doubled, values, neighbours)


def inner_product(first_vec, second_vec):
    keep = tuple(range(first_vec.ndim - 3)) + (first_vec.ndim - 3,)
    first_re = first_vec[..., 0, :, :]
    first_im = first_vec[..., 1, :, :]
    second_re = second_vec[..., 0, :, :]
    second_im = second_vec[..., 1, :, :]
    real_part = jnp.sum(first_re * second_re + first_im * second_im, axis=keep)
    imag_part = jnp.sum(first_re * second_im - first_im * second_re, axis=keep)
    return (real_part, imag_part)


def squared_norm(values):
    return jnp.sum(values * values, axis=tuple(range(values.ndim - 1)))


def complex_scale(values, coef_re, coef_im):
    value_re = values[..., 0, :, :]
    value_im = values[..., 1, :, :]
    return jnp.stack(
        [coef_re * value_re - coef_im * value_im, coef_re * value_im + coef_im * value_re], axis=-3
    )


def widen(parts):
    stacked = jnp.stack(parts, axis=0)
    return stacked


def first_totals(parts):
    summed = lax.psum(widen(parts), ("ta", "gz", "gy"))
    return summed


def proj_totals(parts):
    summed = lax.psum(widen(parts), ("ta", "gz", "gy"))
    return summed


def step_totals(parts):
    summed = lax.psum(widen(parts), ("ta", "gz", "gy"))
    return summed


def local(restricted, couplings, owners, coarse_site):
    agg_count = restricted.shape[0]
    bucket = agg_count // lax.axis_size("gz")
    positions = jnp.arange(agg_count, dtype=jnp.int32)
    same_owner = owners[:, None] == owners[None, :]
    earlier = positions[None, :] < positions[:, None]
    rank_within = jnp.sum((same_owner & earlier).astype(jnp.int32), axis=1)
    target = owners * bucket + rank_within
    picker = (target[None, :] == positions[:, None]).astype(jnp.int32)
    outgoing = jnp.sum(picker * positions[None, :], axis=1)
    send_rows = jnp.take(restricted, outgoing, axis=0)
    send_slots = jnp.take(coarse_site, outgoing).astype(jnp.bfloat16)
    recv_rows, recv_slots = (
        lax.all_to_all(send_rows, "gz", split_axis=0, concat_axis=0, tiled=True),
        lax.all_to_all(send_slots, "gz", split_axis=0, concat_axis=0, tiled=True),
    )
    slot_index = recv_slots.astype(jnp.float32).astype(jnp.int32)
    placer = (slot_index[None, :] == positions[:, None]).astype(jnp.int32)
    arrival = jnp.sum(placer * positions[None, :], axis=1)
    source = jnp.take(recv_rows, arrival, axis=0).reshape(
        couplings.shape[1:5] + restricted.shape[1:]
    )
    doubled = block_double(couplings)
    start = source.astype(jnp.float32)
    image0 = operator_sites(doubled, source)
    c_re, c_im = inner_product(image0, start)
    totals = first_totals([squared_norm(image0), c_re, c_im])
    norm_zero = totals[0]
    alpha_re = totals[1] / norm_zero
    alpha_im = totals[2] / norm_zero
    iterate = complex_scale(start, alpha_re, alpha_im)
    residual = start - complex_scale(image0, alpha_re, alpha_im)
    search = residual.astype(jnp.bfloat16)
    image1 = operator_sites(doubled, search)
    proj_re, proj_im = inner_product(image0, image1)
    projected = proj_totals([proj_re, proj_im])
    beta_re = projected[0] / norm_zero
    beta_im = projected[1] / norm_zero
    update = image1 - complex_scale(image0, beta_re, beta_im)
    part_re, part_im = inner_product(update, residual)
    stepped = step_totals([part_re, part_im, squared_norm(update)])
    num_re = stepped[0]
    num_im = stepped[1]
    denom = stepped[2]
    direction = search.astype(jnp.float32) - complex_scale(start, beta_re, beta_im)
    solution = (iterate + complex_scale(direction, num_re / denom, num_im / denom)).astype(
        jnp.bfloat16
    )
    return solution


def solution(mesh):
    return jax.shard_map(
        local,
        mesh=mesh,
        in_specs=(
            P(("ta", "gz", "gy"), None, None, None),
            P(None, None, "gy", "gz", "ta", None, None),
            P(("ta", "gz", "gy")),
            P(("ta", "gz", "gy")),
        ),
        out_specs=P(None, "gy", "gz", "ta", None, None, None),
        check_vma=False,
    )
```

profile of v0, /device:TPU:26, one launch (start us, length us, event | category | flops | bytes accessed | tf_op | source)
XLA Modules:
  0.0 455.9 jit_solution(12767630806416575832)
XLA Ops:
  0.0 0.9 convert_reduce_fusion.1
  0.9 0.7 add.111
  1.7 1.3 gather_fusion
  3.0 0.7 copy.109
  3.7 10.3 %all-to-all-start.1 = ((bf16[8,1,1]{2,1,0:T(2,128)(2,1)}), bf16[8,1,1]{2,1,0:T(2,128)(2,1)S(1)}, u32[]{:S(2)}, u32[]{:S(2)}) async-start(bf16[8,1,1]{2,1,0:T(2,128)(2,1)} %copy.109), calls=%async_computation.1 | async-start | bytes 8192 | tf_op jit(solution)/shard_map/all_to_all | solution.py:114
  14.1 0.6 gather_fusion.1
  14.7 0.9 broadcast_select_fusion.1
  15.6 6.1 %all-to-all-done.1 = bf16[8,1,1]{2,1,0:T(2,128)(2,1)S(1)} async-done(((bf16[8,1,1]{2,1,0:T(2,128)(2,1)}), bf16[8,1,1]{2,1,0:T(2,128)(2,1)S(1)}, u32[]{:S(2)}, u32[]{:S(2)}) %all-to-all-start.1) | async-done | bytes 48 | tf_op jit(solution)/shard_map/all_to_all | solution.py:114
  21.7 3.5 all-to-all-start
  25.6 15.8 %all-to-all-done = bf16[8,2,64,256]{3,2,1,0:T(8,128)(2,1)S(1)} async-done(((bf16[8,2,64,256]{3,2,1,0:T(8,128)(2,1)}), bf16[8,2,64,256]{3,2,1,0:T(8,128)(2,1)S(1)}, u32[]{:S(2)}, u32[]{:S(2)}) %all-to-all-start) | async-done | bytes 524320 | tf_op jit(solution)/shard_map/all_to_all | solution.py:113
  41.5 0.6 gather_fusion.2
  42.3 0.5 collective-permute-start
  42.8 3.4 collective-permute-done.1
  46.2 1.9 collective-permute-done
  48.3 1.9 collective-permute-start.3
  50.2 3.9 collective-permute-start.2
  54.2 10.7 %collective-permute-done.3 = bf16[1,2,1,4,2,64,256]{6,5,4,3,2,1,0:T(8,128)(2,1)S(1)} collective-permute-done((bf16[1,2,1,4,2,64,256]{6,5,4,3,2,1,0:T(8,128)(2,1)S(1)}, bf16[1,2,1,4,2,64,256]{6,5,4,3,2,1,0:T(8,128)(2,1)S(1)}, u32[]{:S(2)}, u32[]{:S(2)}) %collective-permute-start.3) | collective-permute-done | bytes 524320 | tf_op jit(solution)/shard_map/ppermute | solution.py:16
  64.8 3.1 collective-permute-done.2
  68.5 3.5 collective-permute-start.5
  72.1 2.4 collective-permute-start.4
  74.5 0.6 fusion.34
  75.6 20.1 %collective-permute-done.5 = bf16[1,1,4,4,2,64,256]{6,5,4,3,2,1,0:T(8,128)(2,1)S(1)} collective-permute-done((bf16[1,1,4,4,2,64,256]{6,5,4,3,2,1,0:T(8,128)(2,1)S(1)}, bf16[1,1,4,4,2,64,256]{6,5,4,3,2,1,0:T(8,128)(2,1)S(1)}, u32[]{:S(2)}, u32[]{:S(2)}) %collective-permute-start.5) | collective-permute-done | bytes 1048608 | tf_op jit(solution)/shard_map/ppermute | solution.py:14
  95.7 3.1 collective-permute-done.4
  99.4 1.7 fusion.3
  101.2 94.2 %psum.21 = f32[3,256]{1,0:T(4,128)S(1)} all-reduce(f32[3,256]{1,0:T(4,128)S(1)} %pad_maximum_fusion.44), channel_id=1, replica_groups=mesh['ta'=16,'gz'=8,'gy'=4] {'ta','gz','gy'}, use_global_device_ids=true, to_apply=%region_6.8 | all-reduce | flops 768 | bytes 6144 | tf_op jit(solution)/shard_map/psum | solution.py:86
  195.5 1.2 fusion.19
  196.7 1.2 fusion.31
  198.0 0.5 collective-permute-start.6
  198.5 3.4 collective-permute-done.7
  201.9 1.9 collective-permute-done.6
  204.0 2.2 collective-permute-start.9
  206.3 3.6 collective-permute-start.8
  209.9 10.8 %collective-permute-done.9 = bf16[1,2,1,4,2,64,256]{6,5,4,3,2,1,0:T(8,128)(2,1)S(1)} collective-permute-done((bf16[1,2,1,4,2,64,256]{6,5,4,3,2,1,0:T(8,128)(2,1)S(1)}, bf16[1,2,1,4,2,64,256]{6,5,4,3,2,1,0:T(8,128)(2,1)S(1)}, u32[]{:S(2)}, u32[]{:S(2)}) %collective-permute-start.9) | collective-permute-done | bytes 524320 | tf_op jit(solution)/shard_map/ppermute | solution.py:16
  220.7 3.5 collective-permute-done.8
  224.6 2.4 collective-permute-start.11
  227.0 3.5 collective-permute-start.10
  231.2 20.6 %collective-permute-done.11 = bf16[1,1,4,4,2,64,256]{6,5,4,3,2,1,0:T(8,128)(2,1)S(1)} collective-permute-done((bf16[1,1,4,4,2,64,256]{6,5,4,3,2,1,0:T(8,128)(2,1)S(1)}, bf16[1,1,4,4,2,64,256]{6,5,4,3,2,1,0:T(8,128)(2,1)S(1)}, u32[]{:S(2)}, u32[]{:S(2)}) %collective-permute-start.11) | collective-permute-done | bytes 1048608 | tf_op jit(solution)/shard_map/ppermute | solution.py:14
  251.7 2.1 collective-permute-done.10
  254.4 1.1 copy-done.6
  255.4 0.4 copy-done.11
  255.8 0.4 copy-done.13
  256.1 1.6 fusion.21
  257.7 1.0 copy-done.2
  258.9 96.0 %psum.22 = f32[2,256]{1,0:T(2,128)S(1)} all-reduce(f32[2,256]{1,0:T(2,128)S(1)} %pad_maximum_fusion.46), channel_id=1, replica_groups=mesh['ta'=16,'gz'=8,'gy'=4] {'ta','gz','gy'}, use_global_device_ids=true, to_apply=%region_9.11 | all-reduce | flops 512 | bytes 4096 | tf_op jit(solution)/shard_map/psum | solution.py:91
  354.9 1.5 fusion.4
  357.1 0.9 copy-done.7
  358.3 96.6 %psum.23 = f32[3,256]{1,0:T(4,128)S(1)} all-reduce(f32[3,256]{1,0:T(4,128)S(1)} %pad_maximum_fusion.45), channel_id=1, replica_groups=mesh['ta'=16,'gz'=8,'gy'=4] {'ta','gz','gy'}, use_global_device_ids=true, to_apply=%region_13.15 | all-reduce | flops 768 | bytes 6144 | tf_op jit(solution)/shard_map/psum | solution.py:96
  455.0 0.9 fusion
  (88 shorter events, 5.7 us)
Async XLA Ops:
  0.0 14.1 %copy-start = (bf16[8,2,64,256]{3,2,1,0:T(8,128)(2,1)S(1)}, bf16[8,2,64,256]{3,2,1,0:T(8,128)(2,1)}, u32[]{:S(2)}) copy-start(bf16[8,2,64,256]{3,2,1,0:T(8,128)(2,1)} %param.6) | copy-start | bytes 1572868
  3.7 18.0 %all-to-all-start.1 = ((bf16[8,1,1]{2,1,0:T(2,128)(2,1)}), bf16[8,1,1]{2,1,0:T(2,128)(2,1)S(1)}, u32[]{:S(2)}, u32[]{:S(2)}) async-start(bf16[8,1,1]{2,1,0:T(2,128)(2,1)} %copy.109), calls=%async_computation.1 | async-start | bytes 8192 | tf_op jit(solution)/shard_map/all_to_all | solution.py:114
  21.7 19.7 %all-to-all-start = ((bf16[8,2,64,256]{3,2,1,0:T(8,128)(2,1)}), bf16[8,2,64,256]{3,2,1,0:T(8,128)(2,1)S(1)}, u32[]{:S(2)}, u32[]{:S(2)}) async-start(bf16[8,2,64,256]{3,2,1,0:T(8,128)(2,1)} %broadcast_select_fusion.1), calls=%async_computation | async-start | bytes 1048576 | tf_op jit(solution)/shard_map/all_to_all | solution.py:113
  42.2 153.2 %copy-start.1 = (f32[1,2,2,2,2,64,256]{6,5,4,3,2,1,0:T(8,128)}, f32[1,2,2,2,2,64,256]{6,5,4,3,2,1,0:T(8,128)S(1)}, u32[]{:S(2)}) copy-start(f32[1,2,2,2,2,64,256]{6,5,4,3,2,1,0:T(8,128)S(1)} %get-tuple-element.16) | copy-start | bytes 3145732
  42.3 3.9 collective-permute-start.1
  42.3 5.8 %collective-permute-start = (bf16[1,2,2,1,2,64,256]{6,5,4,3,2,1,0:T(8,128)(2,1)S(1)}, bf16[1,2,2,1,2,64,256]{6,5,4,3,2,1,0:T(8,128)(2,1)S(1)}, u32[]{:S(2)}, u32[]{:S(2)}) collective-permute-start(bf16[1,2,2,1,2,64,256]{6,5,4,3,2,1,0:T(8,128)(2,1)S(1)} %get-tuple-element.52), channel_id=1, source_target_pairs={{0,32},{32,64},{64,96},{96,128},{128,160},{160,192},{192,224},{224... | collective-permute-start | bytes 786440 | tf_op jit(solution)/shard_map/ppermute | solution.py:14
  48.3 16.5 %collective-permute-start.3 = (bf16[1,2,1,4,2,64,256]{6,5,4,3,2,1,0:T(8,128)(2,1)S(1)}, bf16[1,2,1,4,2,64,256]{6,5,4,3,2,1,0:T(8,128)(2,1)S(1)}, u32[]{:S(2)}, u32[]{:S(2)}) collective-permute-start(bf16[1,2,1,4,2,64,256]{6,5,4,3,2,1,0:T(8,128)(2,1)S(1)} %get-tuple-element.43), channel_id=1, source_target_pairs={{4,0},{8,4},{12,8},{16,12},{20,16},{24,20},{28,24},{0,28},{5,1},{9... | collective-permute-start | bytes 1572872 | tf_op jit(solution)/shard_map/ppermute | solution.py:16
  50.2 17.7 %collective-permute-start.2 = (bf16[1,2,1,4,2,64,256]{6,5,4,3,2,1,0:T(8,128)(2,1)S(1)}, bf16[1,2,1,4,2,64,256]{6,5,4,3,2,1,0:T(8,128)(2,1)S(1)}, u32[]{:S(2)}, u32[]{:S(2)}) collective-permute-start(bf16[1,2,1,4,2,64,256]{6,5,4,3,2,1,0:T(8,128)(2,1)S(1)} %get-tuple-element.42), channel_id=1, source_target_pairs={{0,4},{4,8},{8,12},{12,16},{16,20},{20,24},{24,28},{28,0},{1,5},{5... | collective-permute-start | bytes 1572872 | tf_op jit(solution)/shard_map/ppermute | solution.py:14
  68.3 6.2 %copy-start.4 = (bf16[9,1,2,2,2,64,128]{6,5,4,3,2,1,0:T(8,128)(2,1)S(1)}, bf16[9,1,2,2,2,64,128]{6,5,4,3,2,1,0:T(8,128)(2,1)}, u32[]{:S(2)}) copy-start(bf16[9,1,2,2,2,64,128]{6,5,4,3,2,1,0:T(8,128)(2,1)} %param.7) | copy-start | bytes 3538948
  68.5 27.2 %collective-permute-start.5 = (bf16[1,1,4,4,2,64,256]{6,5,4,3,2,1,0:T(8,128)(2,1)S(1)}, bf16[1,1,4,4,2,64,256]{6,5,4,3,2,1,0:T(8,128)(2,1)S(1)}, u32[]{:S(2)}, u32[]{:S(2)}) collective-permute-start(bf16[1,1,4,4,2,64,256]{6,5,4,3,2,1,0:T(8,128)(2,1)S(1)} %get-tuple-element.24), channel_id=1, source_target_pairs={{0,1},{1,2},{2,3},{3,0},{4,5},{5,6},{6,7},{7,4},{8,9},{9,10},{10,1... | collective-permute-start | bytes 3145736 | tf_op jit(solution)/shard_map/ppermute | solution.py:14
  72.1 26.8 %collective-permute-start.4 = (bf16[1,1,4,4,2,64,256]{6,5,4,3,2,1,0:T(8,128)(2,1)S(1)}, bf16[1,1,4,4,2,64,256]{6,5,4,3,2,1,0:T(8,128)(2,1)S(1)}, u32[]{:S(2)}, u32[]{:S(2)}) collective-permute-start(bf16[1,1,4,4,2,64,256]{6,5,4,3,2,1,0:T(8,128)(2,1)S(1)} %get-tuple-element.25), channel_id=1, source_target_pairs={{1,0},{2,1},{3,2},{0,3},{5,4},{6,5},{7,6},{4,7},{9,8},{10,9},{11,1... | collective-permute-start | bytes 3145736 | tf_op jit(solution)/shard_map/ppermute | solution.py:16
  75.1 24.3 %copy-start.5 = (bf16[9,1,2,2,2,64,64]{6,5,4,3,2,1,0:T(8,128)(2,1)}, bf16[9,1,2,2,2,64,64]{6,5,4,3,2,1,0:T(8,128)(2,1)S(1)}, u32[]{:S(2)}) copy-start(bf16[9,1,2,2,2,64,64]{6,5,4,3,2,1,0:T(8,128)(2,1)S(1)} %get-tuple-element.28) | copy-start | bytes 1769476
  75.1 24.3 %copy-start.12 = (bf16[9,1,2,2,2,64,64]{6,5,4,3,2,1,0:T(8,128)(2,1)}, bf16[9,1,2,2,2,64,64]{6,5,4,3,2,1,0:T(8,128)(2,1)S(1)}, u32[]{:S(2)}) copy-start(bf16[9,1,2,2,2,64,64]{6,5,4,3,2,1,0:T(8,128)(2,1)S(1)} %get-tuple-element.29) | copy-start | bytes 1769476
  75.3 24.1 %copy-start.10 = (bf16[9,1,2,2,2,64,64]{6,5,0,4,3,2,1:T(8,128)(2,1)}, bf16[9,1,2,2,2,64,64]{6,5,0,4,3,2,1:T(8,128)(2,1)S(1)}, u32[]{:S(2)}) copy-start(bf16[9,1,2,2,2,64,64]{6,5,0,4,3,2,1:T(8,128)(2,1)S(1)} %copy_negate_fusion) | copy-start | bytes 1769476
  198.0 3.9 collective-permute-start.7
  198.0 5.8 %collective-permute-start.6 = (bf16[1,2,2,1,2,64,256]{6,5,4,3,2,1,0:T(8,128)(2,1)S(1)}, bf16[1,2,2,1,2,64,256]{6,5,4,3,2,1,0:T(8,128)(2,1)S(1)}, u32[]{:S(2)}, u32[]{:S(2)}) collective-permute-start(bf16[1,2,2,1,2,64,256]{6,5,4,3,2,1,0:T(8,128)(2,1)S(1)} %get-tuple-element.50), channel_id=1, source_target_pairs={{0,32},{32,64},{64,96},{96,128},{128,160},{160,192},{192,224},{224... | collective-permute-start | bytes 786440 | tf_op jit(solution)/shard_map/ppermute | solution.py:14
  204.0 16.6 %collective-permute-start.9 = (bf16[1,2,1,4,2,64,256]{6,5,4,3,2,1,0:T(8,128)(2,1)S(1)}, bf16[1,2,1,4,2,64,256]{6,5,4,3,2,1,0:T(8,128)(2,1)S(1)}, u32[]{:S(2)}, u32[]{:S(2)}) collective-permute-start(bf16[1,2,1,4,2,64,256]{6,5,4,3,2,1,0:T(8,128)(2,1)S(1)} %get-tuple-element.41), channel_id=1, source_target_pairs={{4,0},{8,4},{12,8},{16,12},{20,16},{24,20},{28,24},{0,28},{5,1},{9... | collective-permute-start | bytes 1572872 | tf_op jit(solution)/shard_map/ppermute | solution.py:16
  206.3 17.9 %collective-permute-start.8 = (bf16[1,2,1,4,2,64,256]{6,5,4,3,2,1,0:T(8,128)(2,1)S(1)}, bf16[1,2,1,4,2,64,256]{6,5,4,3,2,1,0:T(8,128)(2,1)S(1)}, u32[]{:S(2)}, u32[]{:S(2)}) collective-permute-start(bf16[1,2,1,4,2,64,256]{6,5,4,3,2,1,0:T(8,128)(2,1)S(1)} %get-tuple-element.40), channel_id=1, source_target_pairs={{0,4},{4,8},{8,12},{12,16},{16,20},{20,24},{24,28},{28,0},{1,5},{5... | collective-permute-start | bytes 1572872 | tf_op jit(solution)/shard_map/ppermute | solution.py:14
  224.6 27.1 %collective-permute-start.11 = (bf16[1,1,4,4,2,64,256]{6,5,4,3,2,1,0:T(8,128)(2,1)S(1)}, bf16[1,1,4,4,2,64,256]{6,5,4,3,2,1,0:T(8,128)(2,1)S(1)}, u32[]{:S(2)}, u32[]{:S(2)}) collective-permute-start(bf16[1,1,4,4,2,64,256]{6,5,4,3,2,1,0:T(8,128)(2,1)S(1)} %get-tuple-element.20), channel_id=1, source_target_pairs={{0,1},{1,2},{2,3},{3,0},{4,5},{5,6},{6,7},{7,4},{8,9},{9,10},{10,1... | collective-permute-start | bytes 3145736 | tf_op jit(solution)/shard_map/ppermute | solution.py:14
  227.0 26.8 %collective-permute-start.10 = (bf16[1,1,4,4,2,64,256]{6,5,4,3,2,1,0:T(8,128)(2,1)S(1)}, bf16[1,1,4,4,2,64,256]{6,5,4,3,2,1,0:T(8,128)(2,1)S(1)}, u32[]{:S(2)}, u32[]{:S(2)}) collective-permute-start(bf16[1,1,4,4,2,64,256]{6,5,4,3,2,1,0:T(8,128)(2,1)S(1)} %get-tuple-element.21), channel_id=1, source_target_pairs={{1,0},{2,1},{3,2},{0,3},{5,4},{6,5},{7,6},{4,7},{9,8},{10,9},{11,1... | collective-permute-start | bytes 3145736 | tf_op jit(solution)/shard_map/ppermute | solution.py:16
  254.2 1.3 copy-start.6
  254.2 1.6 copy-start.11
  254.2 2.0 copy-start.13
  257.7 1.0 copy-start.2
  354.9 1.5 copy-start.3
  356.9 1.2 copy-start.7
  357.1 97.9 %copy-start.8 = (f32[1,2,2,2,1,64,256]{6,5,3,2,1,4,0:T(8,128)S(1)}, f32[1,2,2,2,1,64,256]{6,5,3,2,1,4,0:T(8,128)}, u32[]{:S(2)}) copy-start(f32[1,2,2,2,1,64,256]{6,5,3,2,1,4,0:T(8,128)} %get-tuple-element.30) | copy-start | bytes 1572868
  357.1 97.9 %copy-start.9 = (f32[1,2,2,2,1,64,256]{6,5,3,2,1,4,0:T(8,128)S(1)}, f32[1,2,2,2,1,64,256]{6,5,3,2,1,4,0:T(8,128)}, u32[]{:S(2)}) copy-start(f32[1,2,2,2,1,64,256]{6,5,3,2,1,4,0:T(8,128)} %get-tuple-element.31) | copy-start | bytes 1572868
where the time goes:
time: 457 us; the launch traced here: 456 us
  blocking collectives  287 us (63%)
  waiting for transfers between devices  107 us (23%)
  starting transfers between devices  38.3 us (8%)
  other arithmetic  11.5 us (3%)
  local copies, waits for them, and re-layouts  8.8 us (2%)
    psum x1, blocking collectives, step_totals(): summed = lax.psum(widen(parts), ('ta', 'gz', 'gy'))  96.6 us
    psum x1, blocking collectives, proj_totals(): summed = lax.psum(widen(parts), ('ta', 'gz', 'gy'))  96 us
    psum x1, blocking collectives, first_totals(): summed = lax.psum(widen(parts), ('ta', 'gz', 'gy'))  94.2 us
    ppermute x6, waiting for transfers between devices, padded_2(): lax.ppermute(tail, axis, [(i, (i + 1) % count) for i in range(count)])  51.2 us
    ppermute x6, waiting for transfers between devices, padded_2(): lax.ppermute(head, axis, [((i + 1) % count, i) for i in range(count)])  33.5 us
    all_to_all x1, waiting for transfers between devices, local(): lax.all_to_all(send_rows, 'gz', split_axis=0, concat_axis=0, tiled=True)  15.8 us
    ppermute x6, starting transfers between devices, padded_2(): lax.ppermute(tail, axis, [(i, (i + 1) % count) for i in range(count)])  14.4 us
    all_to_all x1, starting transfers between devices, local(): lax.all_to_all(send_slots, 'gz', split_axis=0, concat_axis=0, tiled=True)  10.3 us
  transfers between devices with their start and end apart: 14, of which 14 were waited for; matrix products, arithmetic and copies ran while one was open for 1% of the time, Pallas kernels for 0%

commit v1 on v0

v1 whole, which is shorter than its diff:
```python
import jax
import jax.numpy as jnp
from jax import lax
from jax.sharding import Mesh, PartitionSpec as P

ALL_AXES = ("ty", "tc", "gz", "gy")
TIME_AXES = ("ty", "tc")
SLOT_ROWS = 16


def axes_size(axes):
    return lax.axis_size(axes)


def shifted(values, axes, step):
    count = axes_size(axes)
    return lax.ppermute(values, axes, [(i, (i + step) % count) for i in range(count)])


def spread_sum(parts, axes):
    count = axes_size(axes)
    copies = jnp.broadcast_to(parts[None], (count,) + parts.shape)
    landed = lax.all_to_all(copies, axes, split_axis=0, concat_axis=0, tiled=True)
    return jnp.sum(landed, axis=0)


def block_double(blocks):
    columns = blocks.shape[-1] // 2
    real_blk = blocks[..., :columns]
    imag_blk = blocks[..., columns:]
    upper = jnp.concatenate([real_blk, -imag_blk], axis=-1)
    lower = jnp.concatenate([imag_blk, real_blk], axis=-1)
    return jnp.concatenate([upper, lower], axis=-2)


def relay(restricted, owners, coarse_site):
    count = restricted.shape[0]
    positions = jnp.arange(count, dtype=jnp.int32)
    picker = (owners[None, :] == positions[:, None]).astype(jnp.int32)
    order = jnp.sum(picker * positions[None, :], axis=1)
    rows = restricted.reshape(count, -1, restricted.shape[-1])
    tail = jnp.broadcast_to(
        coarse_site.astype(rows.dtype)[:, None, None], (count, SLOT_ROWS, rows.shape[-1])
    )
    payload = jnp.take(jnp.concatenate([rows, tail], axis=1), order, axis=0)
    landed = lax.all_to_all(payload, "gz", split_axis=0, concat_axis=0, tiled=True)
    slots = landed[:, rows.shape[1], 0].astype(jnp.int32)
    placer = (slots[None, :] == positions[:, None]).astype(jnp.int32)
    arrival = jnp.sum(placer * positions[None, :], axis=1)
    return jnp.take(landed[:, : rows.shape[1]], arrival, axis=0)


def exchange(field):
    outer = []
    for axes, dim in (("gz", 1), ("gy", 0), (TIME_AXES, 2)):
        head = lax.slice_in_dim(field, 0, 1, axis=dim)
        tail = lax.slice_in_dim(field, 1, 2, axis=dim)
        outer.append(
            jnp.concatenate([shifted(tail, axes, 1), shifted(head, axes, -1)], axis=dim)
        )
    return [outer[1], outer[0], outer[2]]


def split_couplings(doubled):
    inside = [doubled[0], doubled[1], doubled[2]]
    outside = []
    for dim in range(3):
        ahead, behind = doubled[3 + 2 * dim], doubled[4 + 2 * dim]
        pick = lambda a, s: lax.slice_in_dim(a, s, s + 1, axis=dim)
        inside.append(jnp.concatenate([pick(ahead, 0), pick(behind, 1)], axis=dim))
        outside.append(jnp.concatenate([pick(behind, 0), pick(ahead, 1)], axis=dim))
    return jnp.stack(inside), jnp.stack(outside)


def operate(inside, outside, field):
    outer = jnp.stack(exchange(field))
    inner = jnp.stack([field, field, field] + [jnp.flip(field, axis=d) for d in range(3)])
    form = "kabcoi,kabciw->abcow"
    near = jnp.einsum(form, inside, inner, preferred_element_type=jnp.float32)
    far = jnp.einsum(form, outside, outer, preferred_element_type=jnp.float32)
    return near + far


def dot_parts(first, second):
    half = first.shape[-2] // 2
    a_re, a_im = first[..., :half, :], first[..., half:, :]
    b_re, b_im = second[..., :half, :], second[..., half:, :]
    over = tuple(range(first.ndim - 1))
    real_part = jnp.sum(a_re * b_re + a_im * b_im, axis=over)
    imag_part = jnp.sum(a_re * b_im - a_im * b_re, axis=over)
    return real_part, imag_part


def local(restricted, couplings, owners, coarse_site):
    source = relay(restricted, owners, coarse_site).reshape((2, 2, 2, -1, restricted.shape[-1]))
    inside, outside = split_couplings(block_double(couplings[:, 0]))
    start = source.astype(jnp.float32)
    image = operate(inside, outside, source)
    second = operate(inside, outside, image.astype(jnp.bfloat16))
    over = tuple(range(image.ndim - 1))
    c_re, c_im = dot_parts(image, start)
    d_re, d_im = dot_parts(image, second)
    e_re, e_im = dot_parts(second, start)
    parts = jnp.stack(
        [
            jnp.sum(image * image, axis=over),
            c_re,
            c_im,
            d_re,
            d_im,
            e_re,
            e_im,
            jnp.sum(second * second, axis=over),
        ]
    )
    totals = spread_sum(spread_sum(parts, ("tc", "gz")), ("ty", "gy"))
    norm, c_re, c_im, d_re, d_im, e_re, e_im, tail = [totals[i] for i in range(8)]
    a_re, a_im = c_re / norm, c_im / norm
    g_re, g_im = d_re / norm, d_im / norm
    p_re, p_im = c_re - a_re * norm, c_im - a_im * norm
    q_re = e_re - (a_re * d_re + a_im * d_im)
    q_im = e_im - (a_im * d_re - a_re * d_im)
    num_re = g_re * p_re + g_im * p_im - q_re
    num_im = g_re * p_im - g_im * p_re - q_im
    denom = tail - (g_re * d_re + g_im * d_im)
    y_re, y_im = num_re / denom, num_im / denom
    x_re = a_re + y_re * g_re - y_im * g_im
    x_im = a_im + y_re * g_im + y_im * g_re
    half = image.shape[-2] // 2
    s_re, s_im = start[..., :half, :], start[..., half:, :]
    i_re, i_im = image[..., :half, :], image[..., half:, :]
    out_re = x_re * s_re - x_im * s_im - (y_re * i_re - y_im * i_im)
    out_im = x_re * s_im + x_im * s_re - (y_re * i_im + y_im * i_re)
    out = jnp.stack([out_re, out_im], axis=-3).astype(jnp.bfloat16)
    return out[None]


def solution(mesh):
    cores = 2
    fine = Mesh(
        mesh.devices.reshape((mesh.shape["ta"] // cores, cores) + mesh.devices.shape[1:]),
        ALL_AXES,
    )
    return jax.shard_map(
        local,
        mesh=fine,
        in_specs=(
            P(ALL_AXES, None, None, None),
            P(None, None, "gy", "gz", TIME_AXES, None, None),
            P(ALL_AXES),
            P(ALL_AXES),
        ),
        out_specs=P(None, "gy", "gz", TIME_AXES, None, None, None),
        check_vma=False,
    )
```

time: 457 us -> 117 us (0.26)
  the two profiles are of different devices: /device:TPU:26 before, /device:TPU:8 now
where the time goes in v1:
time: 117 us
  starting transfers between devices  42.2 us (36%)
  blocking collectives  33.3 us (28%)
  waiting for transfers between devices  23 us (20%)
  other arithmetic  10.8 us (9%)
  local copies, waits for them, and re-layouts  3.86 us (3%)
  matrix products  3.04 us (3%)
    all_to_all x2, blocking collectives, spread_sum(): lax.all_to_all(copies, axes, split_axis=0, concat_axis=0, tiled=True)  33.3 us
    ppermute x12, starting transfers between devices, shifted(): lax.ppermute(values, axes, [(i, (i + step) % count) for i in range(count)])  31.8 us
    all_to_all x1, waiting for transfers between devices, relay(): lax.all_to_all(payload, 'gz', split_axis=0, concat_axis=0, tiled=True)  13.9 us
    all_to_all x1, starting transfers between devices, relay(): lax.all_to_all(payload, 'gz', split_axis=0, concat_axis=0, tiled=True)  10.3 us
    ppermute x12, waiting for transfers between devices, shifted(): lax.ppermute(values, axes, [(i, (i + step) % count) for i in range(count)])  9.08 us
    concatenate x1, other arithmetic, block_double(): return jnp.concatenate([upper, lower], axis=-2)  2.56 us
  transfers between devices with their start and end apart: 13, of which 6 were waited for; matrix products, arithmetic and copies ran while one was open for 5% of the time, Pallas kernels for 0%

profile of v1, /device:TPU:8, one launch (start us, length us, event | category | flops | bytes accessed | tf_op | source)
XLA Modules:
  0.0 116.8 jit_solution(17635182896413752450)
XLA Ops:
  0.0 0.9 select_reduce_fusion.1
  0.9 0.7 convert_element_type.29
  1.6 0.1 broadcast_in_dim.35
  1.6 1.1 pad_maximum_fusion.4
  2.7 0.6 gather_fusion
  3.3 0.9 broadcast_select_fusion
  4.2 10.3 %all-to-all-start = ((bf16[8,144,256]{2,1,0:T(8,128)(2,1)}), bf16[8,144,256]{2,1,0:T(8,128)(2,1)S(1)}, u32[]{:S(2)}, u32[]{:S(2)}) async-start(bf16[8,144,256]{2,1,0:T(8,128)(2,1)} %broadcast_select_fusion), calls=%async_computation | async-start | bytes 1179648 | tf_op jit(solution)/shard_map/all_to_all | solution.py:46
  14.6 0.5 slice_negate_fusion
  15.1 0.3 maximum_bitcast_fusion.19
  15.4 0.6 maximum_bitcast_fusion.8
  16.2 0.7 maximum_bitcast_fusion.12
  17.0 2.6 %maximum_maximum_fusion = bf16[9,2,2,2,128,128]{5,4,3,2,1,0:T(8,128)(2,1)} fusion(bf16[9,2,2,2,64,64]{5,4,3,2,1,0:T(8,128)(2,1)S(1)} %get-tuple-element.39, bf16[9,2,2,2,64,64]{5,4,3,2,1,0:T(8,128)(2,1)S(1)} %get-tuple-element.38, bf16[9,2,2,2,64,64]{5,4,3,2,1,0:T(8,128)(2,1)S(1)} %get-tuple-element.37), kind=kLoop, calls=%fused_computation.4 | loop fusion | flops 9437184 | bytes 4128768 | tf_op jit(solution)/shard_map/concatenate | solution.py:33
  19.5 13.9 %all-to-all-done = bf16[8,144,256]{2,1,0:T(8,128)(2,1)S(1)} async-done(((bf16[8,144,256]{2,1,0:T(8,128)(2,1)}), bf16[8,144,256]{2,1,0:T(8,128)(2,1)S(1)}, u32[]{:S(2)}, u32[]{:S(2)}) %all-to-all-start) | async-done | bytes 589856 | tf_op jit(solution)/shard_map/all_to_all | solution.py:46
  33.5 0.2 fusion.26
  33.7 0.1 select_reduce_fusion
  33.8 0.1 reduce_sum.117
  34.0 0.6 gather_fusion.1
  34.6 0.2 fusion.33
  34.8 0.1 broadcast_select_fusion.1
  35.0 4.7 %collective-permute-start.1 = (bf16[1,2,2,128,256]{4,3,2,1,0:T(8,128)(2,1)S(1)}, bf16[1,2,2,128,256]{4,3,2,1,0:T(8,128)(2,1)S(1)}, u32[]{:S(2)}, u32[]{:S(2)}) collective-permute-start(bf16[1,2,2,128,256]{4,3,2,1,0:T(8,128)(2,1)S(1)} %bitcast.120), channel_id=1, source_target_pairs={{0,3},{1,0},{2,1},{3,2},{4,7},{5,4},{6,5},{7,6},{8,11},{9,8},{10,9... | collective-permute-start | bytes 786440 | tf_op jit(solution)/shard_map/ppermute | solution.py:17
  39.7 1.9 %collective-permute-start = (bf16[1,2,2,128,256]{4,3,2,1,0:T(8,128)(2,1)S(1)}, bf16[1,2,2,128,256]{4,3,2,1,0:T(8,128)(2,1)S(1)}, u32[]{:S(2)}, u32[]{:S(2)}) collective-permute-start(bf16[1,2,2,128,256]{4,3,2,1,0:T(8,128)(2,1)S(1)} %bitcast.119), channel_id=1, source_target_pairs={{0,1},{1,2},{2,3},{3,0},{4,5},{5,6},{6,7},{7,4},{8,9},{9,10},{10,1... | collective-permute-start | bytes 786440 | tf_op jit(solution)/shard_map/ppermute | solution.py:17
  41.6 1.7 %collective-permute-start.5 = (bf16[2,2,1,128,256]{4,3,2,1,0:T(8,128)(2,1)S(1)}, bf16[2,2,1,128,256]{4,3,2,1,0:T(8,128)(2,1)S(1)}, u32[]{:S(2)}, u32[]{:S(2)}) collective-permute-start(bf16[2,2,1,128,256]{4,3,2,1,0:T(8,128)(2,1)S(1)} %get-tuple-element.51), channel_id=1, source_target_pairs={{0,480},{32,0},{64,32},{96,64},{128,96},{160,128},{192,160},{224,1... | collective-permute-start | bytes 786440 | tf_op jit(solution)/shard_map/ppermute | solution.py:17
  43.4 2.5 %collective-permute-start.2 = (bf16[2,1,2,128,256]{4,3,2,1,0:T(8,128)(2,1)S(1)}, bf16[2,1,2,128,256]{4,3,2,1,0:T(8,128)(2,1)S(1)}, u32[]{:S(2)}, u32[]{:S(2)}) collective-permute-start(bf16[2,1,2,128,256]{4,3,2,1,0:T(8,128)(2,1)S(1)} %get-tuple-element.48), channel_id=1, source_target_pairs={{0,4},{4,8},{8,12},{12,16},{16,20},{20,24},{24,28},{28,0},{1,5},{5... | collective-permute-start | bytes 786440 | tf_op jit(solution)/shard_map/ppermute | solution.py:17
  45.8 0.2 fusion.22
  46.0 0.2 fusion.21
  46.2 0.2 fusion.23
  46.5 4.6 %collective-permute-start.3 = (bf16[2,1,2,128,256]{4,3,2,1,0:T(8,128)(2,1)S(1)}, bf16[2,1,2,128,256]{4,3,2,1,0:T(8,128)(2,1)S(1)}, u32[]{:S(2)}, u32[]{:S(2)}) collective-permute-start(bf16[2,1,2,128,256]{4,3,2,1,0:T(8,128)(2,1)S(1)} %get-tuple-element.49), channel_id=1, source_target_pairs={{0,28},{4,0},{8,4},{12,8},{16,12},{20,16},{24,20},{28,24},{1,29},{... | collective-permute-start | bytes 786440 | tf_op jit(solution)/shard_map/ppermute | solution.py:17
  51.3 3.3 %collective-permute-done.2 = bf16[2,1,2,128,256]{4,3,2,1,0:T(8,128)(2,1)S(1)} collective-permute-done((bf16[2,1,2,128,256]{4,3,2,1,0:T(8,128)(2,1)S(1)}, bf16[2,1,2,128,256]{4,3,2,1,0:T(8,128)(2,1)S(1)}, u32[]{:S(2)}, u32[]{:S(2)}) %collective-permute-start.2) | collective-permute-done | bytes 262176 | tf_op jit(solution)/shard_map/ppermute | solution.py:17
  54.6 1.9 %collective-permute-done.3 = bf16[2,1,2,128,256]{4,3,2,1,0:T(8,128)(2,1)S(1)} collective-permute-done((bf16[2,1,2,128,256]{4,3,2,1,0:T(8,128)(2,1)S(1)}, bf16[2,1,2,128,256]{4,3,2,1,0:T(8,128)(2,1)S(1)}, u32[]{:S(2)}, u32[]{:S(2)}) %collective-permute-start.3) | collective-permute-done | bytes 262176 | tf_op jit(solution)/shard_map/ppermute | solution.py:17
  56.6 0.7 fusion.6
  57.2 1.0 copy-done.1
  58.2 0.8 multiply_reduce_fusion.1
  59.0 0.1 bitcast_dynamic-update-slice_fusion.6
  59.3 2.0 %collective-permute-start.8 = (bf16[2,1,2,128,256]{4,3,2,1,0:T(8,128)(2,1)S(1)}, bf16[2,1,2,128,256]{4,3,2,1,0:T(8,128)(2,1)S(1)}, u32[]{:S(2)}, u32[]{:S(2)}) collective-permute-start(bf16[2,1,2,128,256]{4,3,2,1,0:T(8,128)(2,1)S(1)} %get-tuple-element.42), channel_id=1, source_target_pairs={{0,4},{4,8},{8,12},{12,16},{16,20},{20,24},{24,28},{28,0},{1,5},{5... | collective-permute-start | bytes 786440 | tf_op jit(solution)/shard_map/ppermute | solution.py:17
  61.4 5.6 %collective-permute-start.9 = (bf16[2,1,2,128,256]{4,3,2,1,0:T(8,128)(2,1)S(1)}, bf16[2,1,2,128,256]{4,3,2,1,0:T(8,128)(2,1)S(1)}, u32[]{:S(2)}, u32[]{:S(2)}) collective-permute-start(bf16[2,1,2,128,256]{4,3,2,1,0:T(8,128)(2,1)S(1)} %get-tuple-element.43), channel_id=1, source_target_pairs={{0,28},{4,0},{8,4},{12,8},{16,12},{20,16},{24,20},{28,24},{1,29},{... | collective-permute-start | bytes 786440 | tf_op jit(solution)/shard_map/ppermute | solution.py:17
  67.1 2.7 %collective-permute-start.6 = (bf16[1,2,2,128,256]{4,3,2,1,0:T(8,128)(2,1)S(1)}, bf16[1,2,2,128,256]{4,3,2,1,0:T(8,128)(2,1)S(1)}, u32[]{:S(2)}, u32[]{:S(2)}) collective-permute-start(bf16[1,2,2,128,256]{4,3,2,1,0:T(8,128)(2,1)S(1)} %get-tuple-element.40), channel_id=1, source_target_pairs={{0,1},{1,2},{2,3},{3,0},{4,5},{5,6},{6,7},{7,4},{8,9},{9,10},{10,1... | collective-permute-start | bytes 786440 | tf_op jit(solution)/shard_map/ppermute | solution.py:17
  69.7 4.4 %collective-permute-start.7 = (bf16[1,2,2,128,256]{4,3,2,1,0:T(8,128)(2,1)S(1)}, bf16[1,2,2,128,256]{4,3,2,1,0:T(8,128)(2,1)S(1)}, u32[]{:S(2)}, u32[]{:S(2)}) collective-permute-start(bf16[1,2,2,128,256]{4,3,2,1,0:T(8,128)(2,1)S(1)} %get-tuple-element.41), channel_id=1, source_target_pairs={{0,3},{1,0},{2,1},{3,2},{4,7},{5,4},{6,5},{7,6},{8,11},{9,8},{10,9... | collective-permute-start | bytes 786440 | tf_op jit(solution)/shard_map/ppermute | solution.py:17
  74.2 1.7 %collective-permute-start.11 = (bf16[2,2,1,128,256]{4,3,2,1,0:T(8,128)(2,1)S(1)}, bf16[2,2,1,128,256]{4,3,2,1,0:T(8,128)(2,1)S(1)}, u32[]{:S(2)}, u32[]{:S(2)}) collective-permute-start(bf16[2,2,1,128,256]{4,3,2,1,0:T(8,128)(2,1)S(1)} %get-tuple-element.45), channel_id=1, source_target_pairs={{0,480},{32,0},{64,32},{96,64},{128,96},{160,128},{192,160},{224,1... | collective-permute-start | bytes 786440 | tf_op jit(solution)/shard_map/ppermute | solution.py:17
  76.0 1.1 collective-permute-done.6
  77.1 1.2 %collective-permute-done.7 = bf16[1,2,2,128,256]{4,3,2,1,0:T(8,128)(2,1)S(1)} collective-permute-done((bf16[1,2,2,128,256]{4,3,2,1,0:T(8,128)(2,1)S(1)}, bf16[1,2,2,128,256]{4,3,2,1,0:T(8,128)(2,1)S(1)}, u32[]{:S(2)}, u32[]{:S(2)}) %collective-permute-start.7) | collective-permute-done | bytes 262176 | tf_op jit(solution)/shard_map/ppermute | solution.py:17
  78.4 1.6 %collective-permute-done.10 = bf16[2,2,1,128,256]{4,3,2,1,0:T(8,128)(2,1)S(1)} collective-permute-done((bf16[2,2,1,128,256]{4,3,2,1,0:T(8,128)(2,1)S(1)}, bf16[2,2,1,128,256]{4,3,2,1,0:T(8,128)(2,1)S(1)}, u32[]{:S(2)}, u32[]{:S(2)}) %collective-permute-start.10) | collective-permute-done | bytes 262176 | tf_op jit(solution)/shard_map/ppermute | solution.py:17
  80.1 0.7 fusion.9
  80.7 0.9 multiply_reduce_fusion
  81.7 0.4 subtract_reduce_fusion.1
  82.2 13.0 %all_to_all.15 = f32[16,8,256]{2,1,0:T(8,128)S(1)} all-to-all(f32[16,8,256]{2,1,0:T(8,128)S(1)} %broadcast_in_dim.70), channel_id=1, replica_groups=mesh['ty'=8,'tc'=2,'gz'=8,'gy'=4] {'tc','gz'}, dimensions={0} | all-to-all | bytes 262144 | tf_op jit(solution)/shard_map/all_to_all | solution.py:23
  95.2 20.4 %all_to_all.16 = f32[32,8,256]{2,1,0:T(8,128)S(1)} all-to-all(f32[32,8,256]{2,1,0:T(8,128)S(1)} %broadcast_in_dim.71), channel_id=1, replica_groups=mesh['ty'=8,'tc'=2,'gz'=8,'gy'=4] {'ty','gy'}, dimensions={0} | all-to-all | bytes 524288 | tf_op jit(solution)/shard_map/all_to_all | solution.py:23
  115.6 0.3 fusion.24
  116.0 0.8 copy.56
  (66 shorter events, 1.4 us)
Async XLA Ops:
  0.0 14.6 %copy-start = (bf16[9,1,2,2,2,64,128]{6,5,4,3,2,1,0:T(8,128)(2,1)S(1)}, bf16[9,1,2,2,2,64,128]{6,5,4,3,2,1,0:T(8,128)(2,1)}, u32[]{:S(2)}) copy-start(bf16[9,1,2,2,2,64,128]{6,5,4,3,2,1,0:T(8,128)(2,1)} %param.5) | copy-start | bytes 3538948
  4.2 29.2 %all-to-all-start = ((bf16[8,144,256]{2,1,0:T(8,128)(2,1)}), bf16[8,144,256]{2,1,0:T(8,128)(2,1)S(1)}, u32[]{:S(2)}, u32[]{:S(2)}) async-start(bf16[8,144,256]{2,1,0:T(8,128)(2,1)} %broadcast_select_fusion), calls=%async_computation | async-start | bytes 1179648 | tf_op jit(solution)/shard_map/all_to_all | solution.py:46
  16.1 40.4 %copy-start.2 = (bf16[1,2,2,2,128,128]{5,4,3,2,1,0:T(8,128)(2,1)}, bf16[1,2,2,2,128,128]{5,4,3,2,1,0:T(8,128)(2,1)S(1)}, u32[]{:S(2)}) copy-start(bf16[1,2,2,2,128,128]{5,4,3,2,1,0:T(8,128)(2,1)S(1)} %maximum_bitcast_fusion.14) | copy-start | bytes 786436
  17.0 39.6 %copy-start.5 = (bf16[1,2,2,2,128,128]{5,4,3,2,1,0:T(8,128)(2,1)}, bf16[1,2,2,2,128,128]{5,4,3,2,1,0:T(8,128)(2,1)S(1)}, u32[]{:S(2)}) copy-start(bf16[1,2,2,2,128,128]{5,4,3,2,1,0:T(8,128)(2,1)S(1)} %maximum_bitcast_fusion.15) | copy-start | bytes 786436
  35.0 11.5 %collective-permute-start.1 = (bf16[1,2,2,128,256]{4,3,2,1,0:T(8,128)(2,1)S(1)}, bf16[1,2,2,128,256]{4,3,2,1,0:T(8,128)(2,1)S(1)}, u32[]{:S(2)}, u32[]{:S(2)}) collective-permute-start(bf16[1,2,2,128,256]{4,3,2,1,0:T(8,128)(2,1)S(1)} %bitcast.120), channel_id=1, source_target_pairs={{0,3},{1,0},{2,1},{3,2},{4,7},{5,4},{6,5},{7,6},{8,11},{9,8},{10,9... | collective-permute-start | bytes 786440 | tf_op jit(solution)/shard_map/ppermute | solution.py:17
  39.7 11.5 %collective-permute-start = (bf16[1,2,2,128,256]{4,3,2,1,0:T(8,128)(2,1)S(1)}, bf16[1,2,2,128,256]{4,3,2,1,0:T(8,128)(2,1)S(1)}, u32[]{:S(2)}, u32[]{:S(2)}) collective-permute-start(bf16[1,2,2,128,256]{4,3,2,1,0:T(8,128)(2,1)S(1)} %bitcast.119), channel_id=1, source_target_pairs={{0,1},{1,2},{2,3},{3,0},{4,5},{5,6},{6,7},{7,4},{8,9},{9,10},{10,1... | collective-permute-start | bytes 786440 | tf_op jit(solution)/shard_map/ppermute | solution.py:17
  41.6 9.6 %collective-permute-start.4 = (bf16[2,2,1,128,256]{4,3,2,1,0:T(8,128)(2,1)S(1)}, bf16[2,2,1,128,256]{4,3,2,1,0:T(8,128)(2,1)S(1)}, u32[]{:S(2)}, u32[]{:S(2)}) collective-permute-start(bf16[2,2,1,128,256]{4,3,2,1,0:T(8,128)(2,1)S(1)} %get-tuple-element.50), channel_id=1, source_target_pairs={{0,32},{32,64},{64,96},{96,128},{128,160},{160,192},{192,224},{224... | collective-permute-start | bytes 786440 | tf_op jit(solution)/shard_map/ppermute | solution.py:17
  41.6 9.6 %collective-permute-start.5 = (bf16[2,2,1,128,256]{4,3,2,1,0:T(8,128)(2,1)S(1)}, bf16[2,2,1,128,256]{4,3,2,1,0:T(8,128)(2,1)S(1)}, u32[]{:S(2)}, u32[]{:S(2)}) collective-permute-start(bf16[2,2,1,128,256]{4,3,2,1,0:T(8,128)(2,1)S(1)} %get-tuple-element.51), channel_id=1, source_target_pairs={{0,480},{32,0},{64,32},{96,64},{128,96},{160,128},{192,160},{224,1... | collective-permute-start | bytes 786440 | tf_op jit(solution)/shard_map/ppermute | solution.py:17
  43.4 11.3 %collective-permute-start.2 = (bf16[2,1,2,128,256]{4,3,2,1,0:T(8,128)(2,1)S(1)}, bf16[2,1,2,128,256]{4,3,2,1,0:T(8,128)(2,1)S(1)}, u32[]{:S(2)}, u32[]{:S(2)}) collective-permute-start(bf16[2,1,2,128,256]{4,3,2,1,0:T(8,128)(2,1)S(1)} %get-tuple-element.48), channel_id=1, source_target_pairs={{0,4},{4,8},{8,12},{12,16},{16,20},{20,24},{24,28},{28,0},{1,5},{5... | collective-permute-start | bytes 786440 | tf_op jit(solution)/shard_map/ppermute | solution.py:17
  46.5 10.0 %collective-permute-start.3 = (bf16[2,1,2,128,256]{4,3,2,1,0:T(8,128)(2,1)S(1)}, bf16[2,1,2,128,256]{4,3,2,1,0:T(8,128)(2,1)S(1)}, u32[]{:S(2)}, u32[]{:S(2)}) collective-permute-start(bf16[2,1,2,128,256]{4,3,2,1,0:T(8,128)(2,1)S(1)} %get-tuple-element.49), channel_id=1, source_target_pairs={{0,28},{4,0},{8,4},{12,8},{16,12},{20,16},{24,20},{28,24},{1,29},{... | collective-permute-start | bytes 786440 | tf_op jit(solution)/shard_map/ppermute | solution.py:17
  56.6 1.7 %copy-start.1 = (bf16[9,2,2,2,128,128]{5,4,3,2,1,0:T(8,128)(2,1)S(1)}, bf16[9,2,2,2,128,128]{5,4,3,2,1,0:T(8,128)(2,1)}, u32[]{:S(2)}) copy-start(bf16[9,2,2,2,128,128]{5,4,3,2,1,0:T(8,128)(2,1)} %maximum_maximum_fusion) | copy-start | bytes 7077892
  56.6 1.7 %copy-start.4 = (bf16[1,2,2,2,128,128]{5,4,0,3,2,1:T(8,128)(2,1)S(1)}, bf16[1,2,2,2,128,128]{5,4,0,3,2,1:T(8,128)(2,1)}, u32[]{:S(2)}) copy-start(bf16[1,2,2,2,128,128]{5,4,0,3,2,1:T(8,128)(2,1)} %maximum_bitcast_fusion.12) | copy-start | bytes 786436
  59.3 14.9 %collective-permute-start.8 = (bf16[2,1,2,128,256]{4,3,2,1,0:T(8,128)(2,1)S(1)}, bf16[2,1,2,128,256]{4,3,2,1,0:T(8,128)(2,1)S(1)}, u32[]{:S(2)}, u32[]{:S(2)}) collective-permute-start(bf16[2,1,2,128,256]{4,3,2,1,0:T(8,128)(2,1)S(1)} %get-tuple-element.42), channel_id=1, source_target_pairs={{0,4},{4,8},{8,12},{12,16},{16,20},{20,24},{24,28},{28,0},{1,5},{5... | collective-permute-start | bytes 786440 | tf_op jit(solution)/shard_map/ppermute | solution.py:17
  61.3 18.7 %copy-start.3 = (bf16[1,2,2,2,128,128]{5,4,3,2,1,0:T(8,128)(2,1)S(1)}, bf16[1,2,2,2,128,128]{5,4,3,2,1,0:T(8,128)(2,1)}, u32[]{:S(2)}) copy-start(bf16[1,2,2,2,128,128]{5,4,3,2,1,0:T(8,128)(2,1)} %copy-done.2) | copy-start | bytes 786436
  61.4 18.7 %copy-start.6 = (bf16[1,2,2,2,128,128]{5,4,3,2,1,0:T(8,128)(2,1)S(1)}, bf16[1,2,2,2,128,128]{5,4,3,2,1,0:T(8,128)(2,1)}, u32[]{:S(2)}) copy-start(bf16[1,2,2,2,128,128]{5,4,3,2,1,0:T(8,128)(2,1)} %copy-done.5) | copy-start | bytes 786436
  61.4 14.6 %collective-permute-start.9 = (bf16[2,1,2,128,256]{4,3,2,1,0:T(8,128)(2,1)S(1)}, bf16[2,1,2,128,256]{4,3,2,1,0:T(8,128)(2,1)S(1)}, u32[]{:S(2)}, u32[]{:S(2)}) collective-permute-start(bf16[2,1,2,128,256]{4,3,2,1,0:T(8,128)(2,1)S(1)} %get-tuple-element.43), channel_id=1, source_target_pairs={{0,28},{4,0},{8,4},{12,8},{16,12},{20,16},{24,20},{28,24},{1,29},{... | collective-permute-start | bytes 786440 | tf_op jit(solution)/shard_map/ppermute | solution.py:17
  67.1 10.1 %collective-permute-start.6 = (bf16[1,2,2,128,256]{4,3,2,1,0:T(8,128)(2,1)S(1)}, bf16[1,2,2,128,256]{4,3,2,1,0:T(8,128)(2,1)S(1)}, u32[]{:S(2)}, u32[]{:S(2)}) collective-permute-start(bf16[1,2,2,128,256]{4,3,2,1,0:T(8,128)(2,1)S(1)} %get-tuple-element.40), channel_id=1, source_target_pairs={{0,1},{1,2},{2,3},{3,0},{4,5},{5,6},{6,7},{7,4},{8,9},{9,10},{10,1... | collective-permute-start | bytes 786440 | tf_op jit(solution)/shard_map/ppermute | solution.py:17
  69.7 8.6 %collective-permute-start.7 = (bf16[1,2,2,128,256]{4,3,2,1,0:T(8,128)(2,1)S(1)}, bf16[1,2,2,128,256]{4,3,2,1,0:T(8,128)(2,1)S(1)}, u32[]{:S(2)}, u32[]{:S(2)}) collective-permute-start(bf16[1,2,2,128,256]{4,3,2,1,0:T(8,128)(2,1)S(1)} %get-tuple-element.41), channel_id=1, source_target_pairs={{0,3},{1,0},{2,1},{3,2},{4,7},{5,4},{6,5},{7,6},{8,11},{9,8},{10,9... | collective-permute-start | bytes 786440 | tf_op jit(solution)/shard_map/ppermute | solution.py:17
  74.2 5.8 %collective-permute-start.10 = (bf16[2,2,1,128,256]{4,3,2,1,0:T(8,128)(2,1)S(1)}, bf16[2,2,1,128,256]{4,3,2,1,0:T(8,128)(2,1)S(1)}, u32[]{:S(2)}, u32[]{:S(2)}) collective-permute-start(bf16[2,2,1,128,256]{4,3,2,1,0:T(8,128)(2,1)S(1)} %get-tuple-element.44), channel_id=1, source_target_pairs={{0,32},{32,64},{64,96},{96,128},{128,160},{160,192},{192,224},{224... | collective-permute-start | bytes 786440 | tf_op jit(solution)/shard_map/ppermute | solution.py:17
  74.2 5.8 %collective-permute-start.11 = (bf16[2,2,1,128,256]{4,3,2,1,0:T(8,128)(2,1)S(1)}, bf16[2,2,1,128,256]{4,3,2,1,0:T(8,128)(2,1)S(1)}, u32[]{:S(2)}, u32[]{:S(2)}) collective-permute-start(bf16[2,2,1,128,256]{4,3,2,1,0:T(8,128)(2,1)S(1)} %get-tuple-element.45), channel_id=1, source_target_pairs={{0,480},{32,0},{64,32},{96,64},{128,96},{160,128},{192,160},{224,1... | collective-permute-start | bytes 786440 | tf_op jit(solution)/shard_map/ppermute | solution.py:17

commit v2 on v1

v2 whole, which is shorter than its diff:
```python
import jax
import jax.numpy as jnp
from jax import lax
from jax.experimental import pallas as pl
from jax.experimental.pallas import tpu as pltpu
from jax.sharding import Mesh, PartitionSpec as P

ALL_AXES = ("ty", "tc", "gz", "gy")
TIME_AXES = ("ty", "tc")
SLOT_ROWS = 16
SITES = 8
BITS = (4, 2, 1)
LOW = tuple(tuple(s for s in range(SITES) if not s & bit) for bit in BITS)
HIGH = tuple(tuple(s for s in range(SITES) if s & bit) for bit in BITS)
VMEM_LIMIT = 24 * 1024 * 1024
WHOLE = pl.BlockSpec(memory_space=pltpu.VMEM)
SCALARS = pl.BlockSpec(memory_space=pltpu.SMEM)


def call(body, outs, ins, cost=None, scratch=()):
    return pl.pallas_call(
        body,
        out_shape=outs,
        in_specs=ins,
        out_specs=[WHOLE] * len(outs),
        scratch_shapes=scratch,
        cost_estimate=cost,
        compiler_params=pltpu.CompilerParams(vmem_limit_bytes=VMEM_LIMIT),
    )


def shape_of(shape, dtype):
    return jax.ShapeDtypeStruct(shape, dtype)


def shifted(values, axes, step):
    count = lax.axis_size(axes)
    return lax.ppermute(values, axes, [(i, (i + step) % count) for i in range(count)])


def pack_body(owners, slots, rows, payload):
    count, depth = rows.shape[0], rows.shape[1]
    for j in range(count):
        to = owners[j]
        payload[to, 0:depth, :] = rows[j]
        mark = jnp.full((SLOT_ROWS, rows.shape[2]), slots[j].astype(jnp.float32))
        payload[to, depth : depth + SLOT_ROWS, :] = mark.astype(payload.dtype)


def pack(rows, owners, slots):
    count, depth, width = rows.shape
    return call(
        pack_body,
        [shape_of((count, depth + SLOT_ROWS, width), rows.dtype)],
        [SCALARS, SCALARS, WHOLE],
    )(owners, slots, rows)[0]


def cut_faces(field, faces):
    for axis in range(3):
        for f in range(4):
            faces[2 * axis][f] = field[LOW[axis][f]]
            faces[2 * axis + 1][f] = field[HIGH[axis][f]]


def place_body(landed, field, *faces):
    depth = field.shape[1]
    for j in range(SITES):
        mark = landed[j, depth : depth + SLOT_ROWS, 0:128].astype(jnp.float32)
        slot = jnp.max(mark).astype(jnp.int32)
        field[slot] = landed[j, 0:depth, :]
    cut_faces(field, faces)


def place(landed):
    count, depth, width = landed.shape
    depth = depth - SLOT_ROWS
    face = shape_of((4, depth, width), landed.dtype)
    out = call(place_body, [shape_of((count, depth, width), landed.dtype)] + [face] * 6, [WHOLE])(landed)
    return out[0], out[1:]


def exchange(faces):
    (low_y, high_y, low_z, high_z, low_t, high_t) = faces
    before_z = shifted(high_z, "gz", 1)
    before_y = shifted(high_y, "gy", 1)
    behind_z = shifted(low_z, "gz", -1)
    behind_y = shifted(low_y, "gy", -1)
    before_t = shifted(high_t, TIME_AXES, 1)
    behind_t = shifted(low_t, TIME_AXES, -1)
    return [before_y, behind_y, before_z, behind_z, before_t, behind_t]


def near_body(inside, field, out):
    for s in range(SITES):
        own = field[s]
        operand = jnp.concatenate([own, own, own] + [field[s ^ bit] for bit in BITS], axis=0)
        out[s] = jnp.dot(inside[s], operand, preferred_element_type=jnp.float32)


def near(inside, field):
    count, depth, width = field.shape
    cost = pl.CostEstimate(
        flops=2 * count * depth * 6 * depth * width, bytes_accessed=4 * 2**20, transcendentals=0
    )
    return call(near_body, [shape_of(field.shape, jnp.float32)], [WHOLE, WHOLE], cost)(inside, field)[0]


def far_operand(s, received):
    parts = []
    for axis, bit in enumerate(BITS):
        if s & bit:
            parts.append(received[2 * axis + 1][HIGH[axis].index(s)])
        else:
            parts.append(received[2 * axis][LOW[axis].index(s)])
    return jnp.concatenate(parts, axis=0)


def image_body(outside, partial, r0, r1, r2, r3, r4, r5, image, field, *faces):
    received = (r0, r1, r2, r3, r4, r5)
    for s in range(SITES):
        total = partial[s] + jnp.dot(
            outside[s], far_operand(s, received), preferred_element_type=jnp.float32
        )
        image[s] = total
        field[s] = total.astype(field.dtype)
    cut_faces(field, faces)


def first_image(outside, partial, received):
    count, depth, width = partial.shape
    dtype = received[0].dtype
    outs = [shape_of(partial.shape, jnp.float32), shape_of(partial.shape, dtype)]
    outs += [shape_of((4, depth, width), dtype)] * 6
    out = call(image_body, outs, [WHOLE] * 8)(outside, partial, *received)
    return out[0], out[1], out[2:]


def fold(values):
    return jnp.sum(values.reshape((values.shape[0] // 8, 8, values.shape[1])), axis=0)


def sums_body(outside, partial, r0, r1, r2, r3, r4, r5, image, source, out):
    received = (r0, r1, r2, r3, r4, r5)
    half = image.shape[1] // 2
    sums = [jnp.zeros((8, image.shape[2]), jnp.float32) for _ in range(8)]
    for s in range(SITES):
        second = partial[s] + jnp.dot(
            outside[s], far_operand(s, received), preferred_element_type=jnp.float32
        )
        first = image[s]
        start = source[s].astype(jnp.float32)
        w_re, w_im = second[:half], second[half:]
        i_re, i_im = first[:half], first[half:]
        s_re, s_im = start[:half], start[half:]
        terms = (
            i_re * i_re + i_im * i_im,
            i_re * s_re + i_im * s_im,
            i_re * s_im - i_im * s_re,
            i_re * w_re + i_im * w_im,
            i_re * w_im - i_im * w_re,
            w_re * s_re + w_im * s_im,
            w_re * s_im - w_im * s_re,
            w_re * w_re + w_im * w_im,
        )
        sums = [a + fold(b) for a, b in zip(sums, terms)]
    rows = jnp.concatenate([jnp.sum(a, axis=0, keepdims=True) for a in sums], axis=0)
    for i in range(out.shape[0]):
        out[i] = rows


def local_sums(outside, partial, received, image, source, copies):
    width = image.shape[2]
    return call(sums_body, [shape_of((copies, 8, width), jnp.float32)], [WHOLE] * 10)(
        outside, partial, *received, image, source
    )[0]


def combine_body(landed, image, source, out):
    half = image.shape[1] // 2
    totals = jnp.sum(landed[...], axis=0)
    norm, c_re, c_im, d_re, d_im, e_re, e_im, tail = [totals[i : i + 1] for i in range(8)]
    a_re, a_im = c_re / norm, c_im / norm
    g_re, g_im = d_re / norm, d_im / norm
    p_re, p_im = c_re - a_re * norm, c_im - a_im * norm
    q_re = e_re - (a_re * d_re + a_im * d_im)
    q_im = e_im - (a_im * d_re - a_re * d_im)
    num_re = g_re * p_re + g_im * p_im - q_re
    num_im = g_re * p_im - g_im * p_re - q_im
    denom = tail - (g_re * d_re + g_im * d_im)
    y_re, y_im = num_re / denom, num_im / denom
    x_re = a_re + y_re * g_re - y_im * g_im
    x_im = a_im + y_re * g_im + y_im * g_re
    for s in range(SITES):
        first = image[s]
        start = source[s].astype(jnp.float32)
        i_re, i_im = first[:half], first[half:]
        s_re, s_im = start[:half], start[half:]
        out_re = x_re * s_re - x_im * s_im - (y_re * i_re - y_im * i_im)
        out_im = x_re * s_im + x_im * s_re - (y_re * i_im + y_im * i_re)
        out[s, 0:half, :] = out_re.astype(out.dtype)
        out[s, half:, :] = out_im.astype(out.dtype)


def combine(landed, image, source):
    return call(combine_body, [shape_of(source.shape, source.dtype)], [WHOLE] * 3)(
        landed, image, source
    )[0]


def block_double(blocks):
    columns = blocks.shape[-1] // 2
    real_blk = blocks[..., :columns]
    imag_blk = blocks[..., columns:]
    upper = jnp.concatenate([real_blk, -imag_blk], axis=-1)
    lower = jnp.concatenate([imag_blk, real_blk], axis=-1)
    return jnp.concatenate([upper, lower], axis=-2)


def split_couplings(doubled):
    inside = [doubled[0], doubled[1], doubled[2]]
    outside = []
    for dim in range(3):
        ahead, behind = doubled[3 + 2 * dim], doubled[4 + 2 * dim]
        pick = lambda a, s: lax.slice_in_dim(a, s, s + 1, axis=dim)
        inside.append(jnp.concatenate([pick(ahead, 0), pick(behind, 1)], axis=dim))
        outside.append(jnp.concatenate([pick(behind, 0), pick(ahead, 1)], axis=dim))
    flat = lambda a: a.reshape((SITES,) + a.shape[-2:])
    return flat(jnp.concatenate(inside, axis=-1)), flat(jnp.concatenate(outside, axis=-1))


def everyone(parts, axes):
    return lax.all_to_all(parts, axes, split_axis=0, concat_axis=0, tiled=True)


def local(restricted, couplings, owners, coarse_site):
    count, width = restricted.shape[0], restricted.shape[-1]
    rows = restricted.reshape(count, -1, width)
    landed = everyone(pack(rows, owners, coarse_site), "gz")
    inside, outside = split_couplings(block_double(couplings[:, 0]))
    source, faces = place(landed)
    received = exchange(faces)
    image, field, faces = first_image(outside, near(inside, source), received)
    received = exchange(faces)
    group, rest = ("tc", "gz"), ("ty", "gy")
    parts = local_sums(
        outside, near(inside, field), received, image, source, lax.axis_size(group)
    )
    parts = jnp.sum(everyone(parts, group), axis=0)
    parts = jnp.broadcast_to(parts[None], (lax.axis_size(rest),) + parts.shape)
    out = combine(everyone(parts, rest), image, source)
    return out.reshape(couplings.shape[1:5] + restricted.shape[1:])


def solution(mesh):
    cores = 2
    fine = Mesh(
        mesh.devices.reshape((mesh.shape["ta"] // cores, cores) + mesh.devices.shape[1:]),
        ALL_AXES,
    )
    return jax.shard_map(
        local,
        mesh=fine,
        in_specs=(
            P(ALL_AXES, None, None, None),
            P(None, None, "gy", "gz", TIME_AXES, None, None),
            P(ALL_AXES),
            P(ALL_AXES),
        ),
        out_specs=P(None, "gy", "gz", TIME_AXES, None, None, None),
        check_vma=False,
    )
```

time: 117 us -> 109 us (0.932)
  the two profiles are of different devices: /device:TPU:8 before, /device:TPU:64 now
where the time goes in v2:
time: 109 us
  starting transfers between devices  42.3 us (39%)
  blocking collectives  33.7 us (31%)
  waiting for transfers between devices  17.4 us (16%)
  Pallas kernels  5.37 us (5%)
  other arithmetic  5.14 us (5%)
  local copies, waits for them, and re-layouts  4.38 us (4%)
    all_to_all x2, blocking collectives, everyone(): return lax.all_to_all(parts, axes, split_axis=0, concat_axis=0, tiled=True)  33.7 us
    ppermute x12, starting transfers between devices, shifted(): lax.ppermute(values, axes, [(i, (i + step) % count) for i in range(count)])  32.4 us
    all_to_all x1, waiting for transfers between devices, everyone(): return lax.all_to_all(parts, axes, split_axis=0, concat_axis=0, tiled=True)  11.8 us
    all_to_all x1, starting transfers between devices, everyone(): return lax.all_to_all(parts, axes, split_axis=0, concat_axis=0, tiled=True)  9.96 us
    ppermute x12, waiting for transfers between devices, shifted(): lax.ppermute(values, axes, [(i, (i + step) % count) for i in range(count)])  5.51 us
    unnamed x15, local copies, waits for them, and re-layouts  2.66 us
  transfers between devices with their start and end apart: 13, of which 5 were waited for; matrix products, arithmetic and copies ran while one was open for 7% of the time, Pallas kernels for 1%

profile of v2, /device:TPU:64, one launch (start us, length us, event | category | flops | bytes accessed | tf_op | source)
XLA Modules:
  0.0 108.5 jit_solution(12510158415319299403)
XLA Ops:
  0.0 1.0 copy-done
  1.0 0.7 copy-done.1
  1.7 0.7 copy-done.2
  2.4 1.4 %shard_map.46 = bf16[8,144,256]{2,1,0:T(8,128)(2,1)} custom-call(s32[8]{0:T(128)S(1)} %copy-done.1, s32[8]{0:T(128)S(1)} %copy-done.2, bf16[8,128,256]{2,1,0:T(8,128)(2,1)S(1)} %bitcast.28), custom_call_target="tpu_custom_call" | custom-call | tf_op jit(solution)/shard_map/pallas_call | solution.py:52
  3.8 10.0 %all-to-all-start = ((bf16[8,144,256]{2,1,0:T(8,128)(2,1)}), bf16[8,144,256]{2,1,0:T(8,128)(2,1)S(1)}, u32[]{:S(2)}, u32[]{:S(2)}) async-start(bf16[8,144,256]{2,1,0:T(8,128)(2,1)} %shard_map.46), calls=%async_computation | async-start | bytes 1179648 | tf_op jit(solution)/shard_map/all_to_all | solution.py:233
  13.7 0.5 slice_negate_fusion
  14.2 1.0 maximum_bitcast_fusion.1
  15.2 1.6 %maximum_maximum_fusion = bf16[9,2,2,2,128,128]{5,4,3,2,1,0:T(8,128)(2,1)S(1)} fusion(bf16[9,2,2,2,64,64]{5,4,3,2,1,0:T(8,128)(2,1)S(1)} %get-tuple-element.48, bf16[9,2,2,2,64,64]{5,4,3,2,1,0:T(8,128)(2,1)S(1)} %get-tuple-element.47, bf16[9,2,2,2,64,64]{5,4,3,2,1,0:T(8,128)(2,1)S(1)} %get-tuple-element.46), kind=kLoop, calls=%fused_computation | loop fusion | flops 9437184 | bytes 4128768 | tf_op jit(solution)/shard_map/concatenate | solution.py:217
  16.8 0.2 fusion
  17.0 0.7 fusion.1
  17.8 0.7 fusion.3
  18.5 0.7 pad_maximum_fusion.1
  19.3 0.1 constant_dynamic-update-slice_fusion.4
  19.3 11.8 %all-to-all-done.landed = bf16[8,144,256]{2,1,0:T(8,128)(2,1)S(1)} async-done(((bf16[8,144,256]{2,1,0:T(8,128)(2,1)}), bf16[8,144,256]{2,1,0:T(8,128)(2,1)S(1)}, u32[]{:S(2)}, u32[]{:S(2)}) %all-to-all-start) | async-done | bytes 589856 | tf_op jit(solution)/shard_map/all_to_all | solution.py:233
  31.2 0.3 shard_map.47
  31.4 3.4 %collective-permute-start = (bf16[4,128,256]{2,1,0:T(8,128)(2,1)S(1)}, bf16[4,128,256]{2,1,0:T(8,128)(2,1)S(1)}, u32[]{:S(2)}, u32[]{:S(2)}) collective-permute-start(bf16[4,128,256]{2,1,0:T(8,128)(2,1)S(1)} %get-tuple-element.21), channel_id=1, source_target_pairs={{0,1},{1,2},{2,3},{3,0},{4,5},{5,6},{6,7},{7,4},{8,9},{9,10},{10,1... | collective-permute-start | bytes 786440 | tf_op jit(solution)/shard_map/ppermute | solution.py:38
  34.9 0.1 constant_dynamic-update-slice_fusion.3
  34.9 0.1 constant_dynamic-update-slice_fusion.2
  35.0 0.1 constant_dynamic-update-slice_fusion.1
  35.1 3.7 %collective-permute-start.1 = (bf16[4,128,256]{2,1,0:T(8,128)(2,1)S(1)}, bf16[4,128,256]{2,1,0:T(8,128)(2,1)S(1)}, u32[]{:S(2)}, u32[]{:S(2)}) collective-permute-start(bf16[4,128,256]{2,1,0:T(8,128)(2,1)S(1)} %get-tuple-element.22), channel_id=1, source_target_pairs={{0,3},{1,0},{2,1},{3,2},{4,7},{5,4},{6,5},{7,6},{8,11},{9,8},{10,9... | collective-permute-start | bytes 786440 | tf_op jit(solution)/shard_map/ppermute | solution.py:38
  38.7 1.9 %collective-permute-start.2 = (bf16[4,128,256]{2,1,0:T(8,128)(2,1)S(1)}, bf16[4,128,256]{2,1,0:T(8,128)(2,1)S(1)}, u32[]{:S(2)}, u32[]{:S(2)}) collective-permute-start(bf16[4,128,256]{2,1,0:T(8,128)(2,1)S(1)} %get-tuple-element.23), channel_id=1, source_target_pairs={{0,4},{4,8},{8,12},{12,16},{16,20},{20,24},{24,28},{28,0},{1,5},{5... | collective-permute-start | bytes 786440 | tf_op jit(solution)/shard_map/ppermute | solution.py:38
  40.7 3.9 %collective-permute-start.3 = (bf16[4,128,256]{2,1,0:T(8,128)(2,1)S(1)}, bf16[4,128,256]{2,1,0:T(8,128)(2,1)S(1)}, u32[]{:S(2)}, u32[]{:S(2)}) collective-permute-start(bf16[4,128,256]{2,1,0:T(8,128)(2,1)S(1)} %get-tuple-element.24), channel_id=1, source_target_pairs={{0,28},{4,0},{8,4},{12,8},{16,12},{20,16},{24,20},{28,24},{1,29},{... | collective-permute-start | bytes 786440 | tf_op jit(solution)/shard_map/ppermute | solution.py:38
  44.6 0.0 collective-permute-start.4
  44.6 0.0 collective-permute-done.r0
  44.6 2.9 %collective-permute-start.5 = (bf16[4,128,256]{2,1,0:T(8,128)(2,1)S(1)}, bf16[4,128,256]{2,1,0:T(8,128)(2,1)S(1)}, u32[]{:S(2)}, u32[]{:S(2)}) collective-permute-start(bf16[4,128,256]{2,1,0:T(8,128)(2,1)S(1)} %get-tuple-element.26), channel_id=1, source_target_pairs={{0,480},{32,0},{64,32},{96,64},{128,96},{160,128},{192,160},{224,1... | collective-permute-start | bytes 786440 | tf_op jit(solution)/shard_map/ppermute | solution.py:38
  47.6 0.1 constant_dynamic-update-slice_fusion.inside
  47.6 1.3 %maximum_maximum_fusion.1 = bf16[2,2,2,128,384]{4,3,2,1,0:T(8,128)(2,1)S(1)} fusion(bf16[2,2,1,128,128]{4,3,2,1,0:T(8,128)(2,1)} %get-tuple-element.50, bf16[2,2,1,128,128]{4,3,2,1,0:T(8,128)(2,1)} %get-tuple-element.57, bf16[2,1,2,128,128]{4,3,2,1,0:T(8,128)(2,1)} %get-tuple-element.54, bf16[2,1,2,128,128]{4,3,2,1,0:T(8,128)(2,1)} %get-tuple-element.59, ...), kind=kLoop, calls=%fused_computation.1 | loop fusion | flops 4718592 | bytes 1572864 | tf_op jit(solution)/shard_map/concatenate | solution.py:229
  49.0 0.6 shard_map.48.partial
  49.6 0.0 collective-permute-done.1.r1
  49.6 0.0 collective-permute-done.2.r2
  49.6 0.0 collective-permute-done.3.r3
  49.6 2.0 %collective-permute-done.4.r4 = bf16[4,128,256]{2,1,0:T(8,128)(2,1)S(1)} collective-permute-done((bf16[4,128,256]{2,1,0:T(8,128)(2,1)S(1)}, bf16[4,128,256]{2,1,0:T(8,128)(2,1)S(1)}, u32[]{:S(2)}, u32[]{:S(2)}) %collective-permute-start.4) | collective-permute-done | bytes 262176 | tf_op jit(solution)/shard_map/ppermute | solution.py:38
  51.6 0.5 shard_map.49
  52.1 2.2 %collective-permute-start.6 = (bf16[4,128,256]{2,1,0:T(8,128)(2,1)S(1)}, bf16[4,128,256]{2,1,0:T(8,128)(2,1)S(1)}, u32[]{:S(2)}, u32[]{:S(2)}) collective-permute-start(bf16[4,128,256]{2,1,0:T(8,128)(2,1)S(1)} %get-tuple-element.28), channel_id=1, source_target_pairs={{0,1},{1,2},{2,3},{3,0},{4,5},{5,6},{6,7},{7,4},{8,9},{9,10},{10,1... | collective-permute-start | bytes 786440 | tf_op jit(solution)/shard_map/ppermute | solution.py:38
  54.3 4.9 %collective-permute-start.7 = (bf16[4,128,256]{2,1,0:T(8,128)(2,1)S(1)}, bf16[4,128,256]{2,1,0:T(8,128)(2,1)S(1)}, u32[]{:S(2)}, u32[]{:S(2)}) collective-permute-start(bf16[4,128,256]{2,1,0:T(8,128)(2,1)S(1)} %get-tuple-element.29), channel_id=1, source_target_pairs={{0,3},{1,0},{2,1},{3,2},{4,7},{5,4},{6,5},{7,6},{8,11},{9,8},{10,9... | collective-permute-start | bytes 786440 | tf_op jit(solution)/shard_map/ppermute | solution.py:38
  59.2 1.9 %collective-permute-start.8 = (bf16[4,128,256]{2,1,0:T(8,128)(2,1)S(1)}, bf16[4,128,256]{2,1,0:T(8,128)(2,1)S(1)}, u32[]{:S(2)}, u32[]{:S(2)}) collective-permute-start(bf16[4,128,256]{2,1,0:T(8,128)(2,1)S(1)} %get-tuple-element.30), channel_id=1, source_target_pairs={{0,4},{4,8},{8,12},{12,16},{16,20},{20,24},{24,28},{28,0},{1,5},{5... | collective-permute-start | bytes 786440 | tf_op jit(solution)/shard_map/ppermute | solution.py:38
  61.1 4.6 %collective-permute-start.9 = (bf16[4,128,256]{2,1,0:T(8,128)(2,1)S(1)}, bf16[4,128,256]{2,1,0:T(8,128)(2,1)S(1)}, u32[]{:S(2)}, u32[]{:S(2)}) collective-permute-start(bf16[4,128,256]{2,1,0:T(8,128)(2,1)S(1)} %get-tuple-element.31), channel_id=1, source_target_pairs={{0,28},{4,0},{8,4},{12,8},{16,12},{20,16},{24,20},{28,24},{1,29},{... | collective-permute-start | bytes 786440 | tf_op jit(solution)/shard_map/ppermute | solution.py:38
  65.7 0.0 collective-permute-start.10
  65.8 2.9 %collective-permute-start.11 = (bf16[4,128,256]{2,1,0:T(8,128)(2,1)S(1)}, bf16[4,128,256]{2,1,0:T(8,128)(2,1)S(1)}, u32[]{:S(2)}, u32[]{:S(2)}) collective-permute-start(bf16[4,128,256]{2,1,0:T(8,128)(2,1)S(1)} %get-tuple-element.33), channel_id=1, source_target_pairs={{0,480},{32,0},{64,32},{96,64},{128,96},{160,128},{192,160},{224,1... | collective-permute-start | bytes 786440 | tf_op jit(solution)/shard_map/ppermute | solution.py:38
  68.7 0.6 shard_map.50.partial
  69.3 0.0 collective-permute-done.7.r1
  69.3 0.9 collective-permute-done.8.r2
  70.2 1.2 %collective-permute-done.9.r3 = bf16[4,128,256]{2,1,0:T(8,128)(2,1)S(1)} collective-permute-done((bf16[4,128,256]{2,1,0:T(8,128)(2,1)S(1)}, bf16[4,128,256]{2,1,0:T(8,128)(2,1)S(1)}, u32[]{:S(2)}, u32[]{:S(2)}) %collective-permute-start.9) | collective-permute-done | bytes 262176 | tf_op jit(solution)/shard_map/ppermute | solution.py:38
  71.3 1.4 %collective-permute-done.10.r4 = bf16[4,128,256]{2,1,0:T(8,128)(2,1)S(1)} collective-permute-done((bf16[4,128,256]{2,1,0:T(8,128)(2,1)S(1)}, bf16[4,128,256]{2,1,0:T(8,128)(2,1)S(1)}, u32[]{:S(2)}, u32[]{:S(2)}) %collective-permute-start.10) | collective-permute-done | bytes 262176 | tf_op jit(solution)/shard_map/ppermute | solution.py:38
  72.7 0.9 shard_map.51
  73.6 14.5 %all_to_all.15 = f32[16,8,256]{2,1,0:T(8,128)S(1)} all-to-all(f32[16,8,256]{2,1,0:T(8,128)S(1)} %shard_map.51), channel_id=1, replica_groups=mesh['ty'=8,'tc'=2,'gz'=8,'gy'=4] {'tc','gz'}, dimensions={0} | all-to-all | bytes 262144 | tf_op jit(solution)/shard_map/all_to_all | solution.py:233
  88.2 19.1 %all_to_all.16.landed = f32[32,8,256]{2,1,0:T(8,128)S(1)} all-to-all(f32[32,8,256]{2,1,0:T(8,128)S(1)} %broadcast_in_dim.2), channel_id=1, replica_groups=mesh['ty'=8,'tc'=2,'gz'=8,'gy'=4] {'ty','gy'}, dimensions={0} | all-to-all | bytes 524288 | tf_op jit(solution)/shard_map/all_to_all | solution.py:233
  107.4 1.2 %shard_map.52 = bf16[8,128,256]{2,1,0:T(8,128)(2,1)} custom-call(f32[32,8,256]{2,1,0:T(8,128)S(1)} %all_to_all.16.landed, f32[8,128,256]{2,1,0:T(8,128)S(1)} %get-tuple-element.34.image, bf16[8,128,256]{2,1,0:T(8,128)(2,1)S(1)} %get-tuple-element.20.field.source), custom_call_target="tpu_custom_call" | custom-call | tf_op jit(solution)/shard_map/pallas_call | solution.py:206
  (15 shorter events, 0.2 us)
Async XLA Ops:
  0.0 1.0 copy-start
  1.0 0.7 copy-start.1
  1.7 0.7 copy-start.2
  2.4 11.4 %copy-start.3 = (bf16[9,1,2,2,2,64,128]{6,5,4,3,2,1,0:T(8,128)(2,1)S(1)}, bf16[9,1,2,2,2,64,128]{6,5,4,3,2,1,0:T(8,128)(2,1)}, u32[]{:S(2)}) copy-start(bf16[9,1,2,2,2,64,128]{6,5,4,3,2,1,0:T(8,128)(2,1)} %param.5) | copy-start | bytes 3538948
  3.8 27.4 %all-to-all-start = ((bf16[8,144,256]{2,1,0:T(8,128)(2,1)}), bf16[8,144,256]{2,1,0:T(8,128)(2,1)S(1)}, u32[]{:S(2)}, u32[]{:S(2)}) async-start(bf16[8,144,256]{2,1,0:T(8,128)(2,1)} %shard_map.46), calls=%async_computation | async-start | bytes 1179648 | tf_op jit(solution)/shard_map/all_to_all | solution.py:233
  31.2 3.8 %copy-start.4 = (bf16[2,2,2,128,128]{4,3,2,1,0:T(8,128)(2,1)S(1)}, bf16[2,2,2,128,128]{4,3,2,1,0:T(8,128)(2,1)}, u32[]{:S(2)}) copy-start(bf16[2,2,2,128,128]{4,3,2,1,0:T(8,128)(2,1)} %pad_maximum_fusion.1) | copy-start | bytes 786436
  31.4 13.2 %collective-permute-start = (bf16[4,128,256]{2,1,0:T(8,128)(2,1)S(1)}, bf16[4,128,256]{2,1,0:T(8,128)(2,1)S(1)}, u32[]{:S(2)}, u32[]{:S(2)}) collective-permute-start(bf16[4,128,256]{2,1,0:T(8,128)(2,1)S(1)} %get-tuple-element.21), channel_id=1, source_target_pairs={{0,1},{1,2},{2,3},{3,0},{4,5},{5,6},{6,7},{7,4},{8,9},{9,10},{10,1... | collective-permute-start | bytes 786440 | tf_op jit(solution)/shard_map/ppermute | solution.py:38
  35.1 14.5 %collective-permute-start.1 = (bf16[4,128,256]{2,1,0:T(8,128)(2,1)S(1)}, bf16[4,128,256]{2,1,0:T(8,128)(2,1)S(1)}, u32[]{:S(2)}, u32[]{:S(2)}) collective-permute-start(bf16[4,128,256]{2,1,0:T(8,128)(2,1)S(1)} %get-tuple-element.22), channel_id=1, source_target_pairs={{0,3},{1,0},{2,1},{3,2},{4,7},{5,4},{6,5},{7,6},{8,11},{9,8},{10,9... | collective-permute-start | bytes 786440 | tf_op jit(solution)/shard_map/ppermute | solution.py:38
  38.7 10.8 %collective-permute-start.2 = (bf16[4,128,256]{2,1,0:T(8,128)(2,1)S(1)}, bf16[4,128,256]{2,1,0:T(8,128)(2,1)S(1)}, u32[]{:S(2)}, u32[]{:S(2)}) collective-permute-start(bf16[4,128,256]{2,1,0:T(8,128)(2,1)S(1)} %get-tuple-element.23), channel_id=1, source_target_pairs={{0,4},{4,8},{8,12},{12,16},{16,20},{20,24},{24,28},{28,0},{1,5},{5... | collective-permute-start | bytes 786440 | tf_op jit(solution)/shard_map/ppermute | solution.py:38
  40.7 8.9 %collective-permute-start.3 = (bf16[4,128,256]{2,1,0:T(8,128)(2,1)S(1)}, bf16[4,128,256]{2,1,0:T(8,128)(2,1)S(1)}, u32[]{:S(2)}, u32[]{:S(2)}) collective-permute-start(bf16[4,128,256]{2,1,0:T(8,128)(2,1)S(1)} %get-tuple-element.24), channel_id=1, source_target_pairs={{0,28},{4,0},{8,4},{12,8},{16,12},{20,16},{24,20},{28,24},{1,29},{... | collective-permute-start | bytes 786440 | tf_op jit(solution)/shard_map/ppermute | solution.py:38
  44.6 7.0 %collective-permute-start.4 = (bf16[4,128,256]{2,1,0:T(8,128)(2,1)S(1)}, bf16[4,128,256]{2,1,0:T(8,128)(2,1)S(1)}, u32[]{:S(2)}, u32[]{:S(2)}) collective-permute-start(bf16[4,128,256]{2,1,0:T(8,128)(2,1)S(1)} %get-tuple-element.25), channel_id=1, source_target_pairs={{0,32},{32,64},{64,96},{96,128},{128,160},{160,192},{192,224},{224... | collective-permute-start | bytes 786440 | tf_op jit(solution)/shard_map/ppermute | solution.py:38
  44.6 7.0 %collective-permute-start.5 = (bf16[4,128,256]{2,1,0:T(8,128)(2,1)S(1)}, bf16[4,128,256]{2,1,0:T(8,128)(2,1)S(1)}, u32[]{:S(2)}, u32[]{:S(2)}) collective-permute-start(bf16[4,128,256]{2,1,0:T(8,128)(2,1)S(1)} %get-tuple-element.26), channel_id=1, source_target_pairs={{0,480},{32,0},{64,32},{96,64},{128,96},{160,128},{192,160},{224,1... | collective-permute-start | bytes 786440 | tf_op jit(solution)/shard_map/ppermute | solution.py:38
  52.1 13.6 %collective-permute-start.6 = (bf16[4,128,256]{2,1,0:T(8,128)(2,1)S(1)}, bf16[4,128,256]{2,1,0:T(8,128)(2,1)S(1)}, u32[]{:S(2)}, u32[]{:S(2)}) collective-permute-start(bf16[4,128,256]{2,1,0:T(8,128)(2,1)S(1)} %get-tuple-element.28), channel_id=1, source_target_pairs={{0,1},{1,2},{2,3},{3,0},{4,5},{5,6},{6,7},{7,4},{8,9},{9,10},{10,1... | collective-permute-start | bytes 786440 | tf_op jit(solution)/shard_map/ppermute | solution.py:38
  54.3 14.9 %collective-permute-start.7 = (bf16[4,128,256]{2,1,0:T(8,128)(2,1)S(1)}, bf16[4,128,256]{2,1,0:T(8,128)(2,1)S(1)}, u32[]{:S(2)}, u32[]{:S(2)}) collective-permute-start(bf16[4,128,256]{2,1,0:T(8,128)(2,1)S(1)} %get-tuple-element.29), channel_id=1, source_target_pairs={{0,3},{1,0},{2,1},{3,2},{4,7},{5,4},{6,5},{7,6},{8,11},{9,8},{10,9... | collective-permute-start | bytes 786440 | tf_op jit(solution)/shard_map/ppermute | solution.py:38
  59.2 11.0 %collective-permute-start.8 = (bf16[4,128,256]{2,1,0:T(8,128)(2,1)S(1)}, bf16[4,128,256]{2,1,0:T(8,128)(2,1)S(1)}, u32[]{:S(2)}, u32[]{:S(2)}) collective-permute-start(bf16[4,128,256]{2,1,0:T(8,128)(2,1)S(1)} %get-tuple-element.30), channel_id=1, source_target_pairs={{0,4},{4,8},{8,12},{12,16},{16,20},{20,24},{24,28},{28,0},{1,5},{5... | collective-permute-start | bytes 786440 | tf_op jit(solution)/shard_map/ppermute | solution.py:38
  61.1 10.2 %collective-permute-start.9 = (bf16[4,128,256]{2,1,0:T(8,128)(2,1)S(1)}, bf16[4,128,256]{2,1,0:T(8,128)(2,1)S(1)}, u32[]{:S(2)}, u32[]{:S(2)}) collective-permute-start(bf16[4,128,256]{2,1,0:T(8,128)(2,1)S(1)} %get-tuple-element.31), channel_id=1, source_target_pairs={{0,28},{4,0},{8,4},{12,8},{16,12},{20,16},{24,20},{28,24},{1,29},{... | collective-permute-start | bytes 786440 | tf_op jit(solution)/shard_map/ppermute | solution.py:38
  65.7 7.0 %collective-permute-start.10 = (bf16[4,128,256]{2,1,0:T(8,128)(2,1)S(1)}, bf16[4,128,256]{2,1,0:T(8,128)(2,1)S(1)}, u32[]{:S(2)}, u32[]{:S(2)}) collective-permute-start(bf16[4,128,256]{2,1,0:T(8,128)(2,1)S(1)} %get-tuple-element.32), channel_id=1, source_target_pairs={{0,32},{32,64},{64,96},{96,128},{128,160},{160,192},{192,224},{224... | collective-permute-start | bytes 786440 | tf_op jit(solution)/shard_map/ppermute | solution.py:38
  65.8 7.0 %collective-permute-start.11 = (bf16[4,128,256]{2,1,0:T(8,128)(2,1)S(1)}, bf16[4,128,256]{2,1,0:T(8,128)(2,1)S(1)}, u32[]{:S(2)}, u32[]{:S(2)}) collective-permute-start(bf16[4,128,256]{2,1,0:T(8,128)(2,1)S(1)} %get-tuple-element.33), channel_id=1, source_target_pairs={{0,480},{32,0},{64,32},{96,64},{128,96},{160,128},{192,160},{224,1... | collective-permute-start | bytes 786440 | tf_op jit(solution)/shard_map/ppermute | solution.py:38

commit v3 on v2

--- a/solution.py
+++ b/solution.py
@@ -5,8 +5,8 @@
 from jax.experimental.pallas import tpu as pltpu
 from jax.sharding import Mesh, PartitionSpec as P
 
-ALL_AXES = ("ty", "tc", "gz", "gy")
-TIME_AXES = ("ty", "tc")
+ALL_AXES = ("ya", "yb", "tc", "gz", "gy")
+TIME_AXES = ("ya", "yb", "tc")
 SLOT_ROWS = 16
 SITES = 8
 BITS = (4, 2, 1)
@@ -14,15 +14,15 @@
 HIGH = tuple(tuple(s for s in range(SITES) if s & bit) for bit in BITS)
 VMEM_LIMIT = 24 * 1024 * 1024
 WHOLE = pl.BlockSpec(memory_space=pltpu.VMEM)
-SCALARS = pl.BlockSpec(memory_space=pltpu.SMEM)
-
-
-def call(body, outs, ins, cost=None, scratch=()):
+IN_HBM = pl.BlockSpec(memory_space=pltpu.HBM)
+
+
+def call(body, outs, ins, cost=None, scratch=(), out_spec=WHOLE):
     return pl.pallas_call(
         body,
         out_shape=outs,
         in_specs=ins,
-        out_specs=[WHOLE] * len(outs),
+        out_specs=[out_spec] * len(outs),
         scratch_shapes=scratch,
         cost_estimate=cost,
         compiler_params=pltpu.CompilerParams(vmem_limit_bytes=VMEM_LIMIT),
@@ -38,12 +38,21 @@
     return lax.ppermute(values, axes, [(i, (i + step) % count) for i in range(count)])
 
 
-def pack_body(owners, slots, rows, payload):
-    count, depth = rows.shape[0], rows.shape[1]
+def pack_body(owners, slots, rows, payload, owner_mem, slot_mem, row_mem, sems):
+    count, depth, width = rows.shape
+    copies = [
+        pltpu.make_async_copy(owners, owner_mem, sems.at[0]),
+        pltpu.make_async_copy(slots, slot_mem, sems.at[1]),
+        pltpu.make_async_copy(rows, row_mem, sems.at[2]),
+    ]
+    for copy in copies:
+        copy.start()
+    for copy in copies:
+        copy.wait()
     for j in range(count):
-        to = owners[j]
-        payload[to, 0:depth, :] = rows[j]
-        mark = jnp.full((SLOT_ROWS, rows.shape[2]), slots[j].astype(jnp.float32))
+        to = owner_mem[j]
+        payload[to, 0:depth, :] = row_mem[j]
+        mark = jnp.full((SLOT_ROWS, width), slot_mem[j].astype(jnp.float32))
         payload[to, depth : depth + SLOT_ROWS, :] = mark.astype(payload.dtype)
 
 
@@ -52,7 +61,13 @@
     return call(
         pack_body,
         [shape_of((count, depth + SLOT_ROWS, width), rows.dtype)],
-        [SCALARS, SCALARS, WHOLE],
+        [IN_HBM] * 3,
+        scratch=[
+            pltpu.SMEM(owners.shape, owners.dtype),
+            pltpu.SMEM(slots.shape, slots.dtype),
+            pltpu.VMEM(rows.shape, rows.dtype),
+            pltpu.SemaphoreType.DMA((3,)),
+        ],
     )(owners, slots, rows)[0]
 
 
@@ -91,19 +106,61 @@
     return [before_y, behind_y, before_z, behind_z, before_t, behind_t]
 
 
+def near_product(s, inside, field):
+    own = field[s]
+    operand = jnp.concatenate([own, own, own] + [field[s ^ bit] for bit in BITS], axis=0)
+    return jnp.dot(inside[s], operand, preferred_element_type=jnp.float32)
+
+
 def near_body(inside, field, out):
     for s in range(SITES):
-        own = field[s]
-        operand = jnp.concatenate([own, own, own] + [field[s ^ bit] for bit in BITS], axis=0)
-        out[s] = jnp.dot(inside[s], operand, preferred_element_type=jnp.float32)
-
-
-def near(inside, field):
+        out[s] = near_product(s, inside, field)
+
+
+def near_cost(field):
     count, depth, width = field.shape
-    cost = pl.CostEstimate(
+    return pl.CostEstimate(
         flops=2 * count * depth * 6 * depth * width, bytes_accessed=4 * 2**20, transcendentals=0
     )
-    return call(near_body, [shape_of(field.shape, jnp.float32)], [WHOLE, WHOLE], cost)(inside, field)[0]
+
+
+def near(inside, field):
+    return call(near_body, [shape_of(field.shape, jnp.float32)], [WHOLE] * 2, near_cost(field))(
+        inside, field
+    )[0]
+
+
+def fold(values):
+    return jnp.sum(values.reshape((values.shape[0] // 8, 8, values.shape[1])), axis=0)
+
+
+def row_sums(sums):
+    return jnp.concatenate([jnp.sum(a, axis=0, keepdims=True) for a in sums], axis=0)
+
+
+def halves(values):
+    half = values.shape[0] // 2
+    return values[:half], values[half:]
+
+
+def near_sums_body(inside, field, image, source, out, early):
+    sums = [jnp.zeros((8, image.shape[2]), jnp.float32) for _ in range(3)]
+    for s in range(SITES):
+        out[s] = near_product(s, inside, field)
+        i_re, i_im = halves(image[s])
+        s_re, s_im = halves(source[s].astype(jnp.float32))
+        terms = (
+            i_re * i_re + i_im * i_im,
+            i_re * s_re + i_im * s_im,
+            i_re * s_im - i_im * s_re,
+        )
+        sums = [a + fold(b) for a, b in zip(sums, terms)]
+    early[...] = row_sums(sums + [jnp.zeros((8, image.shape[2]), jnp.float32)] * 5)
+
+
+def near_sums(inside, field, image, source):
+    outs = [shape_of(field.shape, jnp.float32), shape_of((8, field.shape[2]), jnp.float32)]
+    return call(near_sums_body, outs, [WHOLE] * 4, near_cost(field))(inside, field, image, source)
 
 
 def far_operand(s, received):
@@ -136,27 +193,17 @@
     return out[0], out[1], out[2:]
 
 
-def fold(values):
-    return jnp.sum(values.reshape((values.shape[0] // 8, 8, values.shape[1])), axis=0)
-
-
-def sums_body(outside, partial, r0, r1, r2, r3, r4, r5, image, source, out):
+def sums_body(outside, partial, early, r0, r1, r2, r3, r4, r5, image, source, out):
     received = (r0, r1, r2, r3, r4, r5)
-    half = image.shape[1] // 2
-    sums = [jnp.zeros((8, image.shape[2]), jnp.float32) for _ in range(8)]
+    sums = [jnp.zeros((8, image.shape[2]), jnp.float32) for _ in range(5)]
     for s in range(SITES):
         second = partial[s] + jnp.dot(
             outside[s], far_operand(s, received), preferred_element_type=jnp.float32
         )
-        first = image[s]
-        start = source[s].astype(jnp.float32)
-        w_re, w_im = second[:half], second[half:]
-        i_re, i_im = first[:half], first[half:]
-        s_re, s_im = start[:half], start[half:]
+        w_re, w_im = halves(second)
+        i_re, i_im = halves(image[s])
+        s_re, s_im = halves(source[s].astype(jnp.float32))
         terms = (
-            i_re * i_re + i_im * i_im,
-            i_re * s_re + i_im * s_im,
-            i_re * s_im - i_im * s_re,
             i_re * w_re + i_im * w_im,
             i_re * w_im - i_im * w_re,
             w_re * s_re + w_im * s_im,
@@ -164,20 +211,19 @@
             w_re * w_re + w_im * w_im,
         )
         sums = [a + fold(b) for a, b in zip(sums, terms)]
-    rows = jnp.concatenate([jnp.sum(a, axis=0, keepdims=True) for a in sums], axis=0)
-    for i in range(out.shape[0]):
-        out[i] = rows
-
-
-def local_sums(outside, partial, received, image, source, copies):
-    width = image.shape[2]
-    return call(sums_body, [shape_of((copies, 8, width), jnp.float32)], [WHOLE] * 10)(
-        outside, partial, *received, image, source
+    nothing = jnp.zeros((8, image.shape[2]), jnp.float32)
+    out[...] = early[...] + row_sums([nothing] * 3 + sums)
+
+
+def local_sums(outside, partial, early, received, image, source):
+    return call(sums_body, [shape_of(early.shape, early.dtype)], [WHOLE] * 11)(
+        outside, partial, early, *received, image, source
     )[0]
 
 
-def combine_body(landed, image, source, out):
+def combine_body(landed, image, source, out, held, sems):
     half = image.shape[1] // 2
+    copies = []
     totals = jnp.sum(landed[...], axis=0)
     norm, c_re, c_im, d_re, d_im, e_re, e_im, tail = [totals[i : i + 1] for i in range(8)]
     a_re, a_im = c_re / norm, c_im / norm
@@ -192,20 +238,26 @@
     x_re = a_re + y_re * g_re - y_im * g_im
     x_im = a_im + y_re * g_im + y_im * g_re
     for s in range(SITES):
-        first = image[s]
-        start = source[s].astype(jnp.float32)
-        i_re, i_im = first[:half], first[half:]
-        s_re, s_im = start[:half], start[half:]
+        i_re, i_im = halves(image[s])
+        s_re, s_im = halves(source[s].astype(jnp.float32))
         out_re = x_re * s_re - x_im * s_im - (y_re * i_re - y_im * i_im)
         out_im = x_re * s_im + x_im * s_re - (y_re * i_im + y_im * i_re)
-        out[s, 0:half, :] = out_re.astype(out.dtype)
-        out[s, half:, :] = out_im.astype(out.dtype)
+        held[s, 0:half, :] = out_re.astype(held.dtype)
+        held[s, half:, :] = out_im.astype(held.dtype)
+        copies.append(pltpu.make_async_copy(held.at[s], out.at[s], sems.at[s]))
+        copies[s].start()
+    for copy in copies:
+        copy.wait()
 
 
 def combine(landed, image, source):
-    return call(combine_body, [shape_of(source.shape, source.dtype)], [WHOLE] * 3)(
-        landed, image, source
-    )[0]
+    return call(
+        combine_body,
+        [shape_of(source.shape, source.dtype)],
+        [WHOLE] * 3,
+        scratch=[pltpu.VMEM(source.shape, source.dtype), pltpu.SemaphoreType.DMA((SITES,))],
+        out_spec=IN_HBM,
+    )(landed, image, source)[0]
 
 
 def block_double(blocks):
@@ -229,6 +281,10 @@
     return flat(jnp.concatenate(inside, axis=-1)), flat(jnp.concatenate(outside, axis=-1))
 
 
+def copies_of(parts, axes):
+    return jnp.broadcast_to(parts[None], (lax.axis_size(axes),) + parts.shape)
+
+
 def everyone(parts, axes):
     return lax.all_to_all(parts, axes, split_axis=0, concat_axis=0, tiled=True)
 
@@ -242,22 +298,18 @@
     received = exchange(faces)
     image, field, faces = first_image(outside, near(inside, source), received)
     received = exchange(faces)
-    group, rest = ("tc", "gz"), ("ty", "gy")
-    parts = local_sums(
-        outside, near(inside, field), received, image, source, lax.axis_size(group)
-    )
-    parts = jnp.sum(everyone(parts, group), axis=0)
-    parts = jnp.broadcast_to(parts[None], (lax.axis_size(rest),) + parts.shape)
-    out = combine(everyone(parts, rest), image, source)
+    partial, early = near_sums(inside, field, image, source)
+    parts = local_sums(outside, partial, early, received, image, source)
+    parts = jnp.sum(lax.all_gather(parts, "tc"), axis=0)
+    parts = jnp.sum(everyone(copies_of(parts, ("yb", "gz")), ("yb", "gz")), axis=0)
+    parts = everyone(copies_of(parts, ("ya", "gy")), ("ya", "gy"))
+    out = combine(parts, image, source)
     return out.reshape(couplings.shape[1:5] + restricted.shape[1:])
 
 
 def solution(mesh):
-    cores = 2
-    fine = Mesh(
-        mesh.devices.reshape((mesh.shape["ta"] // cores, cores) + mesh.devices.shape[1:]),
-        ALL_AXES,
-    )
+    count = mesh.shape["ta"]
+    fine = Mesh(mesh.devices.reshape((count // 4, 2, 2) + mesh.devices.shape[1:]), ALL_AXES)
     return jax.shard_map(
         local,
         mesh=fine,

time: 109 us -> 110 us (level)
  the two profiles are of different devices: /device:TPU:64 before, /device:TPU:8 now
where the time goes in v3:
time: 110 us
  starting transfers between devices  42 us (38%)
  blocking collectives  31.9 us (29%)
  waiting for transfers between devices  17.3 us (16%)
  other arithmetic  6.38 us (6%)
  local copies, waits for them, and re-layouts  6.29 us (6%)
  Pallas kernels  5.32 us (5%)
    ppermute x12, starting transfers between devices, shifted(): lax.ppermute(values, axes, [(i, (i + step) % count) for i in range(count)])  31.7 us
    all_to_all x2, blocking collectives, everyone(): return lax.all_to_all(parts, axes, split_axis=0, concat_axis=0, tiled=True)  29.5 us
    all_to_all x1, waiting for transfers between devices, everyone(): return lax.all_to_all(parts, axes, split_axis=0, concat_axis=0, tiled=True)  12 us
    all_to_all x1, starting transfers between devices, everyone(): return lax.all_to_all(parts, axes, split_axis=0, concat_axis=0, tiled=True)  10.3 us
    ppermute x12, waiting for transfers between devices, shifted(): lax.ppermute(values, axes, [(i, (i + step) % count) for i in range(count)])  5.34 us
    unnamed x17, local copies, waits for them, and re-layouts  3.61 us
    all_gather x1, blocking collectives, local(): parts = jnp.sum(lax.all_gather(parts, 'tc'), axis=0)  2.43 us
  transfers between devices with their start and end apart: 13, of which 5 were waited for; matrix products, arithmetic and copies ran while one was open for 9% of the time, Pallas kernels for 1%

profile of v3, /device:TPU:8, one launch (start us, length us, event | category | flops | bytes accessed | tf_op | source)
XLA Modules:
  0.0 109.5 jit_solution(16016759395790881992)
XLA Ops:
  0.0 1.0 copy-done
  1.0 0.7 copy-done.1
  1.7 0.7 copy-done.2
  2.4 1.4 %shard_map.46 = bf16[8,144,256]{2,1,0:T(8,128)(2,1)} custom-call(s32[8]{0:T(128)S(1)} %copy-done.1, s32[8]{0:T(128)S(1)} %copy-done.2, bf16[8,128,256]{2,1,0:T(8,128)(2,1)S(1)} %bitcast.30), custom_call_target="tpu_custom_call" | custom-call | tf_op jit(solution)/shard_map/pallas_call | solution.py:61
  3.8 10.3 %all-to-all-start = ((bf16[8,144,256]{2,1,0:T(8,128)(2,1)}), bf16[8,144,256]{2,1,0:T(8,128)(2,1)S(1)}, u32[]{:S(2)}, u32[]{:S(2)}) async-start(bf16[8,144,256]{2,1,0:T(8,128)(2,1)} %shard_map.46), calls=%async_computation | async-start | bytes 1179648 | tf_op jit(solution)/shard_map/all_to_all | solution.py:289
  14.1 0.5 slice_negate_fusion
  14.6 0.9 maximum_bitcast_fusion.1
  15.6 1.6 %maximum_maximum_fusion = bf16[9,2,2,2,128,128]{5,4,3,2,1,0:T(8,128)(2,1)S(1)} fusion(bf16[9,2,2,2,64,64]{5,4,3,2,1,0:T(8,128)(2,1)S(1)} %get-tuple-element.52, bf16[9,2,2,2,64,64]{5,4,3,2,1,0:T(8,128)(2,1)S(1)} %get-tuple-element.51, bf16[9,2,2,2,64,64]{5,4,3,2,1,0:T(8,128)(2,1)S(1)} %get-tuple-element.50), kind=kLoop, calls=%fused_computation | loop fusion | flops 9437184 | bytes 4128768 | tf_op jit(solution)/shard_map/concatenate | solution.py:269
  17.1 0.2 fusion
  17.3 0.7 pad_maximum_fusion
  18.1 0.7 fusion.1
  18.8 0.7 pad_maximum_fusion.2
  19.5 0.7 fusion.3
  20.3 0.7 pad_maximum_fusion.1
  21.0 0.1 constant_dynamic-update-slice_fusion.4
  21.1 12.0 %all-to-all-done.landed = bf16[8,144,256]{2,1,0:T(8,128)(2,1)S(1)} async-done(((bf16[8,144,256]{2,1,0:T(8,128)(2,1)}), bf16[8,144,256]{2,1,0:T(8,128)(2,1)S(1)}, u32[]{:S(2)}, u32[]{:S(2)}) %all-to-all-start) | async-done | bytes 589856 | tf_op jit(solution)/shard_map/all_to_all | solution.py:289
  33.0 0.3 shard_map.47
  33.3 3.4 %collective-permute-start = (bf16[4,128,256]{2,1,0:T(8,128)(2,1)S(1)}, bf16[4,128,256]{2,1,0:T(8,128)(2,1)S(1)}, u32[]{:S(2)}, u32[]{:S(2)}) collective-permute-start(bf16[4,128,256]{2,1,0:T(8,128)(2,1)S(1)} %get-tuple-element.23), channel_id=1, source_target_pairs={{0,1},{1,2},{2,3},{3,0},{4,5},{5,6},{6,7},{7,4},{8,9},{9,10},{10,1... | collective-permute-start | bytes 786440 | tf_op jit(solution)/shard_map/ppermute | solution.py:38
  36.7 0.1 constant_dynamic-update-slice_fusion.3
  36.8 1.0 constant_dynamic-update-slice_fusion.2
  37.8 0.1 constant_dynamic-update-slice_fusion.1
  37.9 3.7 %collective-permute-start.1 = (bf16[4,128,256]{2,1,0:T(8,128)(2,1)S(1)}, bf16[4,128,256]{2,1,0:T(8,128)(2,1)S(1)}, u32[]{:S(2)}, u32[]{:S(2)}) collective-permute-start(bf16[4,128,256]{2,1,0:T(8,128)(2,1)S(1)} %get-tuple-element.24), channel_id=1, source_target_pairs={{0,3},{1,0},{2,1},{3,2},{4,7},{5,4},{6,5},{7,6},{8,11},{9,8},{10,9... | collective-permute-start | bytes 786440 | tf_op jit(solution)/shard_map/ppermute | solution.py:38
  41.5 2.5 %collective-permute-start.2 = (bf16[4,128,256]{2,1,0:T(8,128)(2,1)S(1)}, bf16[4,128,256]{2,1,0:T(8,128)(2,1)S(1)}, u32[]{:S(2)}, u32[]{:S(2)}) collective-permute-start(bf16[4,128,256]{2,1,0:T(8,128)(2,1)S(1)} %get-tuple-element.25), channel_id=1, source_target_pairs={{0,4},{4,8},{8,12},{12,16},{16,20},{20,24},{24,28},{28,0},{1,5},{5... | collective-permute-start | bytes 786440 | tf_op jit(solution)/shard_map/ppermute | solution.py:38
  44.0 4.6 %collective-permute-start.3 = (bf16[4,128,256]{2,1,0:T(8,128)(2,1)S(1)}, bf16[4,128,256]{2,1,0:T(8,128)(2,1)S(1)}, u32[]{:S(2)}, u32[]{:S(2)}) collective-permute-start(bf16[4,128,256]{2,1,0:T(8,128)(2,1)S(1)} %get-tuple-element.26), channel_id=1, source_target_pairs={{0,28},{4,0},{8,4},{12,8},{16,12},{20,16},{24,20},{28,24},{1,29},{... | collective-permute-start | bytes 786440 | tf_op jit(solution)/shard_map/ppermute | solution.py:38
  48.6 0.0 collective-permute-start.4
  48.6 1.7 %collective-permute-start.5 = (bf16[4,128,256]{2,1,0:T(8,128)(2,1)S(1)}, bf16[4,128,256]{2,1,0:T(8,128)(2,1)S(1)}, u32[]{:S(2)}, u32[]{:S(2)}) collective-permute-start(bf16[4,128,256]{2,1,0:T(8,128)(2,1)S(1)} %get-tuple-element.28), channel_id=1, source_target_pairs={{0,480},{32,0},{64,32},{96,64},{128,96},{160,128},{192,160},{224,1... | collective-permute-start | bytes 786440 | tf_op jit(solution)/shard_map/ppermute | solution.py:38
  50.4 1.0 constant_dynamic-update-slice_fusion.inside
  51.4 1.2 %maximum_maximum_fusion.1 = bf16[2,2,2,128,384]{4,3,2,1,0:T(8,128)(2,1)S(1)} fusion(bf16[2,2,1,128,128]{4,3,2,1,0:T(8,128)(2,1)} %get-tuple-element.54, bf16[2,2,1,128,128]{4,3,2,1,0:T(8,128)(2,1)} %get-tuple-element.61, bf16[2,1,2,128,128]{4,3,2,1,0:T(8,128)(2,1)} %get-tuple-element.58, bf16[2,1,2,128,128]{4,3,2,1,0:T(8,128)(2,1)} %get-tuple-element.63, ...), kind=kLoop, calls=%fused_computation.1 | loop fusion | flops 4718592 | bytes 1572864 | tf_op jit(solution)/shard_map/concatenate | solution.py:281
  52.6 0.6 shard_map.48.partial
  53.2 0.0 collective-permute-done.1.r1
  53.2 0.3 collective-permute-done.3.r3
  53.5 0.9 collective-permute-done.4.r4
  54.4 0.0 collective-permute-done.5.r5
  54.4 0.5 shard_map.49
  54.9 2.2 %collective-permute-start.6 = (bf16[4,128,256]{2,1,0:T(8,128)(2,1)S(1)}, bf16[4,128,256]{2,1,0:T(8,128)(2,1)S(1)}, u32[]{:S(2)}, u32[]{:S(2)}) collective-permute-start(bf16[4,128,256]{2,1,0:T(8,128)(2,1)S(1)} %get-tuple-element.33), channel_id=1, source_target_pairs={{0,1},{1,2},{2,3},{3,0},{4,5},{5,6},{6,7},{7,4},{8,9},{9,10},{10,1... | collective-permute-start | bytes 786440 | tf_op jit(solution)/shard_map/ppermute | solution.py:38
  57.1 4.9 %collective-permute-start.7 = (bf16[4,128,256]{2,1,0:T(8,128)(2,1)S(1)}, bf16[4,128,256]{2,1,0:T(8,128)(2,1)S(1)}, u32[]{:S(2)}, u32[]{:S(2)}) collective-permute-start(bf16[4,128,256]{2,1,0:T(8,128)(2,1)S(1)} %get-tuple-element.34), channel_id=1, source_target_pairs={{0,3},{1,0},{2,1},{3,2},{4,7},{5,4},{6,5},{7,6},{8,11},{9,8},{10,9... | collective-permute-start | bytes 786440 | tf_op jit(solution)/shard_map/ppermute | solution.py:38
  62.0 1.9 %collective-permute-start.8 = (bf16[4,128,256]{2,1,0:T(8,128)(2,1)S(1)}, bf16[4,128,256]{2,1,0:T(8,128)(2,1)S(1)}, u32[]{:S(2)}, u32[]{:S(2)}) collective-permute-start(bf16[4,128,256]{2,1,0:T(8,128)(2,1)S(1)} %get-tuple-element.35), channel_id=1, source_target_pairs={{0,4},{4,8},{8,12},{12,16},{16,20},{20,24},{24,28},{28,0},{1,5},{5... | collective-permute-start | bytes 786440 | tf_op jit(solution)/shard_map/ppermute | solution.py:38
  63.9 5.1 %collective-permute-start.9 = (bf16[4,128,256]{2,1,0:T(8,128)(2,1)S(1)}, bf16[4,128,256]{2,1,0:T(8,128)(2,1)S(1)}, u32[]{:S(2)}, u32[]{:S(2)}) collective-permute-start(bf16[4,128,256]{2,1,0:T(8,128)(2,1)S(1)} %get-tuple-element.36), channel_id=1, source_target_pairs={{0,28},{4,0},{8,4},{12,8},{16,12},{20,16},{24,20},{28,24},{1,29},{... | collective-permute-start | bytes 786440 | tf_op jit(solution)/shard_map/ppermute | solution.py:38
  69.1 0.6 collective-permute-start.10
  69.7 1.2 %collective-permute-start.11 = (bf16[4,128,256]{2,1,0:T(8,128)(2,1)S(1)}, bf16[4,128,256]{2,1,0:T(8,128)(2,1)S(1)}, u32[]{:S(2)}, u32[]{:S(2)}) collective-permute-start(bf16[4,128,256]{2,1,0:T(8,128)(2,1)S(1)} %get-tuple-element.38), channel_id=1, source_target_pairs={{0,480},{32,0},{64,32},{96,64},{128,96},{160,128},{192,160},{224,1... | collective-permute-start | bytes 786440 | tf_op jit(solution)/shard_map/ppermute | solution.py:38
  70.8 0.7 shard_map.50
  71.5 2.6 %collective-permute-done.8.r2 = bf16[4,128,256]{2,1,0:T(8,128)(2,1)S(1)} collective-permute-done((bf16[4,128,256]{2,1,0:T(8,128)(2,1)S(1)}, bf16[4,128,256]{2,1,0:T(8,128)(2,1)S(1)}, u32[]{:S(2)}, u32[]{:S(2)}) %collective-permute-start.8) | collective-permute-done | bytes 262176 | tf_op jit(solution)/shard_map/ppermute | solution.py:38
  74.1 1.5 %collective-permute-done.9.r3 = bf16[4,128,256]{2,1,0:T(8,128)(2,1)S(1)} collective-permute-done((bf16[4,128,256]{2,1,0:T(8,128)(2,1)S(1)}, bf16[4,128,256]{2,1,0:T(8,128)(2,1)S(1)}, u32[]{:S(2)}, u32[]{:S(2)}) %collective-permute-start.9) | collective-permute-done | bytes 262176 | tf_op jit(solution)/shard_map/ppermute | solution.py:38
  75.6 0.8 shard_map.51
  76.5 2.4 %all-gather = f32[16,256]{1,0:T(8,128)S(1)} all-gather(f32[8,256]{1,0:T(8,128)S(1)} %shard_map.51), channel_id=2, replica_groups=mesh['ya'=4,'yb'=2,'tc'=2,'gz'=8,'gy'=4] {'tc'}, dimensions={0}, use_global_device_ids=true | all-gather | bytes 24576 | tf_op jit(solution)/shard_map/all_gather | solution.py:303
  78.9 13.7 %all_to_all.15 = f32[16,8,256]{2,1,0:T(8,128)S(1)} all-to-all(f32[16,8,256]{2,1,0:T(8,128)S(1)} %broadcast_in_dim.4), channel_id=1, replica_groups=mesh['ya'=4,'yb'=2,'tc'=2,'gz'=8,'gy'=4] {'yb','gz'}, dimensions={0} | all-to-all | bytes 262144 | tf_op jit(solution)/shard_map/all_to_all | solution.py:289
  92.6 15.8 %all_to_all.16.landed = f32[16,8,256]{2,1,0:T(8,128)S(1)} all-to-all(f32[16,8,256]{2,1,0:T(8,128)S(1)} %broadcast_in_dim.5), channel_id=1, replica_groups=mesh['ya'=4,'yb'=2,'tc'=2,'gz'=8,'gy'=4] {'ya','gy'}, dimensions={0} | all-to-all | bytes 262144 | tf_op jit(solution)/shard_map/all_to_all | solution.py:289
  108.4 1.1 shard_map.52
  (20 shorter events, 0.1 us)
Async XLA Ops:
  0.0 1.0 copy-start
  1.0 0.7 copy-start.1
  1.7 0.7 copy-start.2
  2.4 11.8 %copy-start.3 = (bf16[9,1,2,2,2,64,128]{6,5,4,3,2,1,0:T(8,128)(2,1)S(1)}, bf16[9,1,2,2,2,64,128]{6,5,4,3,2,1,0:T(8,128)(2,1)}, u32[]{:S(2)}) copy-start(bf16[9,1,2,2,2,64,128]{6,5,4,3,2,1,0:T(8,128)(2,1)} %param.5) | copy-start | bytes 3538948
  3.8 29.2 %all-to-all-start = ((bf16[8,144,256]{2,1,0:T(8,128)(2,1)}), bf16[8,144,256]{2,1,0:T(8,128)(2,1)S(1)}, u32[]{:S(2)}, u32[]{:S(2)}) async-start(bf16[8,144,256]{2,1,0:T(8,128)(2,1)} %shard_map.46), calls=%async_computation | async-start | bytes 1179648 | tf_op jit(solution)/shard_map/all_to_all | solution.py:289
  21.0 30.4 %copy-start.5 = (bf16[1,2,2,128,128]{4,3,2,1,0:T(8,128)(2,1)S(1)}, bf16[1,2,2,128,128]{4,3,2,1,0:T(8,128)(2,1)}, u32[]{:S(2)}) copy-start(bf16[1,2,2,128,128]{4,3,2,1,0:T(8,128)(2,1)} %get-tuple-element.41) | copy-start | bytes 393220
  33.0 4.8 %copy-start.4 = (bf16[2,2,2,128,128]{4,3,2,1,0:T(8,128)(2,1)S(1)}, bf16[2,2,2,128,128]{4,3,2,1,0:T(8,128)(2,1)}, u32[]{:S(2)}) copy-start(bf16[2,2,2,128,128]{4,3,2,1,0:T(8,128)(2,1)} %pad_maximum_fusion.1) | copy-start | bytes 786436
  33.3 15.3 %collective-permute-start = (bf16[4,128,256]{2,1,0:T(8,128)(2,1)S(1)}, bf16[4,128,256]{2,1,0:T(8,128)(2,1)S(1)}, u32[]{:S(2)}, u32[]{:S(2)}) collective-permute-start(bf16[4,128,256]{2,1,0:T(8,128)(2,1)S(1)} %get-tuple-element.23), channel_id=1, source_target_pairs={{0,1},{1,2},{2,3},{3,0},{4,5},{5,6},{6,7},{7,4},{8,9},{9,10},{10,1... | collective-permute-start | bytes 786440 | tf_op jit(solution)/shard_map/ppermute | solution.py:38
  37.9 15.3 %collective-permute-start.1 = (bf16[4,128,256]{2,1,0:T(8,128)(2,1)S(1)}, bf16[4,128,256]{2,1,0:T(8,128)(2,1)S(1)}, u32[]{:S(2)}, u32[]{:S(2)}) collective-permute-start(bf16[4,128,256]{2,1,0:T(8,128)(2,1)S(1)} %get-tuple-element.24), channel_id=1, source_target_pairs={{0,3},{1,0},{2,1},{3,2},{4,7},{5,4},{6,5},{7,6},{8,11},{9,8},{10,9... | collective-permute-start | bytes 786440 | tf_op jit(solution)/shard_map/ppermute | solution.py:38
  41.5 11.7 %collective-permute-start.2 = (bf16[4,128,256]{2,1,0:T(8,128)(2,1)S(1)}, bf16[4,128,256]{2,1,0:T(8,128)(2,1)S(1)}, u32[]{:S(2)}, u32[]{:S(2)}) collective-permute-start(bf16[4,128,256]{2,1,0:T(8,128)(2,1)S(1)} %get-tuple-element.25), channel_id=1, source_target_pairs={{0,4},{4,8},{8,12},{12,16},{16,20},{20,24},{24,28},{28,0},{1,5},{5... | collective-permute-start | bytes 786440 | tf_op jit(solution)/shard_map/ppermute | solution.py:38
  44.0 9.5 %collective-permute-start.3 = (bf16[4,128,256]{2,1,0:T(8,128)(2,1)S(1)}, bf16[4,128,256]{2,1,0:T(8,128)(2,1)S(1)}, u32[]{:S(2)}, u32[]{:S(2)}) collective-permute-start(bf16[4,128,256]{2,1,0:T(8,128)(2,1)S(1)} %get-tuple-element.26), channel_id=1, source_target_pairs={{0,28},{4,0},{8,4},{12,8},{16,12},{20,16},{24,20},{28,24},{1,29},{... | collective-permute-start | bytes 786440 | tf_op jit(solution)/shard_map/ppermute | solution.py:38
  48.6 5.8 %collective-permute-start.4 = (bf16[4,128,256]{2,1,0:T(8,128)(2,1)S(1)}, bf16[4,128,256]{2,1,0:T(8,128)(2,1)S(1)}, u32[]{:S(2)}, u32[]{:S(2)}) collective-permute-start(bf16[4,128,256]{2,1,0:T(8,128)(2,1)S(1)} %get-tuple-element.27), channel_id=1, source_target_pairs={{0,32},{32,64},{64,96},{96,128},{128,160},{160,192},{192,224},{224... | collective-permute-start | bytes 786440 | tf_op jit(solution)/shard_map/ppermute | solution.py:38
  48.6 5.8 %collective-permute-start.5 = (bf16[4,128,256]{2,1,0:T(8,128)(2,1)S(1)}, bf16[4,128,256]{2,1,0:T(8,128)(2,1)S(1)}, u32[]{:S(2)}, u32[]{:S(2)}) collective-permute-start(bf16[4,128,256]{2,1,0:T(8,128)(2,1)S(1)} %get-tuple-element.28), channel_id=1, source_target_pairs={{0,480},{32,0},{64,32},{96,64},{128,96},{160,128},{192,160},{224,1... | collective-permute-start | bytes 786440 | tf_op jit(solution)/shard_map/ppermute | solution.py:38
  54.9 14.7 %collective-permute-start.6 = (bf16[4,128,256]{2,1,0:T(8,128)(2,1)S(1)}, bf16[4,128,256]{2,1,0:T(8,128)(2,1)S(1)}, u32[]{:S(2)}, u32[]{:S(2)}) collective-permute-start(bf16[4,128,256]{2,1,0:T(8,128)(2,1)S(1)} %get-tuple-element.33), channel_id=1, source_target_pairs={{0,1},{1,2},{2,3},{3,0},{4,5},{5,6},{6,7},{7,4},{8,9},{9,10},{10,1... | collective-permute-start | bytes 786440 | tf_op jit(solution)/shard_map/ppermute | solution.py:38
  57.1 14.4 %collective-permute-start.7 = (bf16[4,128,256]{2,1,0:T(8,128)(2,1)S(1)}, bf16[4,128,256]{2,1,0:T(8,128)(2,1)S(1)}, u32[]{:S(2)}, u32[]{:S(2)}) collective-permute-start(bf16[4,128,256]{2,1,0:T(8,128)(2,1)S(1)} %get-tuple-element.34), channel_id=1, source_target_pairs={{0,3},{1,0},{2,1},{3,2},{4,7},{5,4},{6,5},{7,6},{8,11},{9,8},{10,9... | collective-permute-start | bytes 786440 | tf_op jit(solution)/shard_map/ppermute | solution.py:38
  62.0 12.1 %collective-permute-start.8 = (bf16[4,128,256]{2,1,0:T(8,128)(2,1)S(1)}, bf16[4,128,256]{2,1,0:T(8,128)(2,1)S(1)}, u32[]{:S(2)}, u32[]{:S(2)}) collective-permute-start(bf16[4,128,256]{2,1,0:T(8,128)(2,1)S(1)} %get-tuple-element.35), channel_id=1, source_target_pairs={{0,4},{4,8},{8,12},{12,16},{16,20},{20,24},{24,28},{28,0},{1,5},{5... | collective-permute-start | bytes 786440 | tf_op jit(solution)/shard_map/ppermute | solution.py:38
  63.9 11.7 %collective-permute-start.9 = (bf16[4,128,256]{2,1,0:T(8,128)(2,1)S(1)}, bf16[4,128,256]{2,1,0:T(8,128)(2,1)S(1)}, u32[]{:S(2)}, u32[]{:S(2)}) collective-permute-start(bf16[4,128,256]{2,1,0:T(8,128)(2,1)S(1)} %get-tuple-element.36), channel_id=1, source_target_pairs={{0,28},{4,0},{8,4},{12,8},{16,12},{20,16},{24,20},{28,24},{1,29},{... | collective-permute-start | bytes 786440 | tf_op jit(solution)/shard_map/ppermute | solution.py:38
  69.1 6.6 %collective-permute-start.10 = (bf16[4,128,256]{2,1,0:T(8,128)(2,1)S(1)}, bf16[4,128,256]{2,1,0:T(8,128)(2,1)S(1)}, u32[]{:S(2)}, u32[]{:S(2)}) collective-permute-start(bf16[4,128,256]{2,1,0:T(8,128)(2,1)S(1)} %get-tuple-element.37), channel_id=1, source_target_pairs={{0,32},{32,64},{64,96},{96,128},{128,160},{160,192},{192,224},{224... | collective-permute-start | bytes 786440 | tf_op jit(solution)/shard_map/ppermute | solution.py:38
  69.7 6.0 %collective-permute-start.11 = (bf16[4,128,256]{2,1,0:T(8,128)(2,1)S(1)}, bf16[4,128,256]{2,1,0:T(8,128)(2,1)S(1)}, u32[]{:S(2)}, u32[]{:S(2)}) collective-permute-start(bf16[4,128,256]{2,1,0:T(8,128)(2,1)S(1)} %get-tuple-element.38), channel_id=1, source_target_pairs={{0,480},{32,0},{64,32},{96,64},{128,96},{160,128},{192,160},{224,1... | collective-permute-start | bytes 786440 | tf_op jit(solution)/shard_map/ppermute | solution.py:38

commit v4 on v3

--- a/solution.py
+++ b/solution.py
@@ -13,11 +13,12 @@
 LOW = tuple(tuple(s for s in range(SITES) if not s & bit) for bit in BITS)
 HIGH = tuple(tuple(s for s in range(SITES) if s & bit) for bit in BITS)
 VMEM_LIMIT = 24 * 1024 * 1024
+PACK_LIMIT = 60 * 1024 * 1024
 WHOLE = pl.BlockSpec(memory_space=pltpu.VMEM)
 IN_HBM = pl.BlockSpec(memory_space=pltpu.HBM)
 
 
-def call(body, outs, ins, cost=None, scratch=(), out_spec=WHOLE):
+def call(body, outs, ins, cost=None, scratch=(), out_spec=WHOLE, limit=VMEM_LIMIT):
     return pl.pallas_call(
         body,
         out_shape=outs,
@@ -25,7 +26,7 @@
         out_specs=[out_spec] * len(outs),
         scratch_shapes=scratch,
         cost_estimate=cost,
-        compiler_params=pltpu.CompilerParams(vmem_limit_bytes=VMEM_LIMIT),
+        compiler_params=pltpu.CompilerParams(vmem_limit_bytes=limit),
     )
 
 
@@ -68,6 +69,7 @@
             pltpu.VMEM(rows.shape, rows.dtype),
             pltpu.SemaphoreType.DMA((3,)),
         ],
+        limit=PACK_LIMIT,
     )(owners, slots, rows)[0]
 
 
@@ -260,25 +262,31 @@
     )(landed, image, source)[0]
 
 
-def block_double(blocks):
-    columns = blocks.shape[-1] // 2
-    real_blk = blocks[..., :columns]
-    imag_blk = blocks[..., columns:]
-    upper = jnp.concatenate([real_blk, -imag_blk], axis=-1)
-    lower = jnp.concatenate([imag_blk, real_blk], axis=-1)
-    return jnp.concatenate([upper, lower], axis=-2)
-
-
-def split_couplings(doubled):
-    inside = [doubled[0], doubled[1], doubled[2]]
-    outside = []
-    for dim in range(3):
-        ahead, behind = doubled[3 + 2 * dim], doubled[4 + 2 * dim]
-        pick = lambda a, s: lax.slice_in_dim(a, s, s + 1, axis=dim)
-        inside.append(jnp.concatenate([pick(ahead, 0), pick(behind, 1)], axis=dim))
-        outside.append(jnp.concatenate([pick(behind, 0), pick(ahead, 1)], axis=dim))
-    flat = lambda a: a.reshape((SITES,) + a.shape[-2:])
-    return flat(jnp.concatenate(inside, axis=-1)), flat(jnp.concatenate(outside, axis=-1))
+def split_body(couplings, inside, outside):
+    half, width = couplings.shape[2], couplings.shape[3]
+    real_lanes = lax.broadcasted_iota(jnp.int32, (half, width), 1) < width // 2
+
+    def put(target, s, j, k):
+        block = couplings[k, s].astype(jnp.float32)
+        upper = jnp.where(real_lanes, block, -block)
+        lower = pltpu.roll(block, width // 2, 1)
+        target[s, 0:half, j * width : (j + 1) * width] = upper.astype(target.dtype)
+        target[s, half:, j * width : (j + 1) * width] = lower.astype(target.dtype)
+
+    for s in range(SITES):
+        for k in range(3):
+            put(inside, s, k, k)
+        for axis, bit in enumerate(BITS):
+            ahead, behind = 3 + 2 * axis, 4 + 2 * axis
+            put(inside, s, 3 + axis, behind if s & bit else ahead)
+            put(outside, s, axis, ahead if s & bit else behind)
+
+
+def split_couplings(couplings):
+    blocks = couplings.reshape((couplings.shape[0], SITES) + couplings.shape[-2:])
+    width = blocks.shape[-1]
+    outs = [shape_of((SITES, width, n * width), blocks.dtype) for n in (6, 3)]
+    return call(split_body, outs, [WHOLE])(blocks)
 
 
 def copies_of(parts, axes):
@@ -293,7 +301,7 @@
     count, width = restricted.shape[0], restricted.shape[-1]
     rows = restricted.reshape(count, -1, width)
     landed = everyone(pack(rows, owners, coarse_site), "gz")
-    inside, outside = split_couplings(block_double(couplings[:, 0]))
+    landed, inside, outside = lax.optimization_barrier((landed, *split_couplings(couplings)))
     source, faces = place(landed)
     received = exchange(faces)
     image, field, faces = first_image(outside, near(inside, source), received)

time: 110 us -> 107 us (0.973)
  waiting for transfers between devices: 17.3 us -> 23.8 us
  other arithmetic: 6.38 us -> 0.02 us
  local copies, waits for them, and re-layouts: 6.29 us -> 2.19 us
    concatenate x5 -> x0, other arithmetic: 4.94 us -> none  [the longest x3 2.18 us: split_couplings(): inside.append(jnp.concatenate([pick(ahead, 0), pick(behind, 1)], axis=dim))]
    all_to_all x1, waiting for transfers between devices: 12 us -> 16.2 us  [everyone(): return lax.all_to_all(parts, axes, split_axis=0, concat_axis=0, tiled=True)]
    ppermute x12, waiting for transfers between devices: 5.34 us -> 7.59 us  [shifted(): lax.ppermute(values, axes, [(i, (i + step) % count) for i in range(count)])]
    slice x3 -> x0, local copies, waits for them, and re-layouts: 1.64 us -> none  [the longest x2 1.48 us: split_couplings(): pick = lambda a, s: lax.slice_in_dim(a, s, s + 1, axis=dim)]
    unnamed x17 -> x6, local copies, waits for them, and re-layouts: 3.61 us -> 2.17 us
  transfers between devices with their start and end apart: 13 -> 13, of which waited for: 5 -> 6; matrix products, arithmetic and copies ran while one was open for 9% -> 0% of each run, Pallas kernels for 1% -> 2%
where the time goes in v4:
time: 107 us; the launch traced here: 106 us
  starting transfers between devices  42 us (39%)
  blocking collectives  31.9 us (30%)
  waiting for transfers between devices  23.8 us (22%)
  Pallas kernels  6.31 us (6%)
  local copies, waits for them, and re-layouts  2.19 us (2%)
    ppermute x12, starting transfers between devices, shifted(): lax.ppermute(values, axes, [(i, (i + step) % count) for i in range(count)])  31.7 us
    all_to_all x2, blocking collectives, everyone(): return lax.all_to_all(parts, axes, split_axis=0, concat_axis=0, tiled=True)  29.5 us
    all_to_all x1, waiting for transfers between devices, everyone(): return lax.all_to_all(parts, axes, split_axis=0, concat_axis=0, tiled=True)  16.2 us
    all_to_all x1, starting transfers between devices, everyone(): return lax.all_to_all(parts, axes, split_axis=0, concat_axis=0, tiled=True)  10.3 us
    ppermute x12, waiting for transfers between devices, shifted(): lax.ppermute(values, axes, [(i, (i + step) % count) for i in range(count)])  7.59 us
    all_gather x1, blocking collectives, local(): parts = jnp.sum(lax.all_gather(parts, 'tc'), axis=0)  2.43 us
    unnamed x6, local copies, waits for them, and re-layouts  2.17 us
  transfers between devices with their start and end apart: 13, of which 6 were waited for; matrix products, arithmetic and copies ran while one was open for 0% of the time, Pallas kernels for 2%

profile of v4, /device:TPU:8, one launch (start us, length us, event | category | flops | bytes accessed | tf_op | source)
XLA Modules:
  0.0 106.4 jit_solution(15029788279326425591)
XLA Ops:
  0.0 1.9 %shard_map.46 = bf16[8,144,256]{2,1,0:T(8,128)(2,1)} custom-call(s32[8]{0:T(128)} %owners.1, s32[8]{0:T(128)} %slots.1, bf16[8,128,256]{2,1,0:T(8,128)(2,1)} %bitcast.6), custom_call_target="tpu_custom_call" | custom-call | tf_op jit(solution)/shard_map/pallas_call | solution.py:62
  1.9 10.3 %all-to-all-start = ((bf16[8,144,256]{2,1,0:T(8,128)(2,1)}), bf16[8,144,256]{2,1,0:T(8,128)(2,1)S(1)}, u32[]{:S(2)}, u32[]{:S(2)}) async-start(bf16[8,144,256]{2,1,0:T(8,128)(2,1)} %shard_map.46), calls=%async_computation | async-start | bytes 1179648 | tf_op jit(solution)/shard_map/all_to_all | solution.py:297
  12.3 0.0 copy-start.2
  12.3 1.3 %copy-done.2 = bf16[9,1,2,2,2,64,128]{6,5,4,3,2,1,0:T(8,128)(2,1)S(1)} copy-done((bf16[9,1,2,2,2,64,128]{6,5,4,3,2,1,0:T(8,128)(2,1)S(1)}, bf16[9,1,2,2,2,64,128]{6,5,4,3,2,1,0:T(8,128)(2,1)}, u32[]{:S(2)}) %copy-start.2) | copy-done | bytes 1179672
  13.5 0.5 shard_map.47
  14.1 0.0 copy-start
  14.1 0.9 copy-done
  15.0 16.2 %all-to-all-done.landed = bf16[8,144,256]{2,1,0:T(8,128)(2,1)S(1)} async-done(((bf16[8,144,256]{2,1,0:T(8,128)(2,1)}), bf16[8,144,256]{2,1,0:T(8,128)(2,1)S(1)}, u32[]{:S(2)}, u32[]{:S(2)}) %all-to-all-start) | async-done | bytes 589856 | tf_op jit(solution)/shard_map/all_to_all | solution.py:297
  31.2 0.3 shard_map.48
  31.4 3.4 %collective-permute-start = (bf16[4,128,256]{2,1,0:T(8,128)(2,1)S(1)}, bf16[4,128,256]{2,1,0:T(8,128)(2,1)S(1)}, u32[]{:S(2)}, u32[]{:S(2)}) collective-permute-start(bf16[4,128,256]{2,1,0:T(8,128)(2,1)S(1)} %get-tuple-element.33), channel_id=1, source_target_pairs={{0,1},{1,2},{2,3},{3,0},{4,5},{5,6},{6,7},{7,4},{8,9},{9,10},{10,1... | collective-permute-start | bytes 786440 | tf_op jit(solution)/shard_map/ppermute | solution.py:39
  34.8 3.7 %collective-permute-start.1 = (bf16[4,128,256]{2,1,0:T(8,128)(2,1)S(1)}, bf16[4,128,256]{2,1,0:T(8,128)(2,1)S(1)}, u32[]{:S(2)}, u32[]{:S(2)}) collective-permute-start(bf16[4,128,256]{2,1,0:T(8,128)(2,1)S(1)} %get-tuple-element.34), channel_id=1, source_target_pairs={{0,3},{1,0},{2,1},{3,2},{4,7},{5,4},{6,5},{7,6},{8,11},{9,8},{10,9... | collective-permute-start | bytes 786440 | tf_op jit(solution)/shard_map/ppermute | solution.py:39
  38.5 2.5 %collective-permute-start.2 = (bf16[4,128,256]{2,1,0:T(8,128)(2,1)S(1)}, bf16[4,128,256]{2,1,0:T(8,128)(2,1)S(1)}, u32[]{:S(2)}, u32[]{:S(2)}) collective-permute-start(bf16[4,128,256]{2,1,0:T(8,128)(2,1)S(1)} %get-tuple-element.35), channel_id=1, source_target_pairs={{0,4},{4,8},{8,12},{12,16},{16,20},{20,24},{24,28},{28,0},{1,5},{5... | collective-permute-start | bytes 786440 | tf_op jit(solution)/shard_map/ppermute | solution.py:39
  41.0 4.6 %collective-permute-start.3 = (bf16[4,128,256]{2,1,0:T(8,128)(2,1)S(1)}, bf16[4,128,256]{2,1,0:T(8,128)(2,1)S(1)}, u32[]{:S(2)}, u32[]{:S(2)}) collective-permute-start(bf16[4,128,256]{2,1,0:T(8,128)(2,1)S(1)} %get-tuple-element.36), channel_id=1, source_target_pairs={{0,28},{4,0},{8,4},{12,8},{16,12},{20,16},{24,20},{28,24},{1,29},{... | collective-permute-start | bytes 786440 | tf_op jit(solution)/shard_map/ppermute | solution.py:39
  45.6 0.0 collective-permute-start.4
  45.6 0.0 collective-permute-done.r0
  45.6 1.7 %collective-permute-start.5 = (bf16[4,128,256]{2,1,0:T(8,128)(2,1)S(1)}, bf16[4,128,256]{2,1,0:T(8,128)(2,1)S(1)}, u32[]{:S(2)}, u32[]{:S(2)}) collective-permute-start(bf16[4,128,256]{2,1,0:T(8,128)(2,1)S(1)} %get-tuple-element.38), channel_id=1, source_target_pairs={{0,480},{32,0},{64,32},{96,64},{128,96},{160,128},{192,160},{224,1... | collective-permute-start | bytes 786440 | tf_op jit(solution)/shard_map/ppermute | solution.py:39
  47.3 0.0 copy-start.1
  47.3 0.6 shard_map.49.partial
  47.9 0.0 collective-permute-done.1.r1
  47.9 1.3 %collective-permute-done.2.r2 = bf16[4,128,256]{2,1,0:T(8,128)(2,1)S(1)} collective-permute-done((bf16[4,128,256]{2,1,0:T(8,128)(2,1)S(1)}, bf16[4,128,256]{2,1,0:T(8,128)(2,1)S(1)}, u32[]{:S(2)}, u32[]{:S(2)}) %collective-permute-start.2) | collective-permute-done | bytes 262176 | tf_op jit(solution)/shard_map/ppermute | solution.py:39
  49.3 1.2 %collective-permute-done.3.r3 = bf16[4,128,256]{2,1,0:T(8,128)(2,1)S(1)} collective-permute-done((bf16[4,128,256]{2,1,0:T(8,128)(2,1)S(1)}, bf16[4,128,256]{2,1,0:T(8,128)(2,1)S(1)}, u32[]{:S(2)}, u32[]{:S(2)}) %collective-permute-start.3) | collective-permute-done | bytes 262176 | tf_op jit(solution)/shard_map/ppermute | solution.py:39
  50.5 0.9 collective-permute-done.4.r4
  51.4 0.0 collective-permute-done.5.r5
  51.4 0.0 copy-done.1
  51.4 0.5 shard_map.50
  51.9 2.2 %collective-permute-start.6 = (bf16[4,128,256]{2,1,0:T(8,128)(2,1)S(1)}, bf16[4,128,256]{2,1,0:T(8,128)(2,1)S(1)}, u32[]{:S(2)}, u32[]{:S(2)}) collective-permute-start(bf16[4,128,256]{2,1,0:T(8,128)(2,1)S(1)} %get-tuple-element.43), channel_id=1, source_target_pairs={{0,1},{1,2},{2,3},{3,0},{4,5},{5,6},{6,7},{7,4},{8,9},{9,10},{10,1... | collective-permute-start | bytes 786440 | tf_op jit(solution)/shard_map/ppermute | solution.py:39
  54.1 4.9 %collective-permute-start.7 = (bf16[4,128,256]{2,1,0:T(8,128)(2,1)S(1)}, bf16[4,128,256]{2,1,0:T(8,128)(2,1)S(1)}, u32[]{:S(2)}, u32[]{:S(2)}) collective-permute-start(bf16[4,128,256]{2,1,0:T(8,128)(2,1)S(1)} %get-tuple-element.44), channel_id=1, source_target_pairs={{0,3},{1,0},{2,1},{3,2},{4,7},{5,4},{6,5},{7,6},{8,11},{9,8},{10,9... | collective-permute-start | bytes 786440 | tf_op jit(solution)/shard_map/ppermute | solution.py:39
  59.0 1.9 %collective-permute-start.8 = (bf16[4,128,256]{2,1,0:T(8,128)(2,1)S(1)}, bf16[4,128,256]{2,1,0:T(8,128)(2,1)S(1)}, u32[]{:S(2)}, u32[]{:S(2)}) collective-permute-start(bf16[4,128,256]{2,1,0:T(8,128)(2,1)S(1)} %get-tuple-element.45), channel_id=1, source_target_pairs={{0,4},{4,8},{8,12},{12,16},{16,20},{20,24},{24,28},{28,0},{1,5},{5... | collective-permute-start | bytes 786440 | tf_op jit(solution)/shard_map/ppermute | solution.py:39
  60.9 5.1 %collective-permute-start.9 = (bf16[4,128,256]{2,1,0:T(8,128)(2,1)S(1)}, bf16[4,128,256]{2,1,0:T(8,128)(2,1)S(1)}, u32[]{:S(2)}, u32[]{:S(2)}) collective-permute-start(bf16[4,128,256]{2,1,0:T(8,128)(2,1)S(1)} %get-tuple-element.46), channel_id=1, source_target_pairs={{0,28},{4,0},{8,4},{12,8},{16,12},{20,16},{24,20},{28,24},{1,29},{... | collective-permute-start | bytes 786440 | tf_op jit(solution)/shard_map/ppermute | solution.py:39
  66.0 0.6 collective-permute-start.10
  66.6 0.0 collective-permute-done.6.r0
  66.6 1.2 %collective-permute-start.11 = (bf16[4,128,256]{2,1,0:T(8,128)(2,1)S(1)}, bf16[4,128,256]{2,1,0:T(8,128)(2,1)S(1)}, u32[]{:S(2)}, u32[]{:S(2)}) collective-permute-start(bf16[4,128,256]{2,1,0:T(8,128)(2,1)S(1)} %get-tuple-element.48), channel_id=1, source_target_pairs={{0,480},{32,0},{64,32},{96,64},{128,96},{160,128},{192,160},{224,1... | collective-permute-start | bytes 786440 | tf_op jit(solution)/shard_map/ppermute | solution.py:39
  67.8 0.7 shard_map.51
  68.5 0.0 collective-permute-done.7.r1
  68.5 2.6 %collective-permute-done.8.r2 = bf16[4,128,256]{2,1,0:T(8,128)(2,1)S(1)} collective-permute-done((bf16[4,128,256]{2,1,0:T(8,128)(2,1)S(1)}, bf16[4,128,256]{2,1,0:T(8,128)(2,1)S(1)}, u32[]{:S(2)}, u32[]{:S(2)}) %collective-permute-start.8) | collective-permute-done | bytes 262176 | tf_op jit(solution)/shard_map/ppermute | solution.py:39
  71.1 1.5 %collective-permute-done.9.r3 = bf16[4,128,256]{2,1,0:T(8,128)(2,1)S(1)} collective-permute-done((bf16[4,128,256]{2,1,0:T(8,128)(2,1)S(1)}, bf16[4,128,256]{2,1,0:T(8,128)(2,1)S(1)}, u32[]{:S(2)}, u32[]{:S(2)}) %collective-permute-start.9) | collective-permute-done | bytes 262176 | tf_op jit(solution)/shard_map/ppermute | solution.py:39
  72.6 0.0 collective-permute-done.10.r4
  72.6 0.0 collective-permute-done.11.r5
  72.6 0.8 shard_map.52
  73.4 2.4 %all-gather = f32[16,256]{1,0:T(8,128)S(1)} all-gather(f32[8,256]{1,0:T(8,128)S(1)} %shard_map.52), channel_id=2, replica_groups=mesh['ya'=4,'yb'=2,'tc'=2,'gz'=8,'gy'=4] {'tc'}, dimensions={0}, use_global_device_ids=true | all-gather | bytes 24576 | tf_op jit(solution)/shard_map/all_gather | solution.py:311
  75.8 13.7 %all_to_all.15 = f32[16,8,256]{2,1,0:T(8,128)S(1)} all-to-all(f32[16,8,256]{2,1,0:T(8,128)S(1)} %broadcast_in_dim.4), channel_id=1, replica_groups=mesh['ya'=4,'yb'=2,'tc'=2,'gz'=8,'gy'=4] {'yb','gz'}, dimensions={0} | all-to-all | bytes 262144 | tf_op jit(solution)/shard_map/all_to_all | solution.py:297
  89.6 15.8 %all_to_all.16.landed = f32[16,8,256]{2,1,0:T(8,128)S(1)} all-to-all(f32[16,8,256]{2,1,0:T(8,128)S(1)} %broadcast_in_dim.5), channel_id=1, replica_groups=mesh['ya'=4,'yb'=2,'tc'=2,'gz'=8,'gy'=4] {'ya','gy'}, dimensions={0} | all-to-all | bytes 262144 | tf_op jit(solution)/shard_map/all_to_all | solution.py:297
  105.4 1.1 %shard_map.53 = bf16[8,128,256]{2,1,0:T(8,128)(2,1)} custom-call(f32[16,8,256]{2,1,0:T(8,128)S(1)} %all_to_all.16.landed, f32[8,128,256]{2,1,0:T(8,128)S(1)} %get-tuple-element.40.image, bf16[8,128,256]{2,1,0:T(8,128)(2,1)S(1)} %get-tuple-element.32.field.source), custom_call_target="tpu_custom_call" | custom-call | tf_op jit(solution)/shard_map/pallas_call | solution.py:256
  (4 shorter events, 0.0 us)
Async XLA Ops:
  1.9 29.2 %all-to-all-start = ((bf16[8,144,256]{2,1,0:T(8,128)(2,1)}), bf16[8,144,256]{2,1,0:T(8,128)(2,1)S(1)}, u32[]{:S(2)}, u32[]{:S(2)}) async-start(bf16[8,144,256]{2,1,0:T(8,128)(2,1)} %shard_map.46), calls=%async_computation | async-start | bytes 1179648 | tf_op jit(solution)/shard_map/all_to_all | solution.py:297
  12.3 1.3 %copy-start.2 = (bf16[9,1,2,2,2,64,128]{6,5,4,3,2,1,0:T(8,128)(2,1)S(1)}, bf16[9,1,2,2,2,64,128]{6,5,4,3,2,1,0:T(8,128)(2,1)}, u32[]{:S(2)}) copy-start(bf16[9,1,2,2,2,64,128]{6,5,4,3,2,1,0:T(8,128)(2,1)} %param.5) | copy-start | bytes 3538948
  14.1 0.9 copy-start
  31.4 14.2 %collective-permute-start = (bf16[4,128,256]{2,1,0:T(8,128)(2,1)S(1)}, bf16[4,128,256]{2,1,0:T(8,128)(2,1)S(1)}, u32[]{:S(2)}, u32[]{:S(2)}) collective-permute-start(bf16[4,128,256]{2,1,0:T(8,128)(2,1)S(1)} %get-tuple-element.33), channel_id=1, source_target_pairs={{0,1},{1,2},{2,3},{3,0},{4,5},{5,6},{6,7},{7,4},{8,9},{9,10},{10,1... | collective-permute-start | bytes 786440 | tf_op jit(solution)/shard_map/ppermute | solution.py:39
  34.8 13.1 %collective-permute-start.1 = (bf16[4,128,256]{2,1,0:T(8,128)(2,1)S(1)}, bf16[4,128,256]{2,1,0:T(8,128)(2,1)S(1)}, u32[]{:S(2)}, u32[]{:S(2)}) collective-permute-start(bf16[4,128,256]{2,1,0:T(8,128)(2,1)S(1)} %get-tuple-element.34), channel_id=1, source_target_pairs={{0,3},{1,0},{2,1},{3,2},{4,7},{5,4},{6,5},{7,6},{8,11},{9,8},{10,9... | collective-permute-start | bytes 786440 | tf_op jit(solution)/shard_map/ppermute | solution.py:39
  38.5 10.8 %collective-permute-start.2 = (bf16[4,128,256]{2,1,0:T(8,128)(2,1)S(1)}, bf16[4,128,256]{2,1,0:T(8,128)(2,1)S(1)}, u32[]{:S(2)}, u32[]{:S(2)}) collective-permute-start(bf16[4,128,256]{2,1,0:T(8,128)(2,1)S(1)} %get-tuple-element.35), channel_id=1, source_target_pairs={{0,4},{4,8},{8,12},{12,16},{16,20},{20,24},{24,28},{28,0},{1,5},{5... | collective-permute-start | bytes 786440 | tf_op jit(solution)/shard_map/ppermute | solution.py:39
  41.0 9.5 %collective-permute-start.3 = (bf16[4,128,256]{2,1,0:T(8,128)(2,1)S(1)}, bf16[4,128,256]{2,1,0:T(8,128)(2,1)S(1)}, u32[]{:S(2)}, u32[]{:S(2)}) collective-permute-start(bf16[4,128,256]{2,1,0:T(8,128)(2,1)S(1)} %get-tuple-element.36), channel_id=1, source_target_pairs={{0,28},{4,0},{8,4},{12,8},{16,12},{20,16},{24,20},{28,24},{1,29},{... | collective-permute-start | bytes 786440 | tf_op jit(solution)/shard_map/ppermute | solution.py:39
  45.6 5.8 %collective-permute-start.4 = (bf16[4,128,256]{2,1,0:T(8,128)(2,1)S(1)}, bf16[4,128,256]{2,1,0:T(8,128)(2,1)S(1)}, u32[]{:S(2)}, u32[]{:S(2)}) collective-permute-start(bf16[4,128,256]{2,1,0:T(8,128)(2,1)S(1)} %get-tuple-element.37), channel_id=1, source_target_pairs={{0,32},{32,64},{64,96},{96,128},{128,160},{160,192},{192,224},{224... | collective-permute-start | bytes 786440 | tf_op jit(solution)/shard_map/ppermute | solution.py:39
  45.6 5.8 %collective-permute-start.5 = (bf16[4,128,256]{2,1,0:T(8,128)(2,1)S(1)}, bf16[4,128,256]{2,1,0:T(8,128)(2,1)S(1)}, u32[]{:S(2)}, u32[]{:S(2)}) collective-permute-start(bf16[4,128,256]{2,1,0:T(8,128)(2,1)S(1)} %get-tuple-element.38), channel_id=1, source_target_pairs={{0,480},{32,0},{64,32},{96,64},{128,96},{160,128},{192,160},{224,1... | collective-permute-start | bytes 786440 | tf_op jit(solution)/shard_map/ppermute | solution.py:39
  47.3 4.1 %copy-start.1 = (bf16[8,128,384]{2,1,0:T(8,128)(2,1)S(1)}, bf16[8,128,384]{2,1,0:T(8,128)(2,1)}, u32[]{:S(2)}) copy-start(bf16[8,128,384]{2,1,0:T(8,128)(2,1)} %copy-done) | copy-start | bytes 2359300
  51.9 14.7 %collective-permute-start.6 = (bf16[4,128,256]{2,1,0:T(8,128)(2,1)S(1)}, bf16[4,128,256]{2,1,0:T(8,128)(2,1)S(1)}, u32[]{:S(2)}, u32[]{:S(2)}) collective-permute-start(bf16[4,128,256]{2,1,0:T(8,128)(2,1)S(1)} %get-tuple-element.43), channel_id=1, source_target_pairs={{0,1},{1,2},{2,3},{3,0},{4,5},{5,6},{6,7},{7,4},{8,9},{9,10},{10,1... | collective-permute-start | bytes 786440 | tf_op jit(solution)/shard_map/ppermute | solution.py:39
  54.1 14.4 %collective-permute-start.7 = (bf16[4,128,256]{2,1,0:T(8,128)(2,1)S(1)}, bf16[4,128,256]{2,1,0:T(8,128)(2,1)S(1)}, u32[]{:S(2)}, u32[]{:S(2)}) collective-permute-start(bf16[4,128,256]{2,1,0:T(8,128)(2,1)S(1)} %get-tuple-element.44), channel_id=1, source_target_pairs={{0,3},{1,0},{2,1},{3,2},{4,7},{5,4},{6,5},{7,6},{8,11},{9,8},{10,9... | collective-permute-start | bytes 786440 | tf_op jit(solution)/shard_map/ppermute | solution.py:39
  59.0 12.1 %collective-permute-start.8 = (bf16[4,128,256]{2,1,0:T(8,128)(2,1)S(1)}, bf16[4,128,256]{2,1,0:T(8,128)(2,1)S(1)}, u32[]{:S(2)}, u32[]{:S(2)}) collective-permute-start(bf16[4,128,256]{2,1,0:T(8,128)(2,1)S(1)} %get-tuple-element.45), channel_id=1, source_target_pairs={{0,4},{4,8},{8,12},{12,16},{16,20},{20,24},{24,28},{28,0},{1,5},{5... | collective-permute-start | bytes 786440 | tf_op jit(solution)/shard_map/ppermute | solution.py:39
  60.9 11.7 %collective-permute-start.9 = (bf16[4,128,256]{2,1,0:T(8,128)(2,1)S(1)}, bf16[4,128,256]{2,1,0:T(8,128)(2,1)S(1)}, u32[]{:S(2)}, u32[]{:S(2)}) collective-permute-start(bf16[4,128,256]{2,1,0:T(8,128)(2,1)S(1)} %get-tuple-element.46), channel_id=1, source_target_pairs={{0,28},{4,0},{8,4},{12,8},{16,12},{20,16},{24,20},{28,24},{1,29},{... | collective-permute-start | bytes 786440 | tf_op jit(solution)/shard_map/ppermute | solution.py:39
  66.0 6.6 %collective-permute-start.10 = (bf16[4,128,256]{2,1,0:T(8,128)(2,1)S(1)}, bf16[4,128,256]{2,1,0:T(8,128)(2,1)S(1)}, u32[]{:S(2)}, u32[]{:S(2)}) collective-permute-start(bf16[4,128,256]{2,1,0:T(8,128)(2,1)S(1)} %get-tuple-element.47), channel_id=1, source_target_pairs={{0,32},{32,64},{64,96},{96,128},{128,160},{160,192},{192,224},{224... | collective-permute-start | bytes 786440 | tf_op jit(solution)/shard_map/ppermute | solution.py:39
  66.6 6.0 %collective-permute-start.11 = (bf16[4,128,256]{2,1,0:T(8,128)(2,1)S(1)}, bf16[4,128,256]{2,1,0:T(8,128)(2,1)S(1)}, u32[]{:S(2)}, u32[]{:S(2)}) collective-permute-start(bf16[4,128,256]{2,1,0:T(8,128)(2,1)S(1)} %get-tuple-element.48), channel_id=1, source_target_pairs={{0,480},{32,0},{64,32},{96,64},{128,96},{160,128},{192,160},{224,1... | collective-permute-start | bytes 786440 | tf_op jit(solution)/shard_map/ppermute | solution.py:39

commit v5 on v4

--- a/solution.py
+++ b/solution.py
@@ -3,11 +3,14 @@
 from jax import lax
 from jax.experimental import pallas as pl
 from jax.experimental.pallas import tpu as pltpu
+import numpy as np
 from jax.sharding import Mesh, PartitionSpec as P
 
 ALL_AXES = ("ya", "yb", "tc", "gz", "gy")
 TIME_AXES = ("ya", "yb", "tc")
+TC, GZ, GY = 2, 3, 4
 SLOT_ROWS = 16
+LANES = 128
 SITES = 8
 BITS = (4, 2, 1)
 LOW = tuple(tuple(s for s in range(SITES) if not s & bit) for bit in BITS)
@@ -39,73 +42,119 @@
     return lax.ppermute(values, axes, [(i, (i + step) % count) for i in range(count)])
 
 
-def pack_body(owners, slots, rows, payload, owner_mem, slot_mem, row_mem, sems):
+def pack_body(owners, slots, rows, payload, owner_mem, slot_mem, row_mem, tail_mem, sems, out_sems):
     count, depth, width = rows.shape
-    copies = [
+    lanes = payload.shape[2]
+    parts = width // lanes
+    loads = [
         pltpu.make_async_copy(owners, owner_mem, sems.at[0]),
         pltpu.make_async_copy(slots, slot_mem, sems.at[1]),
         pltpu.make_async_copy(rows, row_mem, sems.at[2]),
     ]
-    for copy in copies:
-        copy.start()
+    for load in loads:
+        load.start()
+    loads[0].wait()
+    loads[1].wait()
+    copies = []
+    for j in range(count):
+        mark = jnp.full((SLOT_ROWS, lanes), slot_mem[j].astype(jnp.float32))
+        tail_mem[j] = mark.astype(payload.dtype)
+        tail = payload.at[owner_mem[j], pl.ds(parts * depth, SLOT_ROWS)]
+        copies.append(pltpu.make_async_copy(tail_mem.at[j], tail, out_sems.at[j, parts]))
+        copies[-1].start()
+    loads[2].wait()
+    for j in range(count):
+        for part in range(parts):
+            block = row_mem.at[j, :, pl.ds(part * lanes, lanes)]
+            place = payload.at[owner_mem[j], pl.ds(part * depth, depth)]
+            copies.append(pltpu.make_async_copy(block, place, out_sems.at[j, part]))
+            copies[-1].start()
     for copy in copies:
         copy.wait()
-    for j in range(count):
-        to = owner_mem[j]
-        payload[to, 0:depth, :] = row_mem[j]
-        mark = jnp.full((SLOT_ROWS, width), slot_mem[j].astype(jnp.float32))
-        payload[to, depth : depth + SLOT_ROWS, :] = mark.astype(payload.dtype)
 
 
 def pack(rows, owners, slots):
     count, depth, width = rows.shape
+    parts = width // LANES
     return call(
         pack_body,
-        [shape_of((count, depth + SLOT_ROWS, width), rows.dtype)],
+        [shape_of((count, parts * depth + SLOT_ROWS, LANES), rows.dtype)],
         [IN_HBM] * 3,
         scratch=[
             pltpu.SMEM(owners.shape, owners.dtype),
             pltpu.SMEM(slots.shape, slots.dtype),
             pltpu.VMEM(rows.shape, rows.dtype),
+            pltpu.VMEM((count, SLOT_ROWS, LANES), rows.dtype),
             pltpu.SemaphoreType.DMA((3,)),
+            pltpu.SemaphoreType.DMA((count, parts + 1)),
         ],
+        out_spec=IN_HBM,
         limit=PACK_LIMIT,
     )(owners, slots, rows)[0]
 
 
+def each_core(body):
+    core = lax.axis_index("tc")
+
+    @pl.when(core == 0)
+    def _():
+        body((1, 0))
+
+    @pl.when(core != 0)
+    def _():
+        body((0, 1))
+
+
 def cut_faces(field, faces):
-    for axis in range(3):
-        for f in range(4):
-            faces[2 * axis][f] = field[LOW[axis][f]]
-            faces[2 * axis + 1][f] = field[HIGH[axis][f]]
+    def cut(order):
+        for place, axis in enumerate(order):
+            for f in range(4):
+                faces[2 * place][f] = field[HIGH[axis][f]]
+                faces[2 * place + 1][f] = field[LOW[axis][f]]
+
+    each_core(cut)
+    for f in range(4):
+        faces[4][f] = field[HIGH[2][f]]
+        faces[5][f] = field[LOW[2][f]]
 
 
 def place_body(landed, field, *faces):
-    depth = field.shape[1]
+    depth, width = field.shape[1], field.shape[2]
+    lanes = landed.shape[2]
+    parts = width // lanes
     for j in range(SITES):
-        mark = landed[j, depth : depth + SLOT_ROWS, 0:128].astype(jnp.float32)
+        mark = landed[j, parts * depth : parts * depth + SLOT_ROWS, :].astype(jnp.float32)
         slot = jnp.max(mark).astype(jnp.int32)
-        field[slot] = landed[j, 0:depth, :]
+        for part in range(parts):
+            block = landed[j, part * depth : (part + 1) * depth, :]
+            field[slot, :, part * lanes : (part + 1) * lanes] = block
     cut_faces(field, faces)
 
 
-def place(landed):
-    count, depth, width = landed.shape
-    depth = depth - SLOT_ROWS
+def place(landed, depth, width):
     face = shape_of((4, depth, width), landed.dtype)
-    out = call(place_body, [shape_of((count, depth, width), landed.dtype)] + [face] * 6, [WHOLE])(landed)
+    field = shape_of((landed.shape[0], depth, width), landed.dtype)
+    out = call(place_body, [field] + [face] * 6, [WHOLE])(landed)
     return out[0], out[1:]
 
 
+def crossed(values, first, step):
+    sizes = [lax.axis_size(axis) for axis in ALL_AXES]
+    pairs = []
+    for start in np.ndindex(*sizes):
+        to = list(start)
+        axis = GZ if start[TC] == first else GY
+        to[axis] = (to[axis] + step) % sizes[axis]
+        pairs.append(tuple(int(np.ravel_multi_index(at, sizes)) for at in (start, to)))
+    return lax.ppermute(values, ALL_AXES, pairs)
+
+
 def exchange(faces):
-    (low_y, high_y, low_z, high_z, low_t, high_t) = faces
-    before_z = shifted(high_z, "gz", 1)
-    before_y = shifted(high_y, "gy", 1)
-    behind_z = shifted(low_z, "gz", -1)
-    behind_y = shifted(low_y, "gy", -1)
-    before_t = shifted(high_t, TIME_AXES, 1)
-    behind_t = shifted(low_t, TIME_AXES, -1)
-    return [before_y, behind_y, before_z, behind_z, before_t, behind_t]
+    ahead, behind = crossed(faces[0], 0, 1), crossed(faces[1], 0, -1)
+    ahead_b, behind_b = crossed(faces[2], 1, 1), crossed(faces[3], 1, -1)
+    before_t = shifted(faces[4], TIME_AXES, 1)
+    behind_t = shifted(faces[5], TIME_AXES, -1)
+    return [ahead, behind, ahead_b, behind_b, before_t, behind_t]
 
 
 def near_product(s, inside, field):
@@ -165,24 +214,27 @@
     return call(near_sums_body, outs, [WHOLE] * 4, near_cost(field))(inside, field, image, source)
 
 
-def far_operand(s, received):
-    parts = []
-    for axis, bit in enumerate(BITS):
-        if s & bit:
-            parts.append(received[2 * axis + 1][HIGH[axis].index(s)])
+def far_operand(s, received, order):
+    parts = [None] * 3
+    for place, axis in enumerate(order + (2,)):
+        if s & BITS[axis]:
+            parts[axis] = received[2 * place + 1][HIGH[axis].index(s)]
         else:
-            parts.append(received[2 * axis][LOW[axis].index(s)])
+            parts[axis] = received[2 * place][LOW[axis].index(s)]
     return jnp.concatenate(parts, axis=0)
 
 
 def image_body(outside, partial, r0, r1, r2, r3, r4, r5, image, field, *faces):
     received = (r0, r1, r2, r3, r4, r5)
-    for s in range(SITES):
-        total = partial[s] + jnp.dot(
-            outside[s], far_operand(s, received), preferred_element_type=jnp.float32
-        )
-        image[s] = total
-        field[s] = total.astype(field.dtype)
+
+    def add(order):
+        for s in range(SITES):
+            operand = far_operand(s, received, order)
+            total = partial[s] + jnp.dot(outside[s], operand, preferred_element_type=jnp.float32)
+            image[s] = total
+            field[s] = total.astype(field.dtype)
+
+    each_core(add)
     cut_faces(field, faces)
 
 
@@ -197,24 +249,27 @@
 
 def sums_body(outside, partial, early, r0, r1, r2, r3, r4, r5, image, source, out):
     received = (r0, r1, r2, r3, r4, r5)
-    sums = [jnp.zeros((8, image.shape[2]), jnp.float32) for _ in range(5)]
-    for s in range(SITES):
-        second = partial[s] + jnp.dot(
-            outside[s], far_operand(s, received), preferred_element_type=jnp.float32
-        )
-        w_re, w_im = halves(second)
-        i_re, i_im = halves(image[s])
-        s_re, s_im = halves(source[s].astype(jnp.float32))
-        terms = (
-            i_re * w_re + i_im * w_im,
-            i_re * w_im - i_im * w_re,
-            w_re * s_re + w_im * s_im,
-            w_re * s_im - w_im * s_re,
-            w_re * w_re + w_im * w_im,
-        )
-        sums = [a + fold(b) for a, b in zip(sums, terms)]
-    nothing = jnp.zeros((8, image.shape[2]), jnp.float32)
-    out[...] = early[...] + row_sums([nothing] * 3 + sums)
+
+    def add(order):
+        sums = [jnp.zeros((8, image.shape[2]), jnp.float32) for _ in range(5)]
+        for s in range(SITES):
+            operand = far_operand(s, received, order)
+            second = partial[s] + jnp.dot(outside[s], operand, preferred_element_type=jnp.float32)
+            w_re, w_im = halves(second)
+            i_re, i_im = halves(image[s])
+            s_re, s_im = halves(source[s].astype(jnp.float32))
+            terms = (
+                i_re * w_re + i_im * w_im,
+                i_re * w_im - i_im * w_re,
+                w_re * s_re + w_im * s_im,
+                w_re * s_im - w_im * s_re,
+                w_re * w_re + w_im * w_im,
+            )
+            sums = [a + fold(b) for a, b in zip(sums, terms)]
+        nothing = jnp.zeros((8, image.shape[2]), jnp.float32)
+        out[...] = early[...] + row_sums([nothing] * 3 + sums)
+
+    each_core(add)
 
 
 def local_sums(outside, partial, early, received, image, source):
@@ -302,7 +357,7 @@
     rows = restricted.reshape(count, -1, width)
     landed = everyone(pack(rows, owners, coarse_site), "gz")
     landed, inside, outside = lax.optimization_barrier((landed, *split_couplings(couplings)))
-    source, faces = place(landed)
+    source, faces = place(landed, rows.shape[1], width)
     received = exchange(faces)
     image, field, faces = first_image(outside, near(inside, source), received)
     received = exchange(faces)

time: 107 us -> 107 us (level)
  waiting for transfers between devices: 23.8 us -> 22.3 us
    ppermute x0 -> x8, starting transfers between devices: none -> 28.2 us  [crossed(): return lax.ppermute(values, ALL_AXES, pairs)]
    ppermute x12 -> x4, starting transfers between devices: 31.7 us -> 3.5 us  [shifted(): lax.ppermute(values, axes, [(i, (i + step) % count) for i in range(count)])]
    ppermute x12 -> x4, waiting for transfers between devices: 7.59 us -> 3.18 us  [shifted(): lax.ppermute(values, axes, [(i, (i + step) % count) for i in range(count)])]
    ppermute x0 -> x8, waiting for transfers between devices: none -> 3.65 us  [crossed(): return lax.ppermute(values, ALL_AXES, pairs)]
  transfers between devices with their start and end apart: 13 -> 13, of which waited for: 6 -> 5; matrix products, arithmetic and copies ran while one was open for 0% -> 0% of each run, Pallas kernels for 2% -> 2%
where the time goes in v5:
time: 107 us; the launch traced here: 106 us
  starting transfers between devices  42.1 us (39%)
  blocking collectives  32.7 us (31%)
  waiting for transfers between devices  22.3 us (21%)
  Pallas kernels  6.57 us (6%)
  local copies, waits for them, and re-layouts  2.19 us (2%)
    all_to_all x2, blocking collectives, everyone(): return lax.all_to_all(parts, axes, split_axis=0, concat_axis=0, tiled=True)  29.5 us
    ppermute x8, starting transfers between devices, crossed(): return lax.ppermute(values, ALL_AXES, pairs)  28.2 us
    all_to_all x1, waiting for transfers between devices, everyone(): return lax.all_to_all(parts, axes, split_axis=0, concat_axis=0, tiled=True)  15.5 us
    all_to_all x1, starting transfers between devices, everyone(): return lax.all_to_all(parts, axes, split_axis=0, concat_axis=0, tiled=True)  10.4 us
    ppermute x8, waiting for transfers between devices, crossed(): return lax.ppermute(values, ALL_AXES, pairs)  3.65 us
    ppermute x4, starting transfers between devices, shifted(): lax.ppermute(values, axes, [(i, (i + step) % count) for i in range(count)])  3.5 us
    ppermute x4, waiting for transfers between devices, shifted(): lax.ppermute(values, axes, [(i, (i + step) % count) for i in range(count)])  3.18 us
    all_gather x1, blocking collectives, local(): parts = jnp.sum(lax.all_gather(parts, 'tc'), axis=0)  3.16 us
  transfers between devices with their start and end apart: 13, of which 5 were waited for; matrix products, arithmetic and copies ran while one was open for 0% of the time, Pallas kernels for 2%

profile of v5, /device:TPU:8, one launch (start us, length us, event | category | flops | bytes accessed | tf_op | source)
XLA Modules:
  0.0 106.0 jit_solution(10942655462659990008)
XLA Ops:
  0.0 2.1 %shard_map.46 = bf16[8,272,128]{2,1,0:T(8,128)(2,1)} custom-call(s32[8]{0:T(128)} %owners.1, s32[8]{0:T(128)} %slots.1, bf16[8,128,256]{2,1,0:T(8,128)(2,1)} %bitcast.6), custom_call_target="tpu_custom_call" | custom-call | tf_op jit(solution)/shard_map/pallas_call | solution.py:79
  2.1 10.4 %all-to-all-start = ((bf16[8,272,128]{2,1,0:T(8,128)(2,1)}), bf16[8,272,128]{2,1,0:T(8,128)(2,1)S(1)}, u32[]{:S(2)}, u32[]{:S(2)}) async-start(bf16[8,272,128]{2,1,0:T(8,128)(2,1)} %shard_map.46), calls=%async_computation | async-start | bytes 1114112 | tf_op jit(solution)/shard_map/all_to_all | solution.py:352
  12.4 0.0 copy-start.2
  12.5 1.3 %copy-done.2 = bf16[9,1,2,2,2,64,128]{6,5,4,3,2,1,0:T(8,128)(2,1)S(1)} copy-done((bf16[9,1,2,2,2,64,128]{6,5,4,3,2,1,0:T(8,128)(2,1)S(1)}, bf16[9,1,2,2,2,64,128]{6,5,4,3,2,1,0:T(8,128)(2,1)}, u32[]{:S(2)}) %copy-start.2) | copy-done | bytes 1179672
  13.7 0.5 shard_map.47
  14.2 0.0 copy-start
  14.3 0.9 copy-done
  15.2 15.5 %all-to-all-done.landed = bf16[8,272,128]{2,1,0:T(8,128)(2,1)S(1)} async-done(((bf16[8,272,128]{2,1,0:T(8,128)(2,1)}), bf16[8,272,128]{2,1,0:T(8,128)(2,1)S(1)}, u32[]{:S(2)}, u32[]{:S(2)}) %all-to-all-start) | async-done | bytes 557088 | tf_op jit(solution)/shard_map/all_to_all | solution.py:352
  30.6 0.3 shard_map.48
  31.0 2.5 %collective-permute-start = (bf16[4,128,256]{2,1,0:T(8,128)(2,1)S(1)}, bf16[4,128,256]{2,1,0:T(8,128)(2,1)S(1)}, u32[]{:S(2)}, u32[]{:S(2)}) collective-permute-start(bf16[4,128,256]{2,1,0:T(8,128)(2,1)S(1)} %get-tuple-element.33), channel_id=1, source_target_pairs={{0,4},{1,5},{2,6},{3,7},{4,8},{5,9},{6,10},{7,11},{8,12},{9,13},{1... | collective-permute-start | bytes 786440 | tf_op jit(solution)/shard_map/ppermute | solution.py:149
  33.4 4.6 %collective-permute-start.1 = (bf16[4,128,256]{2,1,0:T(8,128)(2,1)S(1)}, bf16[4,128,256]{2,1,0:T(8,128)(2,1)S(1)}, u32[]{:S(2)}, u32[]{:S(2)}) collective-permute-start(bf16[4,128,256]{2,1,0:T(8,128)(2,1)S(1)} %get-tuple-element.34), channel_id=1, source_target_pairs={{0,28},{1,29},{2,30},{3,31},{4,0},{5,1},{6,2},{7,3},{8,4},{9,5},{1... | collective-permute-start | bytes 786440 | tf_op jit(solution)/shard_map/ppermute | solution.py:149
  38.0 3.4 %collective-permute-start.2 = (bf16[4,128,256]{2,1,0:T(8,128)(2,1)S(1)}, bf16[4,128,256]{2,1,0:T(8,128)(2,1)S(1)}, u32[]{:S(2)}, u32[]{:S(2)}) collective-permute-start(bf16[4,128,256]{2,1,0:T(8,128)(2,1)S(1)} %get-tuple-element.35), channel_id=1, source_target_pairs={{0,1},{1,2},{2,3},{3,0},{4,5},{5,6},{6,7},{7,4},{8,9},{9,10},{10,1... | collective-permute-start | bytes 786440 | tf_op jit(solution)/shard_map/ppermute | solution.py:149
  41.4 3.7 %collective-permute-start.3 = (bf16[4,128,256]{2,1,0:T(8,128)(2,1)S(1)}, bf16[4,128,256]{2,1,0:T(8,128)(2,1)S(1)}, u32[]{:S(2)}, u32[]{:S(2)}) collective-permute-start(bf16[4,128,256]{2,1,0:T(8,128)(2,1)S(1)} %get-tuple-element.36), channel_id=1, source_target_pairs={{0,3},{1,0},{2,1},{3,2},{4,7},{5,4},{6,5},{7,6},{8,11},{9,8},{10,9... | collective-permute-start | bytes 786440 | tf_op jit(solution)/shard_map/ppermute | solution.py:149
  45.1 0.0 collective-permute-start.4
  45.1 0.0 collective-permute-done.r0
  45.1 1.7 %collective-permute-start.5 = (bf16[4,128,256]{2,1,0:T(8,128)(2,1)S(1)}, bf16[4,128,256]{2,1,0:T(8,128)(2,1)S(1)}, u32[]{:S(2)}, u32[]{:S(2)}) collective-permute-start(bf16[4,128,256]{2,1,0:T(8,128)(2,1)S(1)} %get-tuple-element.38), channel_id=1, source_target_pairs={{0,480},{32,0},{64,32},{96,64},{128,96},{160,128},{192,160},{224,1... | collective-permute-start | bytes 786440 | tf_op jit(solution)/shard_map/ppermute | solution.py:42
  46.9 0.0 copy-start.1
  46.9 0.6 shard_map.49.partial
  47.4 0.0 collective-permute-done.1.r1
  47.5 0.0 collective-permute-done.2.r2
  47.5 2.2 %collective-permute-done.3.r3 = bf16[4,128,256]{2,1,0:T(8,128)(2,1)S(1)} collective-permute-done((bf16[4,128,256]{2,1,0:T(8,128)(2,1)S(1)}, bf16[4,128,256]{2,1,0:T(8,128)(2,1)S(1)}, u32[]{:S(2)}, u32[]{:S(2)}) %collective-permute-start.3) | collective-permute-done | bytes 262176 | tf_op jit(solution)/shard_map/ppermute | solution.py:149
  49.7 1.2 %collective-permute-done.4.r4 = bf16[4,128,256]{2,1,0:T(8,128)(2,1)S(1)} collective-permute-done((bf16[4,128,256]{2,1,0:T(8,128)(2,1)S(1)}, bf16[4,128,256]{2,1,0:T(8,128)(2,1)S(1)}, u32[]{:S(2)}, u32[]{:S(2)}) %collective-permute-start.4) | collective-permute-done | bytes 262176 | tf_op jit(solution)/shard_map/ppermute | solution.py:42
  50.9 0.0 collective-permute-done.5.r5
  50.9 0.0 copy-done.1
  50.9 0.6 shard_map.50
  51.5 1.9 %collective-permute-start.6 = (bf16[4,128,256]{2,1,0:T(8,128)(2,1)S(1)}, bf16[4,128,256]{2,1,0:T(8,128)(2,1)S(1)}, u32[]{:S(2)}, u32[]{:S(2)}) collective-permute-start(bf16[4,128,256]{2,1,0:T(8,128)(2,1)S(1)} %get-tuple-element.43), channel_id=1, source_target_pairs={{0,4},{1,5},{2,6},{3,7},{4,8},{5,9},{6,10},{7,11},{8,12},{9,13},{1... | collective-permute-start | bytes 786440 | tf_op jit(solution)/shard_map/ppermute | solution.py:149
  53.4 5.1 %collective-permute-start.7 = (bf16[4,128,256]{2,1,0:T(8,128)(2,1)S(1)}, bf16[4,128,256]{2,1,0:T(8,128)(2,1)S(1)}, u32[]{:S(2)}, u32[]{:S(2)}) collective-permute-start(bf16[4,128,256]{2,1,0:T(8,128)(2,1)S(1)} %get-tuple-element.44), channel_id=1, source_target_pairs={{0,28},{1,29},{2,30},{3,31},{4,0},{5,1},{6,2},{7,3},{8,4},{9,5},{1... | collective-permute-start | bytes 786440 | tf_op jit(solution)/shard_map/ppermute | solution.py:149
  58.5 2.2 %collective-permute-start.8 = (bf16[4,128,256]{2,1,0:T(8,128)(2,1)S(1)}, bf16[4,128,256]{2,1,0:T(8,128)(2,1)S(1)}, u32[]{:S(2)}, u32[]{:S(2)}) collective-permute-start(bf16[4,128,256]{2,1,0:T(8,128)(2,1)S(1)} %get-tuple-element.45), channel_id=1, source_target_pairs={{0,1},{1,2},{2,3},{3,0},{4,5},{5,6},{6,7},{7,4},{8,9},{9,10},{10,1... | collective-permute-start | bytes 786440 | tf_op jit(solution)/shard_map/ppermute | solution.py:149
  60.8 4.9 %collective-permute-start.9 = (bf16[4,128,256]{2,1,0:T(8,128)(2,1)S(1)}, bf16[4,128,256]{2,1,0:T(8,128)(2,1)S(1)}, u32[]{:S(2)}, u32[]{:S(2)}) collective-permute-start(bf16[4,128,256]{2,1,0:T(8,128)(2,1)S(1)} %get-tuple-element.46), channel_id=1, source_target_pairs={{0,3},{1,0},{2,1},{3,2},{4,7},{5,4},{6,5},{7,6},{8,11},{9,8},{10,9... | collective-permute-start | bytes 786440 | tf_op jit(solution)/shard_map/ppermute | solution.py:149
  65.6 0.6 collective-permute-start.10
  66.2 0.0 collective-permute-done.6.r0
  66.2 1.2 %collective-permute-start.11 = (bf16[4,128,256]{2,1,0:T(8,128)(2,1)S(1)}, bf16[4,128,256]{2,1,0:T(8,128)(2,1)S(1)}, u32[]{:S(2)}, u32[]{:S(2)}) collective-permute-start(bf16[4,128,256]{2,1,0:T(8,128)(2,1)S(1)} %get-tuple-element.48), channel_id=1, source_target_pairs={{0,480},{32,0},{64,32},{96,64},{128,96},{160,128},{192,160},{224,1... | collective-permute-start | bytes 786440 | tf_op jit(solution)/shard_map/ppermute | solution.py:42
  67.4 0.7 shard_map.51
  68.0 0.0 collective-permute-done.7.r1
  68.1 0.0 collective-permute-done.8.r2
  68.1 1.4 %collective-permute-done.9.r3 = bf16[4,128,256]{2,1,0:T(8,128)(2,1)S(1)} collective-permute-done((bf16[4,128,256]{2,1,0:T(8,128)(2,1)S(1)}, bf16[4,128,256]{2,1,0:T(8,128)(2,1)S(1)}, u32[]{:S(2)}, u32[]{:S(2)}) %collective-permute-start.9) | collective-permute-done | bytes 262176 | tf_op jit(solution)/shard_map/ppermute | solution.py:149
  69.5 1.9 %collective-permute-done.10.r4 = bf16[4,128,256]{2,1,0:T(8,128)(2,1)S(1)} collective-permute-done((bf16[4,128,256]{2,1,0:T(8,128)(2,1)S(1)}, bf16[4,128,256]{2,1,0:T(8,128)(2,1)S(1)}, u32[]{:S(2)}, u32[]{:S(2)}) %collective-permute-start.10) | collective-permute-done | bytes 262176 | tf_op jit(solution)/shard_map/ppermute | solution.py:42
  71.4 0.0 collective-permute-done.11.r5
  71.4 0.8 shard_map.52
  72.2 3.2 %all-gather = f32[16,256]{1,0:T(8,128)S(1)} all-gather(f32[8,256]{1,0:T(8,128)S(1)} %shard_map.52), channel_id=2, replica_groups=mesh['ya'=4,'yb'=2,'tc'=2,'gz'=8,'gy'=4] {'tc'}, dimensions={0}, use_global_device_ids=true | all-gather | bytes 24576 | tf_op jit(solution)/shard_map/all_gather | solution.py:366
  75.4 12.2 %all_to_all.15 = f32[16,8,256]{2,1,0:T(8,128)S(1)} all-to-all(f32[16,8,256]{2,1,0:T(8,128)S(1)} %broadcast_in_dim.4), channel_id=1, replica_groups=mesh['ya'=4,'yb'=2,'tc'=2,'gz'=8,'gy'=4] {'yb','gz'}, dimensions={0} | all-to-all | bytes 262144 | tf_op jit(solution)/shard_map/all_to_all | solution.py:352
  87.6 17.4 %all_to_all.16.landed = f32[16,8,256]{2,1,0:T(8,128)S(1)} all-to-all(f32[16,8,256]{2,1,0:T(8,128)S(1)} %broadcast_in_dim.5), channel_id=1, replica_groups=mesh['ya'=4,'yb'=2,'tc'=2,'gz'=8,'gy'=4] {'ya','gy'}, dimensions={0} | all-to-all | bytes 262144 | tf_op jit(solution)/shard_map/all_to_all | solution.py:352
  104.9 1.1 %shard_map.53 = bf16[8,128,256]{2,1,0:T(8,128)(2,1)} custom-call(f32[16,8,256]{2,1,0:T(8,128)S(1)} %all_to_all.16.landed, f32[8,128,256]{2,1,0:T(8,128)S(1)} %get-tuple-element.40.image, bf16[8,128,256]{2,1,0:T(8,128)(2,1)S(1)} %get-tuple-element.32.field.source), custom_call_target="tpu_custom_call" | custom-call | tf_op jit(solution)/shard_map/pallas_call | solution.py:311
  (4 shorter events, 0.0 us)
Async XLA Ops:
  2.1 28.6 %all-to-all-start = ((bf16[8,272,128]{2,1,0:T(8,128)(2,1)}), bf16[8,272,128]{2,1,0:T(8,128)(2,1)S(1)}, u32[]{:S(2)}, u32[]{:S(2)}) async-start(bf16[8,272,128]{2,1,0:T(8,128)(2,1)} %shard_map.46), calls=%async_computation | async-start | bytes 1114112 | tf_op jit(solution)/shard_map/all_to_all | solution.py:352
  12.4 1.3 %copy-start.2 = (bf16[9,1,2,2,2,64,128]{6,5,4,3,2,1,0:T(8,128)(2,1)S(1)}, bf16[9,1,2,2,2,64,128]{6,5,4,3,2,1,0:T(8,128)(2,1)}, u32[]{:S(2)}) copy-start(bf16[9,1,2,2,2,64,128]{6,5,4,3,2,1,0:T(8,128)(2,1)} %param.5) | copy-start | bytes 3538948
  14.2 0.9 copy-start
  31.0 14.2 %collective-permute-start = (bf16[4,128,256]{2,1,0:T(8,128)(2,1)S(1)}, bf16[4,128,256]{2,1,0:T(8,128)(2,1)S(1)}, u32[]{:S(2)}, u32[]{:S(2)}) collective-permute-start(bf16[4,128,256]{2,1,0:T(8,128)(2,1)S(1)} %get-tuple-element.33), channel_id=1, source_target_pairs={{0,4},{1,5},{2,6},{3,7},{4,8},{5,9},{6,10},{7,11},{8,12},{9,13},{1... | collective-permute-start | bytes 786440 | tf_op jit(solution)/shard_map/ppermute | solution.py:149
  33.4 14.0 %collective-permute-start.1 = (bf16[4,128,256]{2,1,0:T(8,128)(2,1)S(1)}, bf16[4,128,256]{2,1,0:T(8,128)(2,1)S(1)}, u32[]{:S(2)}, u32[]{:S(2)}) collective-permute-start(bf16[4,128,256]{2,1,0:T(8,128)(2,1)S(1)} %get-tuple-element.34), channel_id=1, source_target_pairs={{0,28},{1,29},{2,30},{3,31},{4,0},{5,1},{6,2},{7,3},{8,4},{9,5},{1... | collective-permute-start | bytes 786440 | tf_op jit(solution)/shard_map/ppermute | solution.py:149
  38.0 9.5 %collective-permute-start.2 = (bf16[4,128,256]{2,1,0:T(8,128)(2,1)S(1)}, bf16[4,128,256]{2,1,0:T(8,128)(2,1)S(1)}, u32[]{:S(2)}, u32[]{:S(2)}) collective-permute-start(bf16[4,128,256]{2,1,0:T(8,128)(2,1)S(1)} %get-tuple-element.35), channel_id=1, source_target_pairs={{0,1},{1,2},{2,3},{3,0},{4,5},{5,6},{6,7},{7,4},{8,9},{9,10},{10,1... | collective-permute-start | bytes 786440 | tf_op jit(solution)/shard_map/ppermute | solution.py:149
  41.4 8.3 %collective-permute-start.3 = (bf16[4,128,256]{2,1,0:T(8,128)(2,1)S(1)}, bf16[4,128,256]{2,1,0:T(8,128)(2,1)S(1)}, u32[]{:S(2)}, u32[]{:S(2)}) collective-permute-start(bf16[4,128,256]{2,1,0:T(8,128)(2,1)S(1)} %get-tuple-element.36), channel_id=1, source_target_pairs={{0,3},{1,0},{2,1},{3,2},{4,7},{5,4},{6,5},{7,6},{8,11},{9,8},{10,9... | collective-permute-start | bytes 786440 | tf_op jit(solution)/shard_map/ppermute | solution.py:149
  45.1 5.8 %collective-permute-start.4 = (bf16[4,128,256]{2,1,0:T(8,128)(2,1)S(1)}, bf16[4,128,256]{2,1,0:T(8,128)(2,1)S(1)}, u32[]{:S(2)}, u32[]{:S(2)}) collective-permute-start(bf16[4,128,256]{2,1,0:T(8,128)(2,1)S(1)} %get-tuple-element.37), channel_id=1, source_target_pairs={{0,32},{32,64},{64,96},{96,128},{128,160},{160,192},{192,224},{224... | collective-permute-start | bytes 786440 | tf_op jit(solution)/shard_map/ppermute | solution.py:42
  45.1 5.8 %collective-permute-start.5 = (bf16[4,128,256]{2,1,0:T(8,128)(2,1)S(1)}, bf16[4,128,256]{2,1,0:T(8,128)(2,1)S(1)}, u32[]{:S(2)}, u32[]{:S(2)}) collective-permute-start(bf16[4,128,256]{2,1,0:T(8,128)(2,1)S(1)} %get-tuple-element.38), channel_id=1, source_target_pairs={{0,480},{32,0},{64,32},{96,64},{128,96},{160,128},{192,160},{224,1... | collective-permute-start | bytes 786440 | tf_op jit(solution)/shard_map/ppermute | solution.py:42
  46.9 4.1 %copy-start.1 = (bf16[8,128,384]{2,1,0:T(8,128)(2,1)S(1)}, bf16[8,128,384]{2,1,0:T(8,128)(2,1)}, u32[]{:S(2)}) copy-start(bf16[8,128,384]{2,1,0:T(8,128)(2,1)} %copy-done) | copy-start | bytes 2359300
  51.5 14.7 %collective-permute-start.6 = (bf16[4,128,256]{2,1,0:T(8,128)(2,1)S(1)}, bf16[4,128,256]{2,1,0:T(8,128)(2,1)S(1)}, u32[]{:S(2)}, u32[]{:S(2)}) collective-permute-start(bf16[4,128,256]{2,1,0:T(8,128)(2,1)S(1)} %get-tuple-element.43), channel_id=1, source_target_pairs={{0,4},{1,5},{2,6},{3,7},{4,8},{5,9},{6,10},{7,11},{8,12},{9,13},{1... | collective-permute-start | bytes 786440 | tf_op jit(solution)/shard_map/ppermute | solution.py:149
  53.4 14.6 %collective-permute-start.7 = (bf16[4,128,256]{2,1,0:T(8,128)(2,1)S(1)}, bf16[4,128,256]{2,1,0:T(8,128)(2,1)S(1)}, u32[]{:S(2)}, u32[]{:S(2)}) collective-permute-start(bf16[4,128,256]{2,1,0:T(8,128)(2,1)S(1)} %get-tuple-element.44), channel_id=1, source_target_pairs={{0,28},{1,29},{2,30},{3,31},{4,0},{5,1},{6,2},{7,3},{8,4},{9,5},{1... | collective-permute-start | bytes 786440 | tf_op jit(solution)/shard_map/ppermute | solution.py:149
  58.5 9.5 %collective-permute-start.8 = (bf16[4,128,256]{2,1,0:T(8,128)(2,1)S(1)}, bf16[4,128,256]{2,1,0:T(8,128)(2,1)S(1)}, u32[]{:S(2)}, u32[]{:S(2)}) collective-permute-start(bf16[4,128,256]{2,1,0:T(8,128)(2,1)S(1)} %get-tuple-element.45), channel_id=1, source_target_pairs={{0,1},{1,2},{2,3},{3,0},{4,5},{5,6},{6,7},{7,4},{8,9},{9,10},{10,1... | collective-permute-start | bytes 786440 | tf_op jit(solution)/shard_map/ppermute | solution.py:149
  60.8 8.7 %collective-permute-start.9 = (bf16[4,128,256]{2,1,0:T(8,128)(2,1)S(1)}, bf16[4,128,256]{2,1,0:T(8,128)(2,1)S(1)}, u32[]{:S(2)}, u32[]{:S(2)}) collective-permute-start(bf16[4,128,256]{2,1,0:T(8,128)(2,1)S(1)} %get-tuple-element.46), channel_id=1, source_target_pairs={{0,3},{1,0},{2,1},{3,2},{4,7},{5,4},{6,5},{7,6},{8,11},{9,8},{10,9... | collective-permute-start | bytes 786440 | tf_op jit(solution)/shard_map/ppermute | solution.py:149
  65.6 5.8 %collective-permute-start.10 = (bf16[4,128,256]{2,1,0:T(8,128)(2,1)S(1)}, bf16[4,128,256]{2,1,0:T(8,128)(2,1)S(1)}, u32[]{:S(2)}, u32[]{:S(2)}) collective-permute-start(bf16[4,128,256]{2,1,0:T(8,128)(2,1)S(1)} %get-tuple-element.47), channel_id=1, source_target_pairs={{0,32},{32,64},{64,96},{96,128},{128,160},{160,192},{192,224},{224... | collective-permute-start | bytes 786440 | tf_op jit(solution)/shard_map/ppermute | solution.py:42
  66.2 5.2 %collective-permute-start.11 = (bf16[4,128,256]{2,1,0:T(8,128)(2,1)S(1)}, bf16[4,128,256]{2,1,0:T(8,128)(2,1)S(1)}, u32[]{:S(2)}, u32[]{:S(2)}) collective-permute-start(bf16[4,128,256]{2,1,0:T(8,128)(2,1)S(1)} %get-tuple-element.48), channel_id=1, source_target_pairs={{0,480},{32,0},{64,32},{96,64},{128,96},{160,128},{192,160},{224,1... | collective-permute-start | bytes 786440 | tf_op jit(solution)/shard_map/ppermute | solution.py:42

commit v6 on v5

--- a/solution.py
+++ b/solution.py
@@ -9,6 +9,7 @@
 ALL_AXES = ("ya", "yb", "tc", "gz", "gy")
 TIME_AXES = ("ya", "yb", "tc")
 TC, GZ, GY = 2, 3, 4
+ORDER = (0, 1, 2, 4, 3, 5)
 SLOT_ROWS = 16
 LANES = 128
 SITES = 8
@@ -49,8 +50,8 @@
     loads = [
         pltpu.make_async_copy(owners, owner_mem, sems.at[0]),
         pltpu.make_async_copy(slots, slot_mem, sems.at[1]),
-        pltpu.make_async_copy(rows, row_mem, sems.at[2]),
     ]
+    loads += [pltpu.make_async_copy(rows.at[j], row_mem.at[j], sems.at[2 + j]) for j in range(count)]
     for load in loads:
         load.start()
     loads[0].wait()
@@ -62,8 +63,8 @@
         tail = payload.at[owner_mem[j], pl.ds(parts * depth, SLOT_ROWS)]
         copies.append(pltpu.make_async_copy(tail_mem.at[j], tail, out_sems.at[j, parts]))
         copies[-1].start()
-    loads[2].wait()
     for j in range(count):
+        loads[2 + j].wait()
         for part in range(parts):
             block = row_mem.at[j, :, pl.ds(part * lanes, lanes)]
             place = payload.at[owner_mem[j], pl.ds(part * depth, depth)]
@@ -85,7 +86,7 @@
             pltpu.SMEM(slots.shape, slots.dtype),
             pltpu.VMEM(rows.shape, rows.dtype),
             pltpu.VMEM((count, SLOT_ROWS, LANES), rows.dtype),
-            pltpu.SemaphoreType.DMA((3,)),
+            pltpu.SemaphoreType.DMA((count + 2,)),
             pltpu.SemaphoreType.DMA((count, parts + 1)),
         ],
         out_spec=IN_HBM,
@@ -105,7 +106,13 @@
         body((0, 1))
 
 
+def logical(listed):
+    return [listed[ORDER.index(i)] for i in range(len(ORDER))]
+
+
 def cut_faces(field, faces):
+    faces = logical(faces)
+
     def cut(order):
         for place, axis in enumerate(order):
             for f in range(4):
@@ -150,11 +157,13 @@
 
 
 def exchange(faces):
+    faces = logical(faces)
     ahead, behind = crossed(faces[0], 0, 1), crossed(faces[1], 0, -1)
     ahead_b, behind_b = crossed(faces[2], 1, 1), crossed(faces[3], 1, -1)
     before_t = shifted(faces[4], TIME_AXES, 1)
     behind_t = shifted(faces[5], TIME_AXES, -1)
-    return [ahead, behind, ahead_b, behind_b, before_t, behind_t]
+    received = [ahead, behind, ahead_b, behind_b, before_t, behind_t]
+    return [received[i] for i in ORDER]
 
 
 def near_product(s, inside, field):
@@ -225,7 +234,7 @@
 
 
 def image_body(outside, partial, r0, r1, r2, r3, r4, r5, image, field, *faces):
-    received = (r0, r1, r2, r3, r4, r5)
+    received = logical((r0, r1, r2, r3, r4, r5))
 
     def add(order):
         for s in range(SITES):
@@ -248,7 +257,7 @@
 
 
 def sums_body(outside, partial, early, r0, r1, r2, r3, r4, r5, image, source, out):
-    received = (r0, r1, r2, r3, r4, r5)
+    received = logical((r0, r1, r2, r3, r4, r5))
 
     def add(order):
         sums = [jnp.zeros((8, image.shape[2]), jnp.float32) for _ in range(5)]

time: 107 us -> 105 us (0.981)
  starting transfers between devices: 42.1 us -> 38.7 us
  waiting for transfers between devices: 22.3 us -> 23.8 us
    ppermute x8, waiting for transfers between devices: 3.65 us -> 8.32 us  [crossed(): return lax.ppermute(values, ALL_AXES, pairs)]
    ppermute x4, waiting for transfers between devices: 3.18 us -> 0.01 us  [shifted(): lax.ppermute(values, axes, [(i, (i + step) % count) for i in range(count)])]
    ppermute x4, starting transfers between devices: 3.5 us -> 0.71 us  [shifted(): lax.ppermute(values, axes, [(i, (i + step) % count) for i in range(count)])]
    all_to_all x2, blocking collectives: 29.5 us -> 31.1 us  [everyone(): return lax.all_to_all(parts, axes, split_axis=0, concat_axis=0, tiled=True)]
where the time goes in v6:
time: 105 us
  starting transfers between devices  38.7 us (37%)
  blocking collectives  33.3 us (32%)
  waiting for transfers between devices  23.8 us (23%)
  Pallas kernels  6.46 us (6%)
  local copies, waits for them, and re-layouts  2.19 us (2%)
    all_to_all x2, blocking collectives, everyone(): return lax.all_to_all(parts, axes, split_axis=0, concat_axis=0, tiled=True)  31.1 us
    ppermute x8, starting transfers between devices, crossed(): return lax.ppermute(values, ALL_AXES, pairs)  27.7 us
    all_to_all x1, waiting for transfers between devices, everyone(): return lax.all_to_all(parts, axes, split_axis=0, concat_axis=0, tiled=True)  15.5 us
    all_to_all x1, starting transfers between devices, everyone(): return lax.all_to_all(parts, axes, split_axis=0, concat_axis=0, tiled=True)  10.3 us
    ppermute x8, waiting for transfers between devices, crossed(): return lax.ppermute(values, ALL_AXES, pairs)  8.32 us
    all_gather x1, blocking collectives, local(): parts = jnp.sum(lax.all_gather(parts, 'tc'), axis=0)  2.21 us
    unnamed x6, local copies, waits for them, and re-layouts  2.17 us
  transfers between devices with their start and end apart: 13, of which 5 were waited for; matrix products, arithmetic and copies ran while one was open for 0% of the time, Pallas kernels for 2%

profile of v6, /device:TPU:8, one launch (start us, length us, event | category | flops | bytes accessed | tf_op | source)
XLA Modules:
  0.0 104.7 jit_solution(7020343581785158401)
XLA Ops:
  0.0 2.0 %shard_map.46 = bf16[8,272,128]{2,1,0:T(8,128)(2,1)} custom-call(s32[8]{0:T(128)} %owners.1, s32[8]{0:T(128)} %slots.1, bf16[8,128,256]{2,1,0:T(8,128)(2,1)} %bitcast.6), custom_call_target="tpu_custom_call" | custom-call | tf_op jit(solution)/shard_map/pallas_call | solution.py:80
  2.0 10.3 %all-to-all-start = ((bf16[8,272,128]{2,1,0:T(8,128)(2,1)}), bf16[8,272,128]{2,1,0:T(8,128)(2,1)S(1)}, u32[]{:S(2)}, u32[]{:S(2)}) async-start(bf16[8,272,128]{2,1,0:T(8,128)(2,1)} %shard_map.46), calls=%async_computation | async-start | bytes 1114112 | tf_op jit(solution)/shard_map/all_to_all | solution.py:361
  12.3 0.0 copy-start.2
  12.3 1.3 %copy-done.2 = bf16[9,1,2,2,2,64,128]{6,5,4,3,2,1,0:T(8,128)(2,1)S(1)} copy-done((bf16[9,1,2,2,2,64,128]{6,5,4,3,2,1,0:T(8,128)(2,1)S(1)}, bf16[9,1,2,2,2,64,128]{6,5,4,3,2,1,0:T(8,128)(2,1)}, u32[]{:S(2)}) %copy-start.2) | copy-done | bytes 1179672
  13.6 0.5 shard_map.47
  14.1 0.0 copy-start
  14.1 0.9 copy-done
  15.0 15.5 %all-to-all-done.landed = bf16[8,272,128]{2,1,0:T(8,128)(2,1)S(1)} async-done(((bf16[8,272,128]{2,1,0:T(8,128)(2,1)}), bf16[8,272,128]{2,1,0:T(8,128)(2,1)S(1)}, u32[]{:S(2)}, u32[]{:S(2)}) %all-to-all-start) | async-done | bytes 557088 | tf_op jit(solution)/shard_map/all_to_all | solution.py:361
  30.5 0.3 shard_map.48
  30.8 2.5 %collective-permute-start = (bf16[4,128,256]{2,1,0:T(8,128)(2,1)S(1)}, bf16[4,128,256]{2,1,0:T(8,128)(2,1)S(1)}, u32[]{:S(2)}, u32[]{:S(2)}) collective-permute-start(bf16[4,128,256]{2,1,0:T(8,128)(2,1)S(1)} %get-tuple-element.33), channel_id=1, source_target_pairs={{0,4},{1,5},{2,6},{3,7},{4,8},{5,9},{6,10},{7,11},{8,12},{9,13},{1... | collective-permute-start | bytes 786440 | tf_op jit(solution)/shard_map/ppermute | solution.py:156
  33.3 4.6 %collective-permute-start.1 = (bf16[4,128,256]{2,1,0:T(8,128)(2,1)S(1)}, bf16[4,128,256]{2,1,0:T(8,128)(2,1)S(1)}, u32[]{:S(2)}, u32[]{:S(2)}) collective-permute-start(bf16[4,128,256]{2,1,0:T(8,128)(2,1)S(1)} %get-tuple-element.34), channel_id=1, source_target_pairs={{0,28},{1,29},{2,30},{3,31},{4,0},{5,1},{6,2},{7,3},{8,4},{9,5},{1... | collective-permute-start | bytes 786440 | tf_op jit(solution)/shard_map/ppermute | solution.py:156
  37.9 3.4 %collective-permute-start.2 = (bf16[4,128,256]{2,1,0:T(8,128)(2,1)S(1)}, bf16[4,128,256]{2,1,0:T(8,128)(2,1)S(1)}, u32[]{:S(2)}, u32[]{:S(2)}) collective-permute-start(bf16[4,128,256]{2,1,0:T(8,128)(2,1)S(1)} %get-tuple-element.35), channel_id=1, source_target_pairs={{0,1},{1,2},{2,3},{3,0},{4,5},{5,6},{6,7},{7,4},{8,9},{9,10},{10,1... | collective-permute-start | bytes 786440 | tf_op jit(solution)/shard_map/ppermute | solution.py:156
  41.3 0.0 collective-permute-start.3
  41.3 3.7 %collective-permute-start.4 = (bf16[4,128,256]{2,1,0:T(8,128)(2,1)S(1)}, bf16[4,128,256]{2,1,0:T(8,128)(2,1)S(1)}, u32[]{:S(2)}, u32[]{:S(2)}) collective-permute-start(bf16[4,128,256]{2,1,0:T(8,128)(2,1)S(1)} %get-tuple-element.37), channel_id=1, source_target_pairs={{0,3},{1,0},{2,1},{3,2},{4,7},{5,4},{6,5},{7,6},{8,11},{9,8},{10,9... | collective-permute-start | bytes 786440 | tf_op jit(solution)/shard_map/ppermute | solution.py:156
  45.0 0.0 collective-permute-done.r0
  45.0 0.0 collective-permute-start.5
  45.0 0.0 copy-start.1
  45.0 0.6 shard_map.49.partial
  45.6 0.0 collective-permute-done.1.r1
  45.6 1.7 %collective-permute-done.2.r2 = bf16[4,128,256]{2,1,0:T(8,128)(2,1)S(1)} collective-permute-done((bf16[4,128,256]{2,1,0:T(8,128)(2,1)S(1)}, bf16[4,128,256]{2,1,0:T(8,128)(2,1)S(1)}, u32[]{:S(2)}, u32[]{:S(2)}) %collective-permute-start.2) | collective-permute-done | bytes 262176 | tf_op jit(solution)/shard_map/ppermute | solution.py:156
  47.4 0.0 collective-permute-done.3.r3
  47.4 2.2 %collective-permute-done.4.r4 = bf16[4,128,256]{2,1,0:T(8,128)(2,1)S(1)} collective-permute-done((bf16[4,128,256]{2,1,0:T(8,128)(2,1)S(1)}, bf16[4,128,256]{2,1,0:T(8,128)(2,1)S(1)}, u32[]{:S(2)}, u32[]{:S(2)}) %collective-permute-start.4) | collective-permute-done | bytes 262176 | tf_op jit(solution)/shard_map/ppermute | solution.py:156
  49.6 0.0 collective-permute-done.5.r5
  49.6 0.0 copy-done.1
  49.6 0.6 shard_map.50
  50.2 2.9 %collective-permute-start.6 = (bf16[4,128,256]{2,1,0:T(8,128)(2,1)S(1)}, bf16[4,128,256]{2,1,0:T(8,128)(2,1)S(1)}, u32[]{:S(2)}, u32[]{:S(2)}) collective-permute-start(bf16[4,128,256]{2,1,0:T(8,128)(2,1)S(1)} %get-tuple-element.43), channel_id=1, source_target_pairs={{0,4},{1,5},{2,6},{3,7},{4,8},{5,9},{6,10},{7,11},{8,12},{9,13},{1... | collective-permute-start | bytes 786440 | tf_op jit(solution)/shard_map/ppermute | solution.py:156
  53.1 4.1 %collective-permute-start.7 = (bf16[4,128,256]{2,1,0:T(8,128)(2,1)S(1)}, bf16[4,128,256]{2,1,0:T(8,128)(2,1)S(1)}, u32[]{:S(2)}, u32[]{:S(2)}) collective-permute-start(bf16[4,128,256]{2,1,0:T(8,128)(2,1)S(1)} %get-tuple-element.44), channel_id=1, source_target_pairs={{0,28},{1,29},{2,30},{3,31},{4,0},{5,1},{6,2},{7,3},{8,4},{9,5},{1... | collective-permute-start | bytes 786440 | tf_op jit(solution)/shard_map/ppermute | solution.py:156
  57.2 3.4 %collective-permute-start.8 = (bf16[4,128,256]{2,1,0:T(8,128)(2,1)S(1)}, bf16[4,128,256]{2,1,0:T(8,128)(2,1)S(1)}, u32[]{:S(2)}, u32[]{:S(2)}) collective-permute-start(bf16[4,128,256]{2,1,0:T(8,128)(2,1)S(1)} %get-tuple-element.45), channel_id=1, source_target_pairs={{0,1},{1,2},{2,3},{3,0},{4,5},{5,6},{6,7},{7,4},{8,9},{9,10},{10,1... | collective-permute-start | bytes 786440 | tf_op jit(solution)/shard_map/ppermute | solution.py:156
  60.6 0.6 collective-permute-start.9
  61.2 3.1 %collective-permute-start.10 = (bf16[4,128,256]{2,1,0:T(8,128)(2,1)S(1)}, bf16[4,128,256]{2,1,0:T(8,128)(2,1)S(1)}, u32[]{:S(2)}, u32[]{:S(2)}) collective-permute-start(bf16[4,128,256]{2,1,0:T(8,128)(2,1)S(1)} %get-tuple-element.47), channel_id=1, source_target_pairs={{0,3},{1,0},{2,1},{3,2},{4,7},{5,4},{6,5},{7,6},{8,11},{9,8},{10,9... | collective-permute-start | bytes 786440 | tf_op jit(solution)/shard_map/ppermute | solution.py:156
  64.3 0.0 collective-permute-done.6.r0
  64.4 0.1 collective-permute-start.11
  64.5 0.7 shard_map.51
  65.1 0.0 collective-permute-done.7.r1
  65.1 1.6 %collective-permute-done.8.r2 = bf16[4,128,256]{2,1,0:T(8,128)(2,1)S(1)} collective-permute-done((bf16[4,128,256]{2,1,0:T(8,128)(2,1)S(1)}, bf16[4,128,256]{2,1,0:T(8,128)(2,1)S(1)}, u32[]{:S(2)}, u32[]{:S(2)}) %collective-permute-start.8) | collective-permute-done | bytes 262176 | tf_op jit(solution)/shard_map/ppermute | solution.py:156
  66.7 0.0 collective-permute-done.9.r3
  66.7 2.7 %collective-permute-done.10.r4 = bf16[4,128,256]{2,1,0:T(8,128)(2,1)S(1)} collective-permute-done((bf16[4,128,256]{2,1,0:T(8,128)(2,1)S(1)}, bf16[4,128,256]{2,1,0:T(8,128)(2,1)S(1)}, u32[]{:S(2)}, u32[]{:S(2)}) %collective-permute-start.10) | collective-permute-done | bytes 262176 | tf_op jit(solution)/shard_map/ppermute | solution.py:156
  69.5 0.0 collective-permute-done.11.r5
  69.5 0.8 shard_map.52
  70.3 2.2 %all-gather = f32[16,256]{1,0:T(8,128)S(1)} all-gather(f32[8,256]{1,0:T(8,128)S(1)} %shard_map.52), channel_id=2, replica_groups=mesh['ya'=4,'yb'=2,'tc'=2,'gz'=8,'gy'=4] {'tc'}, dimensions={0}, use_global_device_ids=true | all-gather | bytes 24576 | tf_op jit(solution)/shard_map/all_gather | solution.py:375
  72.5 12.8 %all_to_all.15 = f32[16,8,256]{2,1,0:T(8,128)S(1)} all-to-all(f32[16,8,256]{2,1,0:T(8,128)S(1)} %broadcast_in_dim.4), channel_id=1, replica_groups=mesh['ya'=4,'yb'=2,'tc'=2,'gz'=8,'gy'=4] {'yb','gz'}, dimensions={0} | all-to-all | bytes 262144 | tf_op jit(solution)/shard_map/all_to_all | solution.py:361
  85.3 18.4 %all_to_all.16.landed = f32[16,8,256]{2,1,0:T(8,128)S(1)} all-to-all(f32[16,8,256]{2,1,0:T(8,128)S(1)} %broadcast_in_dim.5), channel_id=1, replica_groups=mesh['ya'=4,'yb'=2,'tc'=2,'gz'=8,'gy'=4] {'ya','gy'}, dimensions={0} | all-to-all | bytes 262144 | tf_op jit(solution)/shard_map/all_to_all | solution.py:361
  103.6 1.1 %shard_map.53 = bf16[8,128,256]{2,1,0:T(8,128)(2,1)} custom-call(f32[16,8,256]{2,1,0:T(8,128)S(1)} %all_to_all.16.landed, f32[8,128,256]{2,1,0:T(8,128)S(1)} %get-tuple-element.40.image, bf16[8,128,256]{2,1,0:T(8,128)(2,1)S(1)} %get-tuple-element.32.field.source), custom_call_target="tpu_custom_call" | custom-call | tf_op jit(solution)/shard_map/pallas_call | solution.py:320
  (4 shorter events, 0.0 us)
Async XLA Ops:
  2.0 28.5 %all-to-all-start = ((bf16[8,272,128]{2,1,0:T(8,128)(2,1)}), bf16[8,272,128]{2,1,0:T(8,128)(2,1)S(1)}, u32[]{:S(2)}, u32[]{:S(2)}) async-start(bf16[8,272,128]{2,1,0:T(8,128)(2,1)} %shard_map.46), calls=%async_computation | async-start | bytes 1114112 | tf_op jit(solution)/shard_map/all_to_all | solution.py:361
  12.3 1.3 %copy-start.2 = (bf16[9,1,2,2,2,64,128]{6,5,4,3,2,1,0:T(8,128)(2,1)S(1)}, bf16[9,1,2,2,2,64,128]{6,5,4,3,2,1,0:T(8,128)(2,1)}, u32[]{:S(2)}) copy-start(bf16[9,1,2,2,2,64,128]{6,5,4,3,2,1,0:T(8,128)(2,1)} %param.5) | copy-start | bytes 3538948
  14.1 0.9 copy-start
  30.8 14.2 %collective-permute-start = (bf16[4,128,256]{2,1,0:T(8,128)(2,1)S(1)}, bf16[4,128,256]{2,1,0:T(8,128)(2,1)S(1)}, u32[]{:S(2)}, u32[]{:S(2)}) collective-permute-start(bf16[4,128,256]{2,1,0:T(8,128)(2,1)S(1)} %get-tuple-element.33), channel_id=1, source_target_pairs={{0,4},{1,5},{2,6},{3,7},{4,8},{5,9},{6,10},{7,11},{8,12},{9,13},{1... | collective-permute-start | bytes 786440 | tf_op jit(solution)/shard_map/ppermute | solution.py:156
  33.3 12.3 %collective-permute-start.1 = (bf16[4,128,256]{2,1,0:T(8,128)(2,1)S(1)}, bf16[4,128,256]{2,1,0:T(8,128)(2,1)S(1)}, u32[]{:S(2)}, u32[]{:S(2)}) collective-permute-start(bf16[4,128,256]{2,1,0:T(8,128)(2,1)S(1)} %get-tuple-element.34), channel_id=1, source_target_pairs={{0,28},{1,29},{2,30},{3,31},{4,0},{5,1},{6,2},{7,3},{8,4},{9,5},{1... | collective-permute-start | bytes 786440 | tf_op jit(solution)/shard_map/ppermute | solution.py:156
  37.9 9.5 %collective-permute-start.2 = (bf16[4,128,256]{2,1,0:T(8,128)(2,1)S(1)}, bf16[4,128,256]{2,1,0:T(8,128)(2,1)S(1)}, u32[]{:S(2)}, u32[]{:S(2)}) collective-permute-start(bf16[4,128,256]{2,1,0:T(8,128)(2,1)S(1)} %get-tuple-element.35), channel_id=1, source_target_pairs={{0,1},{1,2},{2,3},{3,0},{4,5},{5,6},{6,7},{7,4},{8,9},{9,10},{10,1... | collective-permute-start | bytes 786440 | tf_op jit(solution)/shard_map/ppermute | solution.py:156
  41.3 6.1 %collective-permute-start.3 = (bf16[4,128,256]{2,1,0:T(8,128)(2,1)S(1)}, bf16[4,128,256]{2,1,0:T(8,128)(2,1)S(1)}, u32[]{:S(2)}, u32[]{:S(2)}) collective-permute-start(bf16[4,128,256]{2,1,0:T(8,128)(2,1)S(1)} %get-tuple-element.36), channel_id=1, source_target_pairs={{0,32},{32,64},{64,96},{96,128},{128,160},{160,192},{192,224},{224... | collective-permute-start | bytes 786440 | tf_op jit(solution)/shard_map/ppermute | solution.py:43
  41.3 8.3 %collective-permute-start.4 = (bf16[4,128,256]{2,1,0:T(8,128)(2,1)S(1)}, bf16[4,128,256]{2,1,0:T(8,128)(2,1)S(1)}, u32[]{:S(2)}, u32[]{:S(2)}) collective-permute-start(bf16[4,128,256]{2,1,0:T(8,128)(2,1)S(1)} %get-tuple-element.37), channel_id=1, source_target_pairs={{0,3},{1,0},{2,1},{3,2},{4,7},{5,4},{6,5},{7,6},{8,11},{9,8},{10,9... | collective-permute-start | bytes 786440 | tf_op jit(solution)/shard_map/ppermute | solution.py:156
  45.0 4.6 %collective-permute-start.5 = (bf16[4,128,256]{2,1,0:T(8,128)(2,1)S(1)}, bf16[4,128,256]{2,1,0:T(8,128)(2,1)S(1)}, u32[]{:S(2)}, u32[]{:S(2)}) collective-permute-start(bf16[4,128,256]{2,1,0:T(8,128)(2,1)S(1)} %get-tuple-element.38), channel_id=1, source_target_pairs={{0,480},{32,0},{64,32},{96,64},{128,96},{160,128},{192,160},{224,1... | collective-permute-start | bytes 786440 | tf_op jit(solution)/shard_map/ppermute | solution.py:43
  45.0 4.6 %copy-start.1 = (bf16[8,128,384]{2,1,0:T(8,128)(2,1)S(1)}, bf16[8,128,384]{2,1,0:T(8,128)(2,1)}, u32[]{:S(2)}) copy-start(bf16[8,128,384]{2,1,0:T(8,128)(2,1)} %copy-done) | copy-start | bytes 2359300
  50.2 14.2 %collective-permute-start.6 = (bf16[4,128,256]{2,1,0:T(8,128)(2,1)S(1)}, bf16[4,128,256]{2,1,0:T(8,128)(2,1)S(1)}, u32[]{:S(2)}, u32[]{:S(2)}) collective-permute-start(bf16[4,128,256]{2,1,0:T(8,128)(2,1)S(1)} %get-tuple-element.43), channel_id=1, source_target_pairs={{0,4},{1,5},{2,6},{3,7},{4,8},{5,9},{6,10},{7,11},{8,12},{9,13},{1... | collective-permute-start | bytes 786440 | tf_op jit(solution)/shard_map/ppermute | solution.py:156
  53.1 12.0 %collective-permute-start.7 = (bf16[4,128,256]{2,1,0:T(8,128)(2,1)S(1)}, bf16[4,128,256]{2,1,0:T(8,128)(2,1)S(1)}, u32[]{:S(2)}, u32[]{:S(2)}) collective-permute-start(bf16[4,128,256]{2,1,0:T(8,128)(2,1)S(1)} %get-tuple-element.44), channel_id=1, source_target_pairs={{0,28},{1,29},{2,30},{3,31},{4,0},{5,1},{6,2},{7,3},{8,4},{9,5},{1... | collective-permute-start | bytes 786440 | tf_op jit(solution)/shard_map/ppermute | solution.py:156
  57.2 9.5 %collective-permute-start.8 = (bf16[4,128,256]{2,1,0:T(8,128)(2,1)S(1)}, bf16[4,128,256]{2,1,0:T(8,128)(2,1)S(1)}, u32[]{:S(2)}, u32[]{:S(2)}) collective-permute-start(bf16[4,128,256]{2,1,0:T(8,128)(2,1)S(1)} %get-tuple-element.45), channel_id=1, source_target_pairs={{0,1},{1,2},{2,3},{3,0},{4,5},{5,6},{6,7},{7,4},{8,9},{9,10},{10,1... | collective-permute-start | bytes 786440 | tf_op jit(solution)/shard_map/ppermute | solution.py:156
  60.6 6.1 %collective-permute-start.9 = (bf16[4,128,256]{2,1,0:T(8,128)(2,1)S(1)}, bf16[4,128,256]{2,1,0:T(8,128)(2,1)S(1)}, u32[]{:S(2)}, u32[]{:S(2)}) collective-permute-start(bf16[4,128,256]{2,1,0:T(8,128)(2,1)S(1)} %get-tuple-element.46), channel_id=1, source_target_pairs={{0,32},{32,64},{64,96},{96,128},{128,160},{160,192},{192,224},{224... | collective-permute-start | bytes 786440 | tf_op jit(solution)/shard_map/ppermute | solution.py:43
  61.2 8.3 %collective-permute-start.10 = (bf16[4,128,256]{2,1,0:T(8,128)(2,1)S(1)}, bf16[4,128,256]{2,1,0:T(8,128)(2,1)S(1)}, u32[]{:S(2)}, u32[]{:S(2)}) collective-permute-start(bf16[4,128,256]{2,1,0:T(8,128)(2,1)S(1)} %get-tuple-element.47), channel_id=1, source_target_pairs={{0,3},{1,0},{2,1},{3,2},{4,7},{5,4},{6,5},{7,6},{8,11},{9,8},{10,9... | collective-permute-start | bytes 786440 | tf_op jit(solution)/shard_map/ppermute | solution.py:156
  64.4 5.1 %collective-permute-start.11 = (bf16[4,128,256]{2,1,0:T(8,128)(2,1)S(1)}, bf16[4,128,256]{2,1,0:T(8,128)(2,1)S(1)}, u32[]{:S(2)}, u32[]{:S(2)}) collective-permute-start(bf16[4,128,256]{2,1,0:T(8,128)(2,1)S(1)} %get-tuple-element.48), channel_id=1, source_target_pairs={{0,480},{32,0},{64,32},{96,64},{128,96},{160,128},{192,160},{224,1... | collective-permute-start | bytes 786440 | tf_op jit(solution)/shard_map/ppermute | solution.py:43

commit v7 on v6

--- a/solution.py
+++ b/solution.py
@@ -223,23 +223,41 @@
     return call(near_sums_body, outs, [WHOLE] * 4, near_cost(field))(inside, field, image, source)
 
 
-def far_operand(s, received, order):
-    parts = [None] * 3
+def far_products(s, outside, received, order, late):
+    total = 0.0
     for place, axis in enumerate(order + (2,)):
-        if s & BITS[axis]:
-            parts[axis] = received[2 * place + 1][HIGH[axis].index(s)]
-        else:
-            parts[axis] = received[2 * place][LOW[axis].index(s)]
-    return jnp.concatenate(parts, axis=0)
-
-
-def image_body(outside, partial, r0, r1, r2, r3, r4, r5, image, field, *faces):
-    received = logical((r0, r1, r2, r3, r4, r5))
+        ahead = s & BITS[axis] != 0
+        if late == (ahead and place > 0):
+            face = received[2 * place + (1 if ahead else 0)]
+            block = outside[s, :, axis * face.shape[1] : (axis + 1) * face.shape[1]]
+            operand = face[(HIGH if ahead else LOW)[axis].index(s)]
+            total = total + jnp.dot(block, operand, preferred_element_type=jnp.float32)
+    return total
+
+
+def early_body(outside, partial, r0, r1, r2, r4, out):
+    received = (r0, r1, r2, None, r4, None)
 
     def add(order):
         for s in range(SITES):
-            operand = far_operand(s, received, order)
-            total = partial[s] + jnp.dot(outside[s], operand, preferred_element_type=jnp.float32)
+            out[s] = partial[s] + far_products(s, outside, received, order, False)
+
+    each_core(add)
+
+
+def early_far(outside, partial, received):
+    r0, r1, r2, _, r4, _ = logical(received)
+    return call(early_body, [shape_of(partial.shape, partial.dtype)], [WHOLE] * 6, near_cost(partial))(
+        outside, partial, r0, r1, r2, r4
+    )[0]
+
+
+def image_body(outside, partial, r3, r5, image, field, *faces):
+    received = (None, None, None, r3, None, r5)
+
+    def add(order):
+        for s in range(SITES):
+            total = partial[s] + far_products(s, outside, received, order, True)
             image[s] = total
             field[s] = total.astype(field.dtype)
 
@@ -252,18 +270,18 @@
     dtype = received[0].dtype
     outs = [shape_of(partial.shape, jnp.float32), shape_of(partial.shape, dtype)]
     outs += [shape_of((4, depth, width), dtype)] * 6
-    out = call(image_body, outs, [WHOLE] * 8)(outside, partial, *received)
+    _, _, _, r3, _, r5 = logical(received)
+    out = call(image_body, outs, [WHOLE] * 4)(outside, partial, r3, r5)
     return out[0], out[1], out[2:]
 
 
-def sums_body(outside, partial, early, r0, r1, r2, r3, r4, r5, image, source, out):
-    received = logical((r0, r1, r2, r3, r4, r5))
+def sums_body(outside, partial, early, r3, r5, image, source, out):
+    received = (None, None, None, r3, None, r5)
 
     def add(order):
         sums = [jnp.zeros((8, image.shape[2]), jnp.float32) for _ in range(5)]
         for s in range(SITES):
-            operand = far_operand(s, received, order)
-            second = partial[s] + jnp.dot(outside[s], operand, preferred_element_type=jnp.float32)
+            second = partial[s] + far_products(s, outside, received, order, True)
             w_re, w_im = halves(second)
             i_re, i_im = halves(image[s])
             s_re, s_im = halves(source[s].astype(jnp.float32))
@@ -282,8 +300,9 @@
 
 
 def local_sums(outside, partial, early, received, image, source):
-    return call(sums_body, [shape_of(early.shape, early.dtype)], [WHOLE] * 11)(
-        outside, partial, early, *received, image, source
+    _, _, _, r3, _, r5 = logical(received)
+    return call(sums_body, [shape_of(early.shape, early.dtype)], [WHOLE] * 7)(
+        outside, partial, early, r3, r5, image, source
     )[0]
 
 
@@ -368,9 +387,11 @@
     landed, inside, outside = lax.optimization_barrier((landed, *split_couplings(couplings)))
     source, faces = place(landed, rows.shape[1], width)
     received = exchange(faces)
-    image, field, faces = first_image(outside, near(inside, source), received)
+    partial = early_far(outside, near(inside, source), received)
+    image, field, faces = first_image(outside, partial, received)
     received = exchange(faces)
     partial, early = near_sums(inside, field, image, source)
+    partial = early_far(outside, partial, received)
     parts = local_sums(outside, partial, early, received, image, source)
     parts = jnp.sum(lax.all_gather(parts, "tc"), axis=0)
     parts = jnp.sum(everyone(copies_of(parts, ("yb", "gz")), ("yb", "gz")), axis=0)

time: 105 us -> 105 us (level)
  waiting for transfers between devices: 23.8 us -> 22.5 us
    ppermute x8, waiting for transfers between devices: 8.32 us -> 6 us  [crossed(): return lax.ppermute(values, ALL_AXES, pairs)]
    unnamed x6 -> x8, local copies, waits for them, and re-layouts: 2.17 us -> 2.58 us
  transfers between devices with their start and end apart: 13 -> 13, of which waited for: 5 -> 5; matrix products, arithmetic and copies ran while one was open for 0% -> 0% of each run, Pallas kernels for 2% -> 3%
where the time goes in v7:
time: 105 us
  starting transfers between devices  38.7 us (37%)
  blocking collectives  33.3 us (32%)
  waiting for transfers between devices  22.5 us (21%)
  Pallas kernels  7.21 us (7%)
  local copies, waits for them, and re-layouts  2.6 us (2%)
    all_to_all x2, blocking collectives, everyone(): return lax.all_to_all(parts, axes, split_axis=0, concat_axis=0, tiled=True)  31.1 us
    ppermute x8, starting transfers between devices, crossed(): return lax.ppermute(values, ALL_AXES, pairs)  27.7 us
    all_to_all x1, waiting for transfers between devices, everyone(): return lax.all_to_all(parts, axes, split_axis=0, concat_axis=0, tiled=True)  16.5 us
    all_to_all x1, starting transfers between devices, everyone(): return lax.all_to_all(parts, axes, split_axis=0, concat_axis=0, tiled=True)  10.3 us
    ppermute x8, waiting for transfers between devices, crossed(): return lax.ppermute(values, ALL_AXES, pairs)  6 us
    unnamed x8, local copies, waits for them, and re-layouts  2.58 us
    all_gather x1, blocking collectives, local(): parts = jnp.sum(lax.all_gather(parts, 'tc'), axis=0)  2.22 us
    pallas_call x1, Pallas kernels, pack(): call(pack_body, [shape_of((count, parts * depth + SLOT_ROWS, LANES), rows...  2.11 us
  transfers between devices with their start and end apart: 13, of which 5 were waited for; matrix products, arithmetic and copies ran while one was open for 0% of the time, Pallas kernels for 3%

profile of v7, /device:TPU:8, one launch (start us, length us, event | category | flops | bytes accessed | tf_op | source)
XLA Modules:
  0.0 104.5 jit_solution(5512895981785630927)
XLA Ops:
  0.0 0.0 copy-start.3
  0.0 2.1 %shard_map.46 = bf16[8,272,128]{2,1,0:T(8,128)(2,1)} custom-call(s32[8]{0:T(128)} %owners.1, s32[8]{0:T(128)} %slots.1, bf16[8,128,256]{2,1,0:T(8,128)(2,1)} %bitcast.6), custom_call_target="tpu_custom_call" | custom-call | tf_op jit(solution)/shard_map/pallas_call | solution.py:80
  2.1 10.3 %all-to-all-start = ((bf16[8,272,128]{2,1,0:T(8,128)(2,1)}), bf16[8,272,128]{2,1,0:T(8,128)(2,1)S(1)}, u32[]{:S(2)}, u32[]{:S(2)}) async-start(bf16[8,272,128]{2,1,0:T(8,128)(2,1)} %shard_map.46), calls=%async_computation | async-start | bytes 1114112 | tf_op jit(solution)/shard_map/all_to_all | solution.py:380
  12.4 0.0 copy-done.3
  12.4 0.5 shard_map.47
  13.0 0.0 copy-start
  13.0 1.2 %copy-done = bf16[8,128,768]{2,1,0:T(8,128)(2,1)} copy-done((bf16[8,128,768]{2,1,0:T(8,128)(2,1)}, bf16[8,128,768]{2,1,0:T(8,128)(2,1)S(1)}, u32[]{:S(2)}) %copy-start) | copy-done | bytes 1572888
  14.1 16.5 %all-to-all-done.landed = bf16[8,272,128]{2,1,0:T(8,128)(2,1)S(1)} async-done(((bf16[8,272,128]{2,1,0:T(8,128)(2,1)}), bf16[8,272,128]{2,1,0:T(8,128)(2,1)S(1)}, u32[]{:S(2)}, u32[]{:S(2)}) %all-to-all-start) | async-done | bytes 557088 | tf_op jit(solution)/shard_map/all_to_all | solution.py:380
  30.6 0.3 shard_map.48
  30.9 2.5 %collective-permute-start = (bf16[4,128,256]{2,1,0:T(8,128)(2,1)S(1)}, bf16[4,128,256]{2,1,0:T(8,128)(2,1)S(1)}, u32[]{:S(2)}, u32[]{:S(2)}) collective-permute-start(bf16[4,128,256]{2,1,0:T(8,128)(2,1)S(1)} %get-tuple-element.33), channel_id=1, source_target_pairs={{0,4},{1,5},{2,6},{3,7},{4,8},{5,9},{6,10},{7,11},{8,12},{9,13},{1... | collective-permute-start | bytes 786440 | tf_op jit(solution)/shard_map/ppermute | solution.py:156
  33.4 4.6 %collective-permute-start.1 = (bf16[4,128,256]{2,1,0:T(8,128)(2,1)S(1)}, bf16[4,128,256]{2,1,0:T(8,128)(2,1)S(1)}, u32[]{:S(2)}, u32[]{:S(2)}) collective-permute-start(bf16[4,128,256]{2,1,0:T(8,128)(2,1)S(1)} %get-tuple-element.34), channel_id=1, source_target_pairs={{0,28},{1,29},{2,30},{3,31},{4,0},{5,1},{6,2},{7,3},{8,4},{9,5},{1... | collective-permute-start | bytes 786440 | tf_op jit(solution)/shard_map/ppermute | solution.py:156
  38.0 3.4 %collective-permute-start.2 = (bf16[4,128,256]{2,1,0:T(8,128)(2,1)S(1)}, bf16[4,128,256]{2,1,0:T(8,128)(2,1)S(1)}, u32[]{:S(2)}, u32[]{:S(2)}) collective-permute-start(bf16[4,128,256]{2,1,0:T(8,128)(2,1)S(1)} %get-tuple-element.35), channel_id=1, source_target_pairs={{0,1},{1,2},{2,3},{3,0},{4,5},{5,6},{6,7},{7,4},{8,9},{9,10},{10,1... | collective-permute-start | bytes 786440 | tf_op jit(solution)/shard_map/ppermute | solution.py:156
  41.4 0.0 collective-permute-start.3
  41.4 3.6 %collective-permute-start.4 = (bf16[4,128,256]{2,1,0:T(8,128)(2,1)S(1)}, bf16[4,128,256]{2,1,0:T(8,128)(2,1)S(1)}, u32[]{:S(2)}, u32[]{:S(2)}) collective-permute-start(bf16[4,128,256]{2,1,0:T(8,128)(2,1)S(1)} %get-tuple-element.37), channel_id=1, source_target_pairs={{0,3},{1,0},{2,1},{3,2},{4,7},{5,4},{6,5},{7,6},{8,11},{9,8},{10,9... | collective-permute-start | bytes 786440 | tf_op jit(solution)/shard_map/ppermute | solution.py:156
  45.1 0.0 collective-permute-done.r0
  45.1 0.0 collective-permute-start.5
  45.1 0.0 copy-start.1
  45.2 1.4 %copy-done.1 = bf16[8,128,768]{2,1,0:T(8,128)(2,1)S(1)} copy-done((bf16[8,128,768]{2,1,0:T(8,128)(2,1)S(1)}, bf16[8,128,768]{2,1,0:T(8,128)(2,1)}, u32[]{:S(2)}) %copy-start.1) | copy-done | bytes 1572888
  46.5 0.6 shard_map.49.partial
  47.1 0.0 collective-permute-done.1.r1
  47.1 0.3 collective-permute-done.2.r2
  47.5 0.0 collective-permute-done.3.r4
  47.5 0.4 shard_map.50.partial
  47.9 0.0 copy-start.2
  47.9 1.8 %collective-permute-done.4.r3 = bf16[4,128,256]{2,1,0:T(8,128)(2,1)S(1)} collective-permute-done((bf16[4,128,256]{2,1,0:T(8,128)(2,1)S(1)}, bf16[4,128,256]{2,1,0:T(8,128)(2,1)S(1)}, u32[]{:S(2)}, u32[]{:S(2)}) %collective-permute-start.4) | collective-permute-done | bytes 262176 | tf_op jit(solution)/shard_map/ppermute | solution.py:156
  49.7 0.0 collective-permute-done.5.r5
  49.7 0.4 shard_map.51
  50.1 2.9 %collective-permute-start.6 = (bf16[4,128,256]{2,1,0:T(8,128)(2,1)S(1)}, bf16[4,128,256]{2,1,0:T(8,128)(2,1)S(1)}, u32[]{:S(2)}, u32[]{:S(2)}) collective-permute-start(bf16[4,128,256]{2,1,0:T(8,128)(2,1)S(1)} %get-tuple-element.42), channel_id=1, source_target_pairs={{0,4},{1,5},{2,6},{3,7},{4,8},{5,9},{6,10},{7,11},{8,12},{9,13},{1... | collective-permute-start | bytes 786440 | tf_op jit(solution)/shard_map/ppermute | solution.py:156
  53.1 4.1 %collective-permute-start.7 = (bf16[4,128,256]{2,1,0:T(8,128)(2,1)S(1)}, bf16[4,128,256]{2,1,0:T(8,128)(2,1)S(1)}, u32[]{:S(2)}, u32[]{:S(2)}) collective-permute-start(bf16[4,128,256]{2,1,0:T(8,128)(2,1)S(1)} %get-tuple-element.43), channel_id=1, source_target_pairs={{0,28},{1,29},{2,30},{3,31},{4,0},{5,1},{6,2},{7,3},{8,4},{9,5},{1... | collective-permute-start | bytes 786440 | tf_op jit(solution)/shard_map/ppermute | solution.py:156
  57.2 3.4 %collective-permute-start.8 = (bf16[4,128,256]{2,1,0:T(8,128)(2,1)S(1)}, bf16[4,128,256]{2,1,0:T(8,128)(2,1)S(1)}, u32[]{:S(2)}, u32[]{:S(2)}) collective-permute-start(bf16[4,128,256]{2,1,0:T(8,128)(2,1)S(1)} %get-tuple-element.44), channel_id=1, source_target_pairs={{0,1},{1,2},{2,3},{3,0},{4,5},{5,6},{6,7},{7,4},{8,9},{9,10},{10,1... | collective-permute-start | bytes 786440 | tf_op jit(solution)/shard_map/ppermute | solution.py:156
  60.6 0.5 collective-permute-start.9
  61.1 3.1 %collective-permute-start.10 = (bf16[4,128,256]{2,1,0:T(8,128)(2,1)S(1)}, bf16[4,128,256]{2,1,0:T(8,128)(2,1)S(1)}, u32[]{:S(2)}, u32[]{:S(2)}) collective-permute-start(bf16[4,128,256]{2,1,0:T(8,128)(2,1)S(1)} %get-tuple-element.47), channel_id=1, source_target_pairs={{0,3},{1,0},{2,1},{3,2},{4,7},{5,4},{6,5},{7,6},{8,11},{9,8},{10,9... | collective-permute-start | bytes 786440 | tf_op jit(solution)/shard_map/ppermute | solution.py:156
  64.3 0.0 collective-permute-done.6.r0
  64.3 0.1 collective-permute-start.11
  64.4 0.0 copy-done.2
  64.4 0.7 shard_map.52
  65.1 0.0 collective-permute-done.7.r1
  65.1 1.6 %collective-permute-done.8.r2 = bf16[4,128,256]{2,1,0:T(8,128)(2,1)S(1)} collective-permute-done((bf16[4,128,256]{2,1,0:T(8,128)(2,1)S(1)}, bf16[4,128,256]{2,1,0:T(8,128)(2,1)S(1)}, u32[]{:S(2)}, u32[]{:S(2)}) %collective-permute-start.8) | collective-permute-done | bytes 262176 | tf_op jit(solution)/shard_map/ppermute | solution.py:156
  66.7 0.0 collective-permute-done.9.r4
  66.7 0.4 shard_map.53.partial
  67.1 2.3 %collective-permute-done.10.r3 = bf16[4,128,256]{2,1,0:T(8,128)(2,1)S(1)} collective-permute-done((bf16[4,128,256]{2,1,0:T(8,128)(2,1)S(1)}, bf16[4,128,256]{2,1,0:T(8,128)(2,1)S(1)}, u32[]{:S(2)}, u32[]{:S(2)}) %collective-permute-start.10) | collective-permute-done | bytes 262176 | tf_op jit(solution)/shard_map/ppermute | solution.py:156
  69.4 0.0 collective-permute-done.11.r5
  69.4 0.7 shard_map.54
  70.1 2.2 %all-gather = f32[16,256]{1,0:T(8,128)S(1)} all-gather(f32[8,256]{1,0:T(8,128)S(1)} %shard_map.54), channel_id=2, replica_groups=mesh['ya'=4,'yb'=2,'tc'=2,'gz'=8,'gy'=4] {'tc'}, dimensions={0}, use_global_device_ids=true | all-gather | bytes 24576 | tf_op jit(solution)/shard_map/all_gather | solution.py:396
  72.3 12.8 %all_to_all.15 = f32[16,8,256]{2,1,0:T(8,128)S(1)} all-to-all(f32[16,8,256]{2,1,0:T(8,128)S(1)} %broadcast_in_dim.4), channel_id=1, replica_groups=mesh['ya'=4,'yb'=2,'tc'=2,'gz'=8,'gy'=4] {'yb','gz'}, dimensions={0} | all-to-all | bytes 262144 | tf_op jit(solution)/shard_map/all_to_all | solution.py:380
  85.1 18.3 %all_to_all.16.landed = f32[16,8,256]{2,1,0:T(8,128)S(1)} all-to-all(f32[16,8,256]{2,1,0:T(8,128)S(1)} %broadcast_in_dim.5), channel_id=1, replica_groups=mesh['ya'=4,'yb'=2,'tc'=2,'gz'=8,'gy'=4] {'ya','gy'}, dimensions={0} | all-to-all | bytes 262144 | tf_op jit(solution)/shard_map/all_to_all | solution.py:380
  103.5 1.1 %shard_map.55 = bf16[8,128,256]{2,1,0:T(8,128)(2,1)} custom-call(f32[16,8,256]{2,1,0:T(8,128)S(1)} %all_to_all.16.landed, f32[8,128,256]{2,1,0:T(8,128)S(1)} %get-tuple-element.40.image, bf16[8,128,256]{2,1,0:T(8,128)(2,1)S(1)} %get-tuple-element.32.field.source), custom_call_target="tpu_custom_call" | custom-call | tf_op jit(solution)/shard_map/pallas_call | solution.py:339
  (4 shorter events, 0.0 us)
Async XLA Ops:
  0.0 12.4 %copy-start.3 = (bf16[9,1,2,2,2,64,128]{6,5,4,3,2,1,0:T(8,128)(2,1)S(1)}, bf16[9,1,2,2,2,64,128]{6,5,4,3,2,1,0:T(8,128)(2,1)}, u32[]{:S(2)}) copy-start(bf16[9,1,2,2,2,64,128]{6,5,4,3,2,1,0:T(8,128)(2,1)} %param.5) | copy-start | bytes 3538948
  2.1 28.5 %all-to-all-start = ((bf16[8,272,128]{2,1,0:T(8,128)(2,1)}), bf16[8,272,128]{2,1,0:T(8,128)(2,1)S(1)}, u32[]{:S(2)}, u32[]{:S(2)}) async-start(bf16[8,272,128]{2,1,0:T(8,128)(2,1)} %shard_map.46), calls=%async_computation | async-start | bytes 1114112 | tf_op jit(solution)/shard_map/all_to_all | solution.py:380
  13.0 1.2 %copy-start = (bf16[8,128,768]{2,1,0:T(8,128)(2,1)}, bf16[8,128,768]{2,1,0:T(8,128)(2,1)S(1)}, u32[]{:S(2)}) copy-start(bf16[8,128,768]{2,1,0:T(8,128)(2,1)S(1)} %get-tuple-element.30.inside) | copy-start | bytes 4718596
  30.9 14.2 %collective-permute-start = (bf16[4,128,256]{2,1,0:T(8,128)(2,1)S(1)}, bf16[4,128,256]{2,1,0:T(8,128)(2,1)S(1)}, u32[]{:S(2)}, u32[]{:S(2)}) collective-permute-start(bf16[4,128,256]{2,1,0:T(8,128)(2,1)S(1)} %get-tuple-element.33), channel_id=1, source_target_pairs={{0,4},{1,5},{2,6},{3,7},{4,8},{5,9},{6,10},{7,11},{8,12},{9,13},{1... | collective-permute-start | bytes 786440 | tf_op jit(solution)/shard_map/ppermute | solution.py:156
  33.4 13.7 %collective-permute-start.1 = (bf16[4,128,256]{2,1,0:T(8,128)(2,1)S(1)}, bf16[4,128,256]{2,1,0:T(8,128)(2,1)S(1)}, u32[]{:S(2)}, u32[]{:S(2)}) collective-permute-start(bf16[4,128,256]{2,1,0:T(8,128)(2,1)S(1)} %get-tuple-element.34), channel_id=1, source_target_pairs={{0,28},{1,29},{2,30},{3,31},{4,0},{5,1},{6,2},{7,3},{8,4},{9,5},{1... | collective-permute-start | bytes 786440 | tf_op jit(solution)/shard_map/ppermute | solution.py:156
  38.0 9.5 %collective-permute-start.2 = (bf16[4,128,256]{2,1,0:T(8,128)(2,1)S(1)}, bf16[4,128,256]{2,1,0:T(8,128)(2,1)S(1)}, u32[]{:S(2)}, u32[]{:S(2)}) collective-permute-start(bf16[4,128,256]{2,1,0:T(8,128)(2,1)S(1)} %get-tuple-element.35), channel_id=1, source_target_pairs={{0,1},{1,2},{2,3},{3,0},{4,5},{5,6},{6,7},{7,4},{8,9},{9,10},{10,1... | collective-permute-start | bytes 786440 | tf_op jit(solution)/shard_map/ppermute | solution.py:156
  41.4 6.1 %collective-permute-start.3 = (bf16[4,128,256]{2,1,0:T(8,128)(2,1)S(1)}, bf16[4,128,256]{2,1,0:T(8,128)(2,1)S(1)}, u32[]{:S(2)}, u32[]{:S(2)}) collective-permute-start(bf16[4,128,256]{2,1,0:T(8,128)(2,1)S(1)} %get-tuple-element.36), channel_id=1, source_target_pairs={{0,32},{32,64},{64,96},{96,128},{128,160},{160,192},{192,224},{224... | collective-permute-start | bytes 786440 | tf_op jit(solution)/shard_map/ppermute | solution.py:43
  41.4 8.3 %collective-permute-start.4 = (bf16[4,128,256]{2,1,0:T(8,128)(2,1)S(1)}, bf16[4,128,256]{2,1,0:T(8,128)(2,1)S(1)}, u32[]{:S(2)}, u32[]{:S(2)}) collective-permute-start(bf16[4,128,256]{2,1,0:T(8,128)(2,1)S(1)} %get-tuple-element.37), channel_id=1, source_target_pairs={{0,3},{1,0},{2,1},{3,2},{4,7},{5,4},{6,5},{7,6},{8,11},{9,8},{10,9... | collective-permute-start | bytes 786440 | tf_op jit(solution)/shard_map/ppermute | solution.py:156
  45.1 4.6 %collective-permute-start.5 = (bf16[4,128,256]{2,1,0:T(8,128)(2,1)S(1)}, bf16[4,128,256]{2,1,0:T(8,128)(2,1)S(1)}, u32[]{:S(2)}, u32[]{:S(2)}) collective-permute-start(bf16[4,128,256]{2,1,0:T(8,128)(2,1)S(1)} %get-tuple-element.38), channel_id=1, source_target_pairs={{0,480},{32,0},{64,32},{96,64},{128,96},{160,128},{192,160},{224,1... | collective-permute-start | bytes 786440 | tf_op jit(solution)/shard_map/ppermute | solution.py:43
  45.1 1.4 %copy-start.1 = (bf16[8,128,768]{2,1,0:T(8,128)(2,1)S(1)}, bf16[8,128,768]{2,1,0:T(8,128)(2,1)}, u32[]{:S(2)}) copy-start(bf16[8,128,768]{2,1,0:T(8,128)(2,1)} %copy-done) | copy-start | bytes 4718596
  47.9 16.5 %copy-start.2 = (bf16[8,128,768]{2,1,0:T(8,128)(2,1)S(1)}, bf16[8,128,768]{2,1,0:T(8,128)(2,1)}, u32[]{:S(2)}) copy-start(bf16[8,128,768]{2,1,0:T(8,128)(2,1)} %copy-done) | copy-start | bytes 4718596
  50.1 14.2 %collective-permute-start.6 = (bf16[4,128,256]{2,1,0:T(8,128)(2,1)S(1)}, bf16[4,128,256]{2,1,0:T(8,128)(2,1)S(1)}, u32[]{:S(2)}, u32[]{:S(2)}) collective-permute-start(bf16[4,128,256]{2,1,0:T(8,128)(2,1)S(1)} %get-tuple-element.42), channel_id=1, source_target_pairs={{0,4},{1,5},{2,6},{3,7},{4,8},{5,9},{6,10},{7,11},{8,12},{9,13},{1... | collective-permute-start | bytes 786440 | tf_op jit(solution)/shard_map/ppermute | solution.py:156
  53.1 12.0 %collective-permute-start.7 = (bf16[4,128,256]{2,1,0:T(8,128)(2,1)S(1)}, bf16[4,128,256]{2,1,0:T(8,128)(2,1)S(1)}, u32[]{:S(2)}, u32[]{:S(2)}) collective-permute-start(bf16[4,128,256]{2,1,0:T(8,128)(2,1)S(1)} %get-tuple-element.43), channel_id=1, source_target_pairs={{0,28},{1,29},{2,30},{3,31},{4,0},{5,1},{6,2},{7,3},{8,4},{9,5},{1... | collective-permute-start | bytes 786440 | tf_op jit(solution)/shard_map/ppermute | solution.py:156
  57.2 9.5 %collective-permute-start.8 = (bf16[4,128,256]{2,1,0:T(8,128)(2,1)S(1)}, bf16[4,128,256]{2,1,0:T(8,128)(2,1)S(1)}, u32[]{:S(2)}, u32[]{:S(2)}) collective-permute-start(bf16[4,128,256]{2,1,0:T(8,128)(2,1)S(1)} %get-tuple-element.44), channel_id=1, source_target_pairs={{0,1},{1,2},{2,3},{3,0},{4,5},{5,6},{6,7},{7,4},{8,9},{9,10},{10,1... | collective-permute-start | bytes 786440 | tf_op jit(solution)/shard_map/ppermute | solution.py:156
  60.6 6.1 %collective-permute-start.9 = (bf16[4,128,256]{2,1,0:T(8,128)(2,1)S(1)}, bf16[4,128,256]{2,1,0:T(8,128)(2,1)S(1)}, u32[]{:S(2)}, u32[]{:S(2)}) collective-permute-start(bf16[4,128,256]{2,1,0:T(8,128)(2,1)S(1)} %get-tuple-element.45), channel_id=1, source_target_pairs={{0,32},{32,64},{64,96},{96,128},{128,160},{160,192},{192,224},{224... | collective-permute-start | bytes 786440 | tf_op jit(solution)/shard_map/ppermute | solution.py:43
  61.1 8.3 %collective-permute-start.10 = (bf16[4,128,256]{2,1,0:T(8,128)(2,1)S(1)}, bf16[4,128,256]{2,1,0:T(8,128)(2,1)S(1)}, u32[]{:S(2)}, u32[]{:S(2)}) collective-permute-start(bf16[4,128,256]{2,1,0:T(8,128)(2,1)S(1)} %get-tuple-element.47), channel_id=1, source_target_pairs={{0,3},{1,0},{2,1},{3,2},{4,7},{5,4},{6,5},{7,6},{8,11},{9,8},{10,9... | collective-permute-start | bytes 786440 | tf_op jit(solution)/shard_map/ppermute | solution.py:156
  64.3 5.1 %collective-permute-start.11 = (bf16[4,128,256]{2,1,0:T(8,128)(2,1)S(1)}, bf16[4,128,256]{2,1,0:T(8,128)(2,1)S(1)}, u32[]{:S(2)}, u32[]{:S(2)}) collective-permute-start(bf16[4,128,256]{2,1,0:T(8,128)(2,1)S(1)} %get-tuple-element.48), channel_id=1, source_target_pairs={{0,480},{32,0},{64,32},{96,64},{128,96},{160,128},{192,160},{224,1... | collective-permute-start | bytes 786440 | tf_op jit(solution)/shard_map/ppermute | solution.py:43

commit v8 on v6

--- a/solution.py
+++ b/solution.py
@@ -372,9 +372,8 @@
     received = exchange(faces)
     partial, early = near_sums(inside, field, image, source)
     parts = local_sums(outside, partial, early, received, image, source)
-    parts = jnp.sum(lax.all_gather(parts, "tc"), axis=0)
-    parts = jnp.sum(everyone(copies_of(parts, ("yb", "gz")), ("yb", "gz")), axis=0)
-    parts = everyone(copies_of(parts, ("ya", "gy")), ("ya", "gy"))
+    parts = jnp.sum(everyone(copies_of(parts, ('tc', 'gz')), ('tc', 'gz')), axis=0)
+    parts = everyone(copies_of(parts, ('ya', 'yb', 'gy')), ('ya', 'yb', 'gy'))
     out = combine(parts, image, source)
     return out.reshape(couplings.shape[1:5] + restricted.shape[1:])
 

time: 105 us -> 105 us (level)
    all_gather x1 -> x0, blocking collectives: 2.21 us -> none  [local(): parts = jnp.sum(lax.all_gather(parts, 'tc'), axis=0)]
    all_to_all x2, blocking collectives: 31.1 us -> 33.2 us  [everyone(): return lax.all_to_all(parts, axes, split_axis=0, concat_axis=0, tiled=True)]
where the time goes in v8:
time: 105 us
  starting transfers between devices  38.7 us (37%)
  blocking collectives  33.2 us (32%)
  waiting for transfers between devices  23.8 us (23%)
  Pallas kernels  6.49 us (6%)
  local copies, waits for them, and re-layouts  2.19 us (2%)
    all_to_all x2, blocking collectives, everyone(): return lax.all_to_all(parts, axes, split_axis=0, concat_axis=0, tiled=True)  33.2 us
    ppermute x8, starting transfers between devices, crossed(): return lax.ppermute(values, ALL_AXES, pairs)  27.7 us
    all_to_all x1, waiting for transfers between devices, everyone(): return lax.all_to_all(parts, axes, split_axis=0, concat_axis=0, tiled=True)  15.5 us
    all_to_all x1, starting transfers between devices, everyone(): return lax.all_to_all(parts, axes, split_axis=0, concat_axis=0, tiled=True)  10.3 us
    ppermute x8, waiting for transfers between devices, crossed(): return lax.ppermute(values, ALL_AXES, pairs)  8.29 us
    unnamed x6, local copies, waits for them, and re-layouts  2.16 us
  transfers between devices with their start and end apart: 13, of which 5 were waited for; matrix products, arithmetic and copies ran while one was open for 0% of the time, Pallas kernels for 2%

profile of v8, /device:TPU:8, one launch (start us, length us, event | category | flops | bytes accessed | tf_op | source)
XLA Modules:
  0.0 104.6 jit_solution(3221647321757349817)
XLA Ops:
  0.0 2.0 %shard_map.46 = bf16[8,272,128]{2,1,0:T(8,128)(2,1)} custom-call(s32[8]{0:T(128)} %owners.1, s32[8]{0:T(128)} %slots.1, bf16[8,128,256]{2,1,0:T(8,128)(2,1)} %bitcast.4), custom_call_target="tpu_custom_call" | custom-call | tf_op jit(solution)/shard_map/pallas_call | solution.py:80
  2.0 10.3 %all-to-all-start = ((bf16[8,272,128]{2,1,0:T(8,128)(2,1)}), bf16[8,272,128]{2,1,0:T(8,128)(2,1)S(1)}, u32[]{:S(2)}, u32[]{:S(2)}) async-start(bf16[8,272,128]{2,1,0:T(8,128)(2,1)} %shard_map.46), calls=%async_computation | async-start | bytes 1114112 | tf_op jit(solution)/shard_map/all_to_all | solution.py:361
  12.3 0.0 copy-start.2
  12.3 1.3 %copy-done.2 = bf16[9,1,2,2,2,64,128]{6,5,4,3,2,1,0:T(8,128)(2,1)S(1)} copy-done((bf16[9,1,2,2,2,64,128]{6,5,4,3,2,1,0:T(8,128)(2,1)S(1)}, bf16[9,1,2,2,2,64,128]{6,5,4,3,2,1,0:T(8,128)(2,1)}, u32[]{:S(2)}) %copy-start.2) | copy-done | bytes 1179672
  13.6 0.5 shard_map.47
  14.1 0.0 copy-start
  14.1 0.9 copy-done
  15.0 15.5 %all-to-all-done.landed = bf16[8,272,128]{2,1,0:T(8,128)(2,1)S(1)} async-done(((bf16[8,272,128]{2,1,0:T(8,128)(2,1)}), bf16[8,272,128]{2,1,0:T(8,128)(2,1)S(1)}, u32[]{:S(2)}, u32[]{:S(2)}) %all-to-all-start) | async-done | bytes 557088 | tf_op jit(solution)/shard_map/all_to_all | solution.py:361
  30.5 0.3 shard_map.48
  30.8 2.5 %collective-permute-start = (bf16[4,128,256]{2,1,0:T(8,128)(2,1)S(1)}, bf16[4,128,256]{2,1,0:T(8,128)(2,1)S(1)}, u32[]{:S(2)}, u32[]{:S(2)}) collective-permute-start(bf16[4,128,256]{2,1,0:T(8,128)(2,1)S(1)} %get-tuple-element.33), channel_id=1, source_target_pairs={{0,4},{1,5},{2,6},{3,7},{4,8},{5,9},{6,10},{7,11},{8,12},{9,13},{1... | collective-permute-start | bytes 786440 | tf_op jit(solution)/shard_map/ppermute | solution.py:156
  33.3 4.6 %collective-permute-start.1 = (bf16[4,128,256]{2,1,0:T(8,128)(2,1)S(1)}, bf16[4,128,256]{2,1,0:T(8,128)(2,1)S(1)}, u32[]{:S(2)}, u32[]{:S(2)}) collective-permute-start(bf16[4,128,256]{2,1,0:T(8,128)(2,1)S(1)} %get-tuple-element.34), channel_id=1, source_target_pairs={{0,28},{1,29},{2,30},{3,31},{4,0},{5,1},{6,2},{7,3},{8,4},{9,5},{1... | collective-permute-start | bytes 786440 | tf_op jit(solution)/shard_map/ppermute | solution.py:156
  37.9 3.4 %collective-permute-start.2 = (bf16[4,128,256]{2,1,0:T(8,128)(2,1)S(1)}, bf16[4,128,256]{2,1,0:T(8,128)(2,1)S(1)}, u32[]{:S(2)}, u32[]{:S(2)}) collective-permute-start(bf16[4,128,256]{2,1,0:T(8,128)(2,1)S(1)} %get-tuple-element.35), channel_id=1, source_target_pairs={{0,1},{1,2},{2,3},{3,0},{4,5},{5,6},{6,7},{7,4},{8,9},{9,10},{10,1... | collective-permute-start | bytes 786440 | tf_op jit(solution)/shard_map/ppermute | solution.py:156
  41.3 0.0 collective-permute-start.3
  41.3 3.7 %collective-permute-start.4 = (bf16[4,128,256]{2,1,0:T(8,128)(2,1)S(1)}, bf16[4,128,256]{2,1,0:T(8,128)(2,1)S(1)}, u32[]{:S(2)}, u32[]{:S(2)}) collective-permute-start(bf16[4,128,256]{2,1,0:T(8,128)(2,1)S(1)} %get-tuple-element.37), channel_id=1, source_target_pairs={{0,3},{1,0},{2,1},{3,2},{4,7},{5,4},{6,5},{7,6},{8,11},{9,8},{10,9... | collective-permute-start | bytes 786440 | tf_op jit(solution)/shard_map/ppermute | solution.py:156
  45.0 0.0 collective-permute-done.r0
  45.0 0.0 collective-permute-start.5
  45.0 0.0 copy-start.1
  45.0 0.6 shard_map.49.partial
  45.6 0.0 collective-permute-done.1.r1
  45.6 1.7 %collective-permute-done.2.r2 = bf16[4,128,256]{2,1,0:T(8,128)(2,1)S(1)} collective-permute-done((bf16[4,128,256]{2,1,0:T(8,128)(2,1)S(1)}, bf16[4,128,256]{2,1,0:T(8,128)(2,1)S(1)}, u32[]{:S(2)}, u32[]{:S(2)}) %collective-permute-start.2) | collective-permute-done | bytes 262176 | tf_op jit(solution)/shard_map/ppermute | solution.py:156
  47.4 0.0 collective-permute-done.3.r3
  47.4 2.2 %collective-permute-done.4.r4 = bf16[4,128,256]{2,1,0:T(8,128)(2,1)S(1)} collective-permute-done((bf16[4,128,256]{2,1,0:T(8,128)(2,1)S(1)}, bf16[4,128,256]{2,1,0:T(8,128)(2,1)S(1)}, u32[]{:S(2)}, u32[]{:S(2)}) %collective-permute-start.4) | collective-permute-done | bytes 262176 | tf_op jit(solution)/shard_map/ppermute | solution.py:156
  49.6 0.0 collective-permute-done.5.r5
  49.6 0.0 copy-done.1
  49.6 0.6 shard_map.50
  50.2 2.9 %collective-permute-start.6 = (bf16[4,128,256]{2,1,0:T(8,128)(2,1)S(1)}, bf16[4,128,256]{2,1,0:T(8,128)(2,1)S(1)}, u32[]{:S(2)}, u32[]{:S(2)}) collective-permute-start(bf16[4,128,256]{2,1,0:T(8,128)(2,1)S(1)} %get-tuple-element.43), channel_id=1, source_target_pairs={{0,4},{1,5},{2,6},{3,7},{4,8},{5,9},{6,10},{7,11},{8,12},{9,13},{1... | collective-permute-start | bytes 786440 | tf_op jit(solution)/shard_map/ppermute | solution.py:156
  53.1 4.1 %collective-permute-start.7 = (bf16[4,128,256]{2,1,0:T(8,128)(2,1)S(1)}, bf16[4,128,256]{2,1,0:T(8,128)(2,1)S(1)}, u32[]{:S(2)}, u32[]{:S(2)}) collective-permute-start(bf16[4,128,256]{2,1,0:T(8,128)(2,1)S(1)} %get-tuple-element.44), channel_id=1, source_target_pairs={{0,28},{1,29},{2,30},{3,31},{4,0},{5,1},{6,2},{7,3},{8,4},{9,5},{1... | collective-permute-start | bytes 786440 | tf_op jit(solution)/shard_map/ppermute | solution.py:156
  57.2 3.4 %collective-permute-start.8 = (bf16[4,128,256]{2,1,0:T(8,128)(2,1)S(1)}, bf16[4,128,256]{2,1,0:T(8,128)(2,1)S(1)}, u32[]{:S(2)}, u32[]{:S(2)}) collective-permute-start(bf16[4,128,256]{2,1,0:T(8,128)(2,1)S(1)} %get-tuple-element.45), channel_id=1, source_target_pairs={{0,1},{1,2},{2,3},{3,0},{4,5},{5,6},{6,7},{7,4},{8,9},{9,10},{10,1... | collective-permute-start | bytes 786440 | tf_op jit(solution)/shard_map/ppermute | solution.py:156
  60.7 0.5 collective-permute-start.9
  61.2 3.1 %collective-permute-start.10 = (bf16[4,128,256]{2,1,0:T(8,128)(2,1)S(1)}, bf16[4,128,256]{2,1,0:T(8,128)(2,1)S(1)}, u32[]{:S(2)}, u32[]{:S(2)}) collective-permute-start(bf16[4,128,256]{2,1,0:T(8,128)(2,1)S(1)} %get-tuple-element.47), channel_id=1, source_target_pairs={{0,3},{1,0},{2,1},{3,2},{4,7},{5,4},{6,5},{7,6},{8,11},{9,8},{10,9... | collective-permute-start | bytes 786440 | tf_op jit(solution)/shard_map/ppermute | solution.py:156
  64.3 0.0 collective-permute-done.6.r0
  64.3 0.1 collective-permute-start.11
  64.5 0.7 shard_map.51
  65.1 0.0 collective-permute-done.7.r1
  65.1 1.6 %collective-permute-done.8.r2 = bf16[4,128,256]{2,1,0:T(8,128)(2,1)S(1)} collective-permute-done((bf16[4,128,256]{2,1,0:T(8,128)(2,1)S(1)}, bf16[4,128,256]{2,1,0:T(8,128)(2,1)S(1)}, u32[]{:S(2)}, u32[]{:S(2)}) %collective-permute-start.8) | collective-permute-done | bytes 262176 | tf_op jit(solution)/shard_map/ppermute | solution.py:156
  66.7 0.0 collective-permute-done.9.r3
  66.7 2.7 %collective-permute-done.10.r4 = bf16[4,128,256]{2,1,0:T(8,128)(2,1)S(1)} collective-permute-done((bf16[4,128,256]{2,1,0:T(8,128)(2,1)S(1)}, bf16[4,128,256]{2,1,0:T(8,128)(2,1)S(1)}, u32[]{:S(2)}, u32[]{:S(2)}) %collective-permute-start.10) | collective-permute-done | bytes 262176 | tf_op jit(solution)/shard_map/ppermute | solution.py:156
  69.5 0.0 collective-permute-done.11.r5
  69.5 0.8 shard_map.52
  70.3 11.6 %all_to_all.15 = f32[16,8,256]{2,1,0:T(8,128)S(1)} all-to-all(f32[16,8,256]{2,1,0:T(8,128)S(1)} %broadcast_in_dim.4), channel_id=1, replica_groups=mesh['ya'=4,'yb'=2,'tc'=2,'gz'=8,'gy'=4] {'tc','gz'}, dimensions={0} | all-to-all | bytes 262144 | tf_op jit(solution)/shard_map/all_to_all | solution.py:361
  81.9 21.6 %all_to_all.16.landed = f32[32,8,256]{2,1,0:T(8,128)S(1)} all-to-all(f32[32,8,256]{2,1,0:T(8,128)S(1)} %broadcast_in_dim.5), channel_id=1, replica_groups=mesh['ya'=4,'yb'=2,'tc'=2,'gz'=8,'gy'=4] {'ya','yb','gy'}, dimensions={0} | all-to-all | bytes 524288 | tf_op jit(solution)/shard_map/all_to_all | solution.py:361
  103.5 1.1 %shard_map.53 = bf16[8,128,256]{2,1,0:T(8,128)(2,1)} custom-call(f32[32,8,256]{2,1,0:T(8,128)S(1)} %all_to_all.16.landed, f32[8,128,256]{2,1,0:T(8,128)S(1)} %get-tuple-element.40.image, bf16[8,128,256]{2,1,0:T(8,128)(2,1)S(1)} %get-tuple-element.32.field.source), custom_call_target="tpu_custom_call" | custom-call | tf_op jit(solution)/shard_map/pallas_call | solution.py:320
  (3 shorter events, 0.0 us)
Async XLA Ops:
  2.0 28.5 %all-to-all-start = ((bf16[8,272,128]{2,1,0:T(8,128)(2,1)}), bf16[8,272,128]{2,1,0:T(8,128)(2,1)S(1)}, u32[]{:S(2)}, u32[]{:S(2)}) async-start(bf16[8,272,128]{2,1,0:T(8,128)(2,1)} %shard_map.46), calls=%async_computation | async-start | bytes 1114112 | tf_op jit(solution)/shard_map/all_to_all | solution.py:361
  12.3 1.3 %copy-start.2 = (bf16[9,1,2,2,2,64,128]{6,5,4,3,2,1,0:T(8,128)(2,1)S(1)}, bf16[9,1,2,2,2,64,128]{6,5,4,3,2,1,0:T(8,128)(2,1)}, u32[]{:S(2)}) copy-start(bf16[9,1,2,2,2,64,128]{6,5,4,3,2,1,0:T(8,128)(2,1)} %param.5) | copy-start | bytes 3538948
  14.1 0.9 copy-start
  30.8 14.2 %collective-permute-start = (bf16[4,128,256]{2,1,0:T(8,128)(2,1)S(1)}, bf16[4,128,256]{2,1,0:T(8,128)(2,1)S(1)}, u32[]{:S(2)}, u32[]{:S(2)}) collective-permute-start(bf16[4,128,256]{2,1,0:T(8,128)(2,1)S(1)} %get-tuple-element.33), channel_id=1, source_target_pairs={{0,4},{1,5},{2,6},{3,7},{4,8},{5,9},{6,10},{7,11},{8,12},{9,13},{1... | collective-permute-start | bytes 786440 | tf_op jit(solution)/shard_map/ppermute | solution.py:156
  33.3 12.3 %collective-permute-start.1 = (bf16[4,128,256]{2,1,0:T(8,128)(2,1)S(1)}, bf16[4,128,256]{2,1,0:T(8,128)(2,1)S(1)}, u32[]{:S(2)}, u32[]{:S(2)}) collective-permute-start(bf16[4,128,256]{2,1,0:T(8,128)(2,1)S(1)} %get-tuple-element.34), channel_id=1, source_target_pairs={{0,28},{1,29},{2,30},{3,31},{4,0},{5,1},{6,2},{7,3},{8,4},{9,5},{1... | collective-permute-start | bytes 786440 | tf_op jit(solution)/shard_map/ppermute | solution.py:156
  37.9 9.5 %collective-permute-start.2 = (bf16[4,128,256]{2,1,0:T(8,128)(2,1)S(1)}, bf16[4,128,256]{2,1,0:T(8,128)(2,1)S(1)}, u32[]{:S(2)}, u32[]{:S(2)}) collective-permute-start(bf16[4,128,256]{2,1,0:T(8,128)(2,1)S(1)} %get-tuple-element.35), channel_id=1, source_target_pairs={{0,1},{1,2},{2,3},{3,0},{4,5},{5,6},{6,7},{7,4},{8,9},{9,10},{10,1... | collective-permute-start | bytes 786440 | tf_op jit(solution)/shard_map/ppermute | solution.py:156
  41.3 6.1 %collective-permute-start.3 = (bf16[4,128,256]{2,1,0:T(8,128)(2,1)S(1)}, bf16[4,128,256]{2,1,0:T(8,128)(2,1)S(1)}, u32[]{:S(2)}, u32[]{:S(2)}) collective-permute-start(bf16[4,128,256]{2,1,0:T(8,128)(2,1)S(1)} %get-tuple-element.36), channel_id=1, source_target_pairs={{0,32},{32,64},{64,96},{96,128},{128,160},{160,192},{192,224},{224... | collective-permute-start | bytes 786440 | tf_op jit(solution)/shard_map/ppermute | solution.py:43
  41.3 8.3 %collective-permute-start.4 = (bf16[4,128,256]{2,1,0:T(8,128)(2,1)S(1)}, bf16[4,128,256]{2,1,0:T(8,128)(2,1)S(1)}, u32[]{:S(2)}, u32[]{:S(2)}) collective-permute-start(bf16[4,128,256]{2,1,0:T(8,128)(2,1)S(1)} %get-tuple-element.37), channel_id=1, source_target_pairs={{0,3},{1,0},{2,1},{3,2},{4,7},{5,4},{6,5},{7,6},{8,11},{9,8},{10,9... | collective-permute-start | bytes 786440 | tf_op jit(solution)/shard_map/ppermute | solution.py:156
  45.0 4.6 %collective-permute-start.5 = (bf16[4,128,256]{2,1,0:T(8,128)(2,1)S(1)}, bf16[4,128,256]{2,1,0:T(8,128)(2,1)S(1)}, u32[]{:S(2)}, u32[]{:S(2)}) collective-permute-start(bf16[4,128,256]{2,1,0:T(8,128)(2,1)S(1)} %get-tuple-element.38), channel_id=1, source_target_pairs={{0,480},{32,0},{64,32},{96,64},{128,96},{160,128},{192,160},{224,1... | collective-permute-start | bytes 786440 | tf_op jit(solution)/shard_map/ppermute | solution.py:43
  45.0 4.6 %copy-start.1 = (bf16[8,128,384]{2,1,0:T(8,128)(2,1)S(1)}, bf16[8,128,384]{2,1,0:T(8,128)(2,1)}, u32[]{:S(2)}) copy-start(bf16[8,128,384]{2,1,0:T(8,128)(2,1)} %copy-done) | copy-start | bytes 2359300
  50.2 14.2 %collective-permute-start.6 = (bf16[4,128,256]{2,1,0:T(8,128)(2,1)S(1)}, bf16[4,128,256]{2,1,0:T(8,128)(2,1)S(1)}, u32[]{:S(2)}, u32[]{:S(2)}) collective-permute-start(bf16[4,128,256]{2,1,0:T(8,128)(2,1)S(1)} %get-tuple-element.43), channel_id=1, source_target_pairs={{0,4},{1,5},{2,6},{3,7},{4,8},{5,9},{6,10},{7,11},{8,12},{9,13},{1... | collective-permute-start | bytes 786440 | tf_op jit(solution)/shard_map/ppermute | solution.py:156
  53.1 12.0 %collective-permute-start.7 = (bf16[4,128,256]{2,1,0:T(8,128)(2,1)S(1)}, bf16[4,128,256]{2,1,0:T(8,128)(2,1)S(1)}, u32[]{:S(2)}, u32[]{:S(2)}) collective-permute-start(bf16[4,128,256]{2,1,0:T(8,128)(2,1)S(1)} %get-tuple-element.44), channel_id=1, source_target_pairs={{0,28},{1,29},{2,30},{3,31},{4,0},{5,1},{6,2},{7,3},{8,4},{9,5},{1... | collective-permute-start | bytes 786440 | tf_op jit(solution)/shard_map/ppermute | solution.py:156
  57.2 9.5 %collective-permute-start.8 = (bf16[4,128,256]{2,1,0:T(8,128)(2,1)S(1)}, bf16[4,128,256]{2,1,0:T(8,128)(2,1)S(1)}, u32[]{:S(2)}, u32[]{:S(2)}) collective-permute-start(bf16[4,128,256]{2,1,0:T(8,128)(2,1)S(1)} %get-tuple-element.45), channel_id=1, source_target_pairs={{0,1},{1,2},{2,3},{3,0},{4,5},{5,6},{6,7},{7,4},{8,9},{9,10},{10,1... | collective-permute-start | bytes 786440 | tf_op jit(solution)/shard_map/ppermute | solution.py:156
  60.7 6.1 %collective-permute-start.9 = (bf16[4,128,256]{2,1,0:T(8,128)(2,1)S(1)}, bf16[4,128,256]{2,1,0:T(8,128)(2,1)S(1)}, u32[]{:S(2)}, u32[]{:S(2)}) collective-permute-start(bf16[4,128,256]{2,1,0:T(8,128)(2,1)S(1)} %get-tuple-element.46), channel_id=1, source_target_pairs={{0,32},{32,64},{64,96},{96,128},{128,160},{160,192},{192,224},{224... | collective-permute-start | bytes 786440 | tf_op jit(solution)/shard_map/ppermute | solution.py:43
  61.2 8.3 %collective-permute-start.10 = (bf16[4,128,256]{2,1,0:T(8,128)(2,1)S(1)}, bf16[4,128,256]{2,1,0:T(8,128)(2,1)S(1)}, u32[]{:S(2)}, u32[]{:S(2)}) collective-permute-start(bf16[4,128,256]{2,1,0:T(8,128)(2,1)S(1)} %get-tuple-element.47), channel_id=1, source_target_pairs={{0,3},{1,0},{2,1},{3,2},{4,7},{5,4},{6,5},{7,6},{8,11},{9,8},{10,9... | collective-permute-start | bytes 786440 | tf_op jit(solution)/shard_map/ppermute | solution.py:156
  64.3 5.1 %collective-permute-start.11 = (bf16[4,128,256]{2,1,0:T(8,128)(2,1)S(1)}, bf16[4,128,256]{2,1,0:T(8,128)(2,1)S(1)}, u32[]{:S(2)}, u32[]{:S(2)}) collective-permute-start(bf16[4,128,256]{2,1,0:T(8,128)(2,1)S(1)} %get-tuple-element.48), channel_id=1, source_target_pairs={{0,480},{32,0},{64,32},{96,64},{128,96},{160,128},{192,160},{224,1... | collective-permute-start | bytes 786440 | tf_op jit(solution)/shard_map/ppermute | solution.py:43

commit v9 on v6

--- a/solution.py
+++ b/solution.py
@@ -9,7 +9,7 @@
 ALL_AXES = ("ya", "yb", "tc", "gz", "gy")
 TIME_AXES = ("ya", "yb", "tc")
 TC, GZ, GY = 2, 3, 4
-ORDER = (0, 1, 2, 4, 3, 5)
+ORDER = (0, 2, 1, 4, 3, 5)
 SLOT_ROWS = 16
 LANES = 128
 SITES = 8

time: 105 us -> 105 us (level)
    ppermute x8, waiting for transfers between devices: 8.32 us -> 5.49 us  [crossed(): return lax.ppermute(values, ALL_AXES, pairs)]
    ppermute x4, waiting for transfers between devices: 0.01 us -> 2.8 us  [shifted(): lax.ppermute(values, axes, [(i, (i + step) % count) for i in range(count)])]
where the time goes in v9:
time: 105 us
  starting transfers between devices  38.7 us (37%)
  blocking collectives  33.4 us (32%)
  waiting for transfers between devices  23.8 us (23%)
  Pallas kernels  6.47 us (6%)
  local copies, waits for them, and re-layouts  2.19 us (2%)
    all_to_all x2, blocking collectives, everyone(): return lax.all_to_all(parts, axes, split_axis=0, concat_axis=0, tiled=True)  31.1 us
    ppermute x8, starting transfers between devices, crossed(): return lax.ppermute(values, ALL_AXES, pairs)  27.7 us
    all_to_all x1, waiting for transfers between devices, everyone(): return lax.all_to_all(parts, axes, split_axis=0, concat_axis=0, tiled=True)  15.5 us
    all_to_all x1, starting transfers between devices, everyone(): return lax.all_to_all(parts, axes, split_axis=0, concat_axis=0, tiled=True)  10.3 us
    ppermute x8, waiting for transfers between devices, crossed(): return lax.ppermute(values, ALL_AXES, pairs)  5.49 us
    ppermute x4, waiting for transfers between devices, shifted(): lax.ppermute(values, axes, [(i, (i + step) % count) for i in range(count)])  2.8 us
    all_gather x1, blocking collectives, local(): parts = jnp.sum(lax.all_gather(parts, 'tc'), axis=0)  2.23 us
    unnamed x6, local copies, waits for them, and re-layouts  2.17 us
  transfers between devices with their start and end apart: 13, of which 5 were waited for; matrix products, arithmetic and copies ran while one was open for 0% of the time, Pallas kernels for 2%

profile of v9, /device:TPU:8, one launch (start us, length us, event | category | flops | bytes accessed | tf_op | source)
XLA Modules:
  0.0 104.7 jit_solution(17022881878987043285)
XLA Ops:
  0.0 2.0 %shard_map.46 = bf16[8,272,128]{2,1,0:T(8,128)(2,1)} custom-call(s32[8]{0:T(128)} %owners.1, s32[8]{0:T(128)} %slots.1, bf16[8,128,256]{2,1,0:T(8,128)(2,1)} %bitcast.6), custom_call_target="tpu_custom_call" | custom-call | tf_op jit(solution)/shard_map/pallas_call | solution.py:80
  2.0 10.3 %all-to-all-start = ((bf16[8,272,128]{2,1,0:T(8,128)(2,1)}), bf16[8,272,128]{2,1,0:T(8,128)(2,1)S(1)}, u32[]{:S(2)}, u32[]{:S(2)}) async-start(bf16[8,272,128]{2,1,0:T(8,128)(2,1)} %shard_map.46), calls=%async_computation | async-start | bytes 1114112 | tf_op jit(solution)/shard_map/all_to_all | solution.py:361
  12.3 0.0 copy-start.2
  12.3 1.3 %copy-done.2 = bf16[9,1,2,2,2,64,128]{6,5,4,3,2,1,0:T(8,128)(2,1)S(1)} copy-done((bf16[9,1,2,2,2,64,128]{6,5,4,3,2,1,0:T(8,128)(2,1)S(1)}, bf16[9,1,2,2,2,64,128]{6,5,4,3,2,1,0:T(8,128)(2,1)}, u32[]{:S(2)}) %copy-start.2) | copy-done | bytes 1179672
  13.6 0.5 shard_map.47
  14.1 0.0 copy-start
  14.1 0.9 copy-done
  15.0 15.5 %all-to-all-done.landed = bf16[8,272,128]{2,1,0:T(8,128)(2,1)S(1)} async-done(((bf16[8,272,128]{2,1,0:T(8,128)(2,1)}), bf16[8,272,128]{2,1,0:T(8,128)(2,1)S(1)}, u32[]{:S(2)}, u32[]{:S(2)}) %all-to-all-start) | async-done | bytes 557088 | tf_op jit(solution)/shard_map/all_to_all | solution.py:361
  30.5 0.3 shard_map.48
  30.8 2.5 %collective-permute-start = (bf16[4,128,256]{2,1,0:T(8,128)(2,1)S(1)}, bf16[4,128,256]{2,1,0:T(8,128)(2,1)S(1)}, u32[]{:S(2)}, u32[]{:S(2)}) collective-permute-start(bf16[4,128,256]{2,1,0:T(8,128)(2,1)S(1)} %get-tuple-element.33), channel_id=1, source_target_pairs={{0,4},{1,5},{2,6},{3,7},{4,8},{5,9},{6,10},{7,11},{8,12},{9,13},{1... | collective-permute-start | bytes 786440 | tf_op jit(solution)/shard_map/ppermute | solution.py:156
  33.3 3.4 %collective-permute-start.1 = (bf16[4,128,256]{2,1,0:T(8,128)(2,1)S(1)}, bf16[4,128,256]{2,1,0:T(8,128)(2,1)S(1)}, u32[]{:S(2)}, u32[]{:S(2)}) collective-permute-start(bf16[4,128,256]{2,1,0:T(8,128)(2,1)S(1)} %get-tuple-element.34), channel_id=1, source_target_pairs={{0,1},{1,2},{2,3},{3,0},{4,5},{5,6},{6,7},{7,4},{8,9},{9,10},{10,1... | collective-permute-start | bytes 786440 | tf_op jit(solution)/shard_map/ppermute | solution.py:156
  36.7 4.6 %collective-permute-start.2 = (bf16[4,128,256]{2,1,0:T(8,128)(2,1)S(1)}, bf16[4,128,256]{2,1,0:T(8,128)(2,1)S(1)}, u32[]{:S(2)}, u32[]{:S(2)}) collective-permute-start(bf16[4,128,256]{2,1,0:T(8,128)(2,1)S(1)} %get-tuple-element.35), channel_id=1, source_target_pairs={{0,28},{1,29},{2,30},{3,31},{4,0},{5,1},{6,2},{7,3},{8,4},{9,5},{1... | collective-permute-start | bytes 786440 | tf_op jit(solution)/shard_map/ppermute | solution.py:156
  41.3 0.0 collective-permute-start.3
  41.3 3.7 %collective-permute-start.4 = (bf16[4,128,256]{2,1,0:T(8,128)(2,1)S(1)}, bf16[4,128,256]{2,1,0:T(8,128)(2,1)S(1)}, u32[]{:S(2)}, u32[]{:S(2)}) collective-permute-start(bf16[4,128,256]{2,1,0:T(8,128)(2,1)S(1)} %get-tuple-element.37), channel_id=1, source_target_pairs={{0,3},{1,0},{2,1},{3,2},{4,7},{5,4},{6,5},{7,6},{8,11},{9,8},{10,9... | collective-permute-start | bytes 786440 | tf_op jit(solution)/shard_map/ppermute | solution.py:156
  45.0 0.0 collective-permute-done.r0
  45.0 0.0 collective-permute-start.5
  45.0 0.0 copy-start.1
  45.1 0.6 shard_map.49.partial
  45.6 0.0 collective-permute-done.1.r1
  45.6 0.0 collective-permute-done.2.r2
  45.7 1.5 %collective-permute-done.3.r3 = bf16[4,128,256]{2,1,0:T(8,128)(2,1)S(1)} collective-permute-done((bf16[4,128,256]{2,1,0:T(8,128)(2,1)S(1)}, bf16[4,128,256]{2,1,0:T(8,128)(2,1)S(1)}, u32[]{:S(2)}, u32[]{:S(2)}) %collective-permute-start.3) | collective-permute-done | bytes 262176 | tf_op jit(solution)/shard_map/ppermute | solution.py:43
  47.1 2.5 %collective-permute-done.4.r4 = bf16[4,128,256]{2,1,0:T(8,128)(2,1)S(1)} collective-permute-done((bf16[4,128,256]{2,1,0:T(8,128)(2,1)S(1)}, bf16[4,128,256]{2,1,0:T(8,128)(2,1)S(1)}, u32[]{:S(2)}, u32[]{:S(2)}) %collective-permute-start.4) | collective-permute-done | bytes 262176 | tf_op jit(solution)/shard_map/ppermute | solution.py:156
  49.6 0.0 collective-permute-done.5.r5
  49.6 0.0 copy-done.1
  49.6 0.6 shard_map.50
  50.2 2.9 %collective-permute-start.6 = (bf16[4,128,256]{2,1,0:T(8,128)(2,1)S(1)}, bf16[4,128,256]{2,1,0:T(8,128)(2,1)S(1)}, u32[]{:S(2)}, u32[]{:S(2)}) collective-permute-start(bf16[4,128,256]{2,1,0:T(8,128)(2,1)S(1)} %get-tuple-element.43), channel_id=1, source_target_pairs={{0,4},{1,5},{2,6},{3,7},{4,8},{5,9},{6,10},{7,11},{8,12},{9,13},{1... | collective-permute-start | bytes 786440 | tf_op jit(solution)/shard_map/ppermute | solution.py:156
  53.1 3.4 %collective-permute-start.7 = (bf16[4,128,256]{2,1,0:T(8,128)(2,1)S(1)}, bf16[4,128,256]{2,1,0:T(8,128)(2,1)S(1)}, u32[]{:S(2)}, u32[]{:S(2)}) collective-permute-start(bf16[4,128,256]{2,1,0:T(8,128)(2,1)S(1)} %get-tuple-element.44), channel_id=1, source_target_pairs={{0,1},{1,2},{2,3},{3,0},{4,5},{5,6},{6,7},{7,4},{8,9},{9,10},{10,1... | collective-permute-start | bytes 786440 | tf_op jit(solution)/shard_map/ppermute | solution.py:156
  56.5 4.1 %collective-permute-start.8 = (bf16[4,128,256]{2,1,0:T(8,128)(2,1)S(1)}, bf16[4,128,256]{2,1,0:T(8,128)(2,1)S(1)}, u32[]{:S(2)}, u32[]{:S(2)}) collective-permute-start(bf16[4,128,256]{2,1,0:T(8,128)(2,1)S(1)} %get-tuple-element.45), channel_id=1, source_target_pairs={{0,28},{1,29},{2,30},{3,31},{4,0},{5,1},{6,2},{7,3},{8,4},{9,5},{1... | collective-permute-start | bytes 786440 | tf_op jit(solution)/shard_map/ppermute | solution.py:156
  60.7 0.5 collective-permute-start.9
  61.2 3.1 %collective-permute-start.10 = (bf16[4,128,256]{2,1,0:T(8,128)(2,1)S(1)}, bf16[4,128,256]{2,1,0:T(8,128)(2,1)S(1)}, u32[]{:S(2)}, u32[]{:S(2)}) collective-permute-start(bf16[4,128,256]{2,1,0:T(8,128)(2,1)S(1)} %get-tuple-element.47), channel_id=1, source_target_pairs={{0,3},{1,0},{2,1},{3,2},{4,7},{5,4},{6,5},{7,6},{8,11},{9,8},{10,9... | collective-permute-start | bytes 786440 | tf_op jit(solution)/shard_map/ppermute | solution.py:156
  64.3 0.0 collective-permute-done.6.r0
  64.4 0.1 collective-permute-start.11
  64.5 0.7 shard_map.51
  65.1 0.0 collective-permute-done.7.r1
  65.1 0.0 collective-permute-done.8.r2
  65.1 1.3 %collective-permute-done.9.r3 = bf16[4,128,256]{2,1,0:T(8,128)(2,1)S(1)} collective-permute-done((bf16[4,128,256]{2,1,0:T(8,128)(2,1)S(1)}, bf16[4,128,256]{2,1,0:T(8,128)(2,1)S(1)}, u32[]{:S(2)}, u32[]{:S(2)}) %collective-permute-start.9) | collective-permute-done | bytes 262176 | tf_op jit(solution)/shard_map/ppermute | solution.py:43
  66.5 3.0 %collective-permute-done.10.r4 = bf16[4,128,256]{2,1,0:T(8,128)(2,1)S(1)} collective-permute-done((bf16[4,128,256]{2,1,0:T(8,128)(2,1)S(1)}, bf16[4,128,256]{2,1,0:T(8,128)(2,1)S(1)}, u32[]{:S(2)}, u32[]{:S(2)}) %collective-permute-start.10) | collective-permute-done | bytes 262176 | tf_op jit(solution)/shard_map/ppermute | solution.py:156
  69.5 0.0 collective-permute-done.11.r5
  69.5 0.8 shard_map.52
  70.2 2.2 %all-gather = f32[16,256]{1,0:T(8,128)S(1)} all-gather(f32[8,256]{1,0:T(8,128)S(1)} %shard_map.52), channel_id=2, replica_groups=mesh['ya'=4,'yb'=2,'tc'=2,'gz'=8,'gy'=4] {'tc'}, dimensions={0}, use_global_device_ids=true | all-gather | bytes 24576 | tf_op jit(solution)/shard_map/all_gather | solution.py:375
  72.5 12.7 %all_to_all.15 = f32[16,8,256]{2,1,0:T(8,128)S(1)} all-to-all(f32[16,8,256]{2,1,0:T(8,128)S(1)} %broadcast_in_dim.4), channel_id=1, replica_groups=mesh['ya'=4,'yb'=2,'tc'=2,'gz'=8,'gy'=4] {'yb','gz'}, dimensions={0} | all-to-all | bytes 262144 | tf_op jit(solution)/shard_map/all_to_all | solution.py:361
  85.3 18.4 %all_to_all.16.landed = f32[16,8,256]{2,1,0:T(8,128)S(1)} all-to-all(f32[16,8,256]{2,1,0:T(8,128)S(1)} %broadcast_in_dim.5), channel_id=1, replica_groups=mesh['ya'=4,'yb'=2,'tc'=2,'gz'=8,'gy'=4] {'ya','gy'}, dimensions={0} | all-to-all | bytes 262144 | tf_op jit(solution)/shard_map/all_to_all | solution.py:361
  103.7 1.1 %shard_map.53 = bf16[8,128,256]{2,1,0:T(8,128)(2,1)} custom-call(f32[16,8,256]{2,1,0:T(8,128)S(1)} %all_to_all.16.landed, f32[8,128,256]{2,1,0:T(8,128)S(1)} %get-tuple-element.40.image, bf16[8,128,256]{2,1,0:T(8,128)(2,1)S(1)} %get-tuple-element.32.field.source), custom_call_target="tpu_custom_call" | custom-call | tf_op jit(solution)/shard_map/pallas_call | solution.py:320
  (4 shorter events, 0.0 us)
Async XLA Ops:
  2.0 28.5 %all-to-all-start = ((bf16[8,272,128]{2,1,0:T(8,128)(2,1)}), bf16[8,272,128]{2,1,0:T(8,128)(2,1)S(1)}, u32[]{:S(2)}, u32[]{:S(2)}) async-start(bf16[8,272,128]{2,1,0:T(8,128)(2,1)} %shard_map.46), calls=%async_computation | async-start | bytes 1114112 | tf_op jit(solution)/shard_map/all_to_all | solution.py:361
  12.3 1.3 %copy-start.2 = (bf16[9,1,2,2,2,64,128]{6,5,4,3,2,1,0:T(8,128)(2,1)S(1)}, bf16[9,1,2,2,2,64,128]{6,5,4,3,2,1,0:T(8,128)(2,1)}, u32[]{:S(2)}) copy-start(bf16[9,1,2,2,2,64,128]{6,5,4,3,2,1,0:T(8,128)(2,1)} %param.5) | copy-start | bytes 3538948
  14.1 0.9 copy-start
  30.8 14.2 %collective-permute-start = (bf16[4,128,256]{2,1,0:T(8,128)(2,1)S(1)}, bf16[4,128,256]{2,1,0:T(8,128)(2,1)S(1)}, u32[]{:S(2)}, u32[]{:S(2)}) collective-permute-start(bf16[4,128,256]{2,1,0:T(8,128)(2,1)S(1)} %get-tuple-element.33), channel_id=1, source_target_pairs={{0,4},{1,5},{2,6},{3,7},{4,8},{5,9},{6,10},{7,11},{8,12},{9,13},{1... | collective-permute-start | bytes 786440 | tf_op jit(solution)/shard_map/ppermute | solution.py:156
  33.3 12.3 %collective-permute-start.1 = (bf16[4,128,256]{2,1,0:T(8,128)(2,1)S(1)}, bf16[4,128,256]{2,1,0:T(8,128)(2,1)S(1)}, u32[]{:S(2)}, u32[]{:S(2)}) collective-permute-start(bf16[4,128,256]{2,1,0:T(8,128)(2,1)S(1)} %get-tuple-element.34), channel_id=1, source_target_pairs={{0,1},{1,2},{2,3},{3,0},{4,5},{5,6},{6,7},{7,4},{8,9},{9,10},{10,1... | collective-permute-start | bytes 786440 | tf_op jit(solution)/shard_map/ppermute | solution.py:156
  36.7 8.9 %collective-permute-start.2 = (bf16[4,128,256]{2,1,0:T(8,128)(2,1)S(1)}, bf16[4,128,256]{2,1,0:T(8,128)(2,1)S(1)}, u32[]{:S(2)}, u32[]{:S(2)}) collective-permute-start(bf16[4,128,256]{2,1,0:T(8,128)(2,1)S(1)} %get-tuple-element.35), channel_id=1, source_target_pairs={{0,28},{1,29},{2,30},{3,31},{4,0},{5,1},{6,2},{7,3},{8,4},{9,5},{1... | collective-permute-start | bytes 786440 | tf_op jit(solution)/shard_map/ppermute | solution.py:156
  41.3 5.8 %collective-permute-start.3 = (bf16[4,128,256]{2,1,0:T(8,128)(2,1)S(1)}, bf16[4,128,256]{2,1,0:T(8,128)(2,1)S(1)}, u32[]{:S(2)}, u32[]{:S(2)}) collective-permute-start(bf16[4,128,256]{2,1,0:T(8,128)(2,1)S(1)} %get-tuple-element.36), channel_id=1, source_target_pairs={{0,32},{32,64},{64,96},{96,128},{128,160},{160,192},{192,224},{224... | collective-permute-start | bytes 786440 | tf_op jit(solution)/shard_map/ppermute | solution.py:43
  41.3 8.3 %collective-permute-start.4 = (bf16[4,128,256]{2,1,0:T(8,128)(2,1)S(1)}, bf16[4,128,256]{2,1,0:T(8,128)(2,1)S(1)}, u32[]{:S(2)}, u32[]{:S(2)}) collective-permute-start(bf16[4,128,256]{2,1,0:T(8,128)(2,1)S(1)} %get-tuple-element.37), channel_id=1, source_target_pairs={{0,3},{1,0},{2,1},{3,2},{4,7},{5,4},{6,5},{7,6},{8,11},{9,8},{10,9... | collective-permute-start | bytes 786440 | tf_op jit(solution)/shard_map/ppermute | solution.py:156
  45.0 4.6 %collective-permute-start.5 = (bf16[4,128,256]{2,1,0:T(8,128)(2,1)S(1)}, bf16[4,128,256]{2,1,0:T(8,128)(2,1)S(1)}, u32[]{:S(2)}, u32[]{:S(2)}) collective-permute-start(bf16[4,128,256]{2,1,0:T(8,128)(2,1)S(1)} %get-tuple-element.38), channel_id=1, source_target_pairs={{0,480},{32,0},{64,32},{96,64},{128,96},{160,128},{192,160},{224,1... | collective-permute-start | bytes 786440 | tf_op jit(solution)/shard_map/ppermute | solution.py:43
  45.0 4.6 %copy-start.1 = (bf16[8,128,384]{2,1,0:T(8,128)(2,1)S(1)}, bf16[8,128,384]{2,1,0:T(8,128)(2,1)}, u32[]{:S(2)}) copy-start(bf16[8,128,384]{2,1,0:T(8,128)(2,1)} %copy-done) | copy-start | bytes 2359300
  50.2 14.2 %collective-permute-start.6 = (bf16[4,128,256]{2,1,0:T(8,128)(2,1)S(1)}, bf16[4,128,256]{2,1,0:T(8,128)(2,1)S(1)}, u32[]{:S(2)}, u32[]{:S(2)}) collective-permute-start(bf16[4,128,256]{2,1,0:T(8,128)(2,1)S(1)} %get-tuple-element.43), channel_id=1, source_target_pairs={{0,4},{1,5},{2,6},{3,7},{4,8},{5,9},{6,10},{7,11},{8,12},{9,13},{1... | collective-permute-start | bytes 786440 | tf_op jit(solution)/shard_map/ppermute | solution.py:156
  53.1 12.0 %collective-permute-start.7 = (bf16[4,128,256]{2,1,0:T(8,128)(2,1)S(1)}, bf16[4,128,256]{2,1,0:T(8,128)(2,1)S(1)}, u32[]{:S(2)}, u32[]{:S(2)}) collective-permute-start(bf16[4,128,256]{2,1,0:T(8,128)(2,1)S(1)} %get-tuple-element.44), channel_id=1, source_target_pairs={{0,1},{1,2},{2,3},{3,0},{4,5},{5,6},{6,7},{7,4},{8,9},{9,10},{10,1... | collective-permute-start | bytes 786440 | tf_op jit(solution)/shard_map/ppermute | solution.py:156
  56.5 8.6 %collective-permute-start.8 = (bf16[4,128,256]{2,1,0:T(8,128)(2,1)S(1)}, bf16[4,128,256]{2,1,0:T(8,128)(2,1)S(1)}, u32[]{:S(2)}, u32[]{:S(2)}) collective-permute-start(bf16[4,128,256]{2,1,0:T(8,128)(2,1)S(1)} %get-tuple-element.45), channel_id=1, source_target_pairs={{0,28},{1,29},{2,30},{3,31},{4,0},{5,1},{6,2},{7,3},{8,4},{9,5},{1... | collective-permute-start | bytes 786440 | tf_op jit(solution)/shard_map/ppermute | solution.py:156
  60.7 5.8 %collective-permute-start.9 = (bf16[4,128,256]{2,1,0:T(8,128)(2,1)S(1)}, bf16[4,128,256]{2,1,0:T(8,128)(2,1)S(1)}, u32[]{:S(2)}, u32[]{:S(2)}) collective-permute-start(bf16[4,128,256]{2,1,0:T(8,128)(2,1)S(1)} %get-tuple-element.46), channel_id=1, source_target_pairs={{0,32},{32,64},{64,96},{96,128},{128,160},{160,192},{192,224},{224... | collective-permute-start | bytes 786440 | tf_op jit(solution)/shard_map/ppermute | solution.py:43
  61.2 8.3 %collective-permute-start.10 = (bf16[4,128,256]{2,1,0:T(8,128)(2,1)S(1)}, bf16[4,128,256]{2,1,0:T(8,128)(2,1)S(1)}, u32[]{:S(2)}, u32[]{:S(2)}) collective-permute-start(bf16[4,128,256]{2,1,0:T(8,128)(2,1)S(1)} %get-tuple-element.47), channel_id=1, source_target_pairs={{0,3},{1,0},{2,1},{3,2},{4,7},{5,4},{6,5},{7,6},{8,11},{9,8},{10,9... | collective-permute-start | bytes 786440 | tf_op jit(solution)/shard_map/ppermute | solution.py:156
  64.4 5.1 %collective-permute-start.11 = (bf16[4,128,256]{2,1,0:T(8,128)(2,1)S(1)}, bf16[4,128,256]{2,1,0:T(8,128)(2,1)S(1)}, u32[]{:S(2)}, u32[]{:S(2)}) collective-permute-start(bf16[4,128,256]{2,1,0:T(8,128)(2,1)S(1)} %get-tuple-element.48), channel_id=1, source_target_pairs={{0,480},{32,0},{64,32},{96,64},{128,96},{160,128},{192,160},{224,1... | collective-permute-start | bytes 786440 | tf_op jit(solution)/shard_map/ppermute | solution.py:43
